TPU v7x, 32 devices: a whole 2x2x4 slice. The times are simulated.
32 devices in a mesh: pas: 16 (over z, y, x), mdl: 2 (over core).
Axes of the slice: x: 2, y: 2, z: 4, core: 2. Of those that a mesh axis runs over, the one named last changes fastest.
Arguments:
- target_states: bfloat16 [4096, 768], P('pas'), may hold values from -6 to 6
- passage_states: bfloat16 [640, 64, 768], P('pas', None, 'mdl'), may hold values from -6 to 6
- slot_query: int32 [640], P('pas'), may hold values from 0 to 15, as said below
- slot_live: int32 [640], P('pas'), may hold values from 0 to 1, as said below
- norm_gains: float32 [3, 768], replicated, may hold values from 0.5 to 1.5
- self_query: bfloat16 [768, 768], P('pas', 'mdl'), may hold values from -0.078125 to 0.078125
- self_key: bfloat16 [768, 768], P('pas', 'mdl'), may hold values from -0.21875 to 0.21875
- self_value: bfloat16 [768, 768], P('pas', 'mdl'), may hold values from -0.21875 to 0.21875
- self_output: bfloat16 [768, 768], P('mdl', 'pas'), may hold values from -0.625 to 0.625
- position_bias: float32 [32, 12], P(None, 'mdl'), may hold values from -4 to 4
- cross_query: bfloat16 [768, 768], P('pas', 'mdl'), may hold values from -0.078125 to 0.078125
- cross_key: bfloat16 [768, 768], P('pas', 'mdl'), may hold values from -0.21875 to 0.21875
- cross_value: bfloat16 [768, 768], P('pas', 'mdl'), may hold values from -0.21875 to 0.21875
- cross_output: bfloat16 [768, 768], P('mdl', 'pas'), may hold values from -1.25 to 1.25
- expand_weight: bfloat16 [768, 3072], P('pas', 'mdl'), may hold values from -0.21875 to 0.21875
- reduce_weight: bfloat16 [3072, 768], P('mdl', 'pas'), may hold values from -0.109375 to 0.109375
- output_cotangent: bfloat16 [4096, 768], P('pas'), may hold values from -6 to 6
Outputs:
- block_out: bfloat16 [4096, 768], P('pas')
- target_grad: bfloat16 [4096, 768], P('pas')
- passage_grad: bfloat16 [640, 64, 768], P('pas', None, 'mdl')
- norm_gains_grad: float32 [3, 768], replicated
- self_query_grad: float32 [768, 768], P('pas', 'mdl')
- self_key_grad: float32 [768, 768], P('pas', 'mdl')
- self_value_grad: float32 [768, 768], P('pas', 'mdl')
- self_output_grad: float32 [768, 768], P('mdl', 'pas')
- position_bias_grad: float32 [32, 12], P(None, 'mdl')
- cross_query_grad: float32 [768, 768], P('pas', 'mdl')
- cross_key_grad: float32 [768, 768], P('pas', 'mdl')
- cross_value_grad: float32 [768, 768], P('pas', 'mdl')
- cross_output_grad: float32 [768, 768], P('mdl', 'pas')
- expand_weight_grad: float32 [768, 3072], P('pas', 'mdl')
- reduce_weight_grad: float32 [3072, 768], P('mdl', 'pas')
Inputs may be any that keep to these rules, and one draw needn't show every extreme that they name: `slot_query`: each query id names exactly 40 slots; query q's target tokens are rows q * 256 to (q + 1) * 256 - 1. The 40 slots of one index of pas hold at most 3 slots of the 1 queries of any one index of pas, and in every draw some pair reaches 3. `slot_live`: of each query's 40 slots, 5 or more are live, and some query has all 40 live.
All inputs are finite; a program needn't handle non-finite values.
Results may differ from a plain program's by a relative error of at most 0.025.
The roundings to bfloat16 on the way count: a program that leaves them out, or rounds other values in their place, can miss the bound.
Values may be sent and summed in bfloat16 or wider, within the bound.
A program may use at most 192 MiB of HBM per device.

v0:
```python
from functools import partial
import math

import jax
import jax.numpy as jnp
import numpy as np
from jax import lax
from jax.sharding import PartitionSpec as P

HEAD_DIM = 64
MAXDIST = 128
TLEN = 256
PQ = 40


EPSILON = 1e-06
MASKED = -1e30


def bucket_table(length, buckets, distance):
    later = np.arange(length)[:, None]
    earlier = np.arange(length)[None, :]
    behind = np.maximum(later - earlier, 0)
    exact = buckets // 2
    spread = np.log(np.maximum(behind, 1) / exact) / math.log(distance / exact) * (buckets - exact)
    far_bucket = np.minimum(exact + np.floor(spread).astype(np.int32), buckets - 1)
    return np.where(behind < exact, behind, far_bucket).astype(np.int32)


def rms_forward(values, gain):
    factor = lax.rsqrt(jnp.mean(values * values, axis=-1, keepdims=True) + EPSILON)
    unit_rows = values * factor
    return (unit_rows, factor, (unit_rows * gain).astype(jnp.bfloat16))


def rms_backward(normed_grad, unit_rows, factor, gain):
    scaled_grad = normed_grad * gain
    input_grad = factor * (
        scaled_grad - unit_rows * jnp.mean(scaled_grad * unit_rows, axis=-1, keepdims=True)
    )
    return (input_grad, jnp.sum(normed_grad * unit_rows, axis=0))


def over_heads(partial_rows):
    return lax.psum(partial_rows, "mdl")


def score_block(queries, key_rows, allowed, bias):
    scores = jnp.einsum("sihe,sjhe->shij", queries, key_rows, preferred_element_type=jnp.float32)
    if bias is not None:
        scores = scores + bias
    return jnp.where(allowed, scores, MASKED)


def attend(queries, key_rows, values, allowed, bias):
    scores = score_block(queries, key_rows, allowed, bias)
    highest = jnp.max(scores, axis=-1, keepdims=True)
    totals = highest + jnp.log(jnp.sum(jnp.exp(scores - highest), axis=-1, keepdims=True))
    probability = jnp.exp(scores - totals)
    mixed = jnp.einsum(
        "shij,sjhe->sihe",
        probability.astype(jnp.bfloat16),
        values,
        preferred_element_type=jnp.float32,
    )
    return (mixed.astype(jnp.bfloat16), totals)


def attend_back(queries, key_rows, values, allowed, bias, totals, out_grad):
    scores = score_block(queries, key_rows, allowed, bias)
    probability = jnp.exp(scores - totals)
    prob_grad = jnp.einsum("sihe,sjhe->shij", out_grad, values, preferred_element_type=jnp.float32)
    centered = jnp.sum(probability * prob_grad, axis=-1, keepdims=True)
    score_grad = (probability * (prob_grad - centered)).astype(jnp.bfloat16)
    query_grad = jnp.einsum(
        "shij,sjhe->sihe", score_grad, key_rows, preferred_element_type=jnp.float32
    )
    key_grad = jnp.einsum(
        "shij,sihe->sjhe", score_grad, queries, preferred_element_type=jnp.float32
    )
    value_grad = jnp.einsum(
        "shij,sihe->sjhe",
        probability.astype(jnp.bfloat16),
        out_grad,
        preferred_element_type=jnp.float32,
    )
    return (query_grad, key_grad, value_grad, score_grad)


def send_plan(slot_query, slot_live, per_device, capacity):
    target_device = slot_query // per_device
    matching = target_device[:, None] == target_device[None, :]
    lower_part = jnp.tril(jnp.ones(matching.shape, jnp.bool_), -1)
    ranking = jnp.sum(jnp.logical_and(matching, lower_part), axis=1)
    position = target_device * capacity + ranking
    codes = jnp.where(slot_live > 0, slot_query % per_device + 1, 0).astype(jnp.bfloat16)
    return (position, codes)


def arrange_plan(got_codes, per_device, slots_each):
    local_query = got_codes.astype(jnp.int32) - 1
    matches = (local_query[:, None] == jnp.arange(per_device, dtype=jnp.int32)[None, :]).astype(
        jnp.int32
    )
    ranking = jnp.sum((jnp.cumsum(matches, axis=0) - 1) * matches, axis=1)
    spare_place = per_device * slots_each
    places = jnp.where(local_query >= 0, local_query * slots_each + ranking, spare_place)
    arrivals = got_codes.shape[0]
    gather_index = (
        jnp.zeros((spare_place + 1,), jnp.int32)
        .at[places]
        .set(jnp.arange(arrivals, dtype=jnp.int32))
    )
    valid_slot = jnp.zeros((spare_place + 1,), jnp.int32).at[places].set(1)
    return (gather_index[:spare_place], valid_slot[:spare_place] > 0)


def place_rows(rows, position, total_rows):
    return jnp.zeros((total_rows,) + rows.shape[1:], rows.dtype).at[position].set(rows)


def return_rows(rows, gather_index, total_rows):
    return jnp.zeros((total_rows,) + rows.shape[1:], rows.dtype).at[gather_index].add(rows)


def body(
    target_states,
    passage_states,
    slot_query,
    slot_live,
    norm_gains,
    self_query,
    self_key,
    self_value,
    self_output,
    position_bias,
    cross_query,
    cross_key,
    cross_value,
    cross_output,
    expand_weight,
    reduce_weight,
    output_cotangent,
):
    (
        query_full,
        key_full,
        value_full,
        cross_query_full,
        cross_key_full,
        cross_value_full,
        expand_full,
    ) = (
        lax.all_gather(self_query, "pas", axis=0, tiled=True),
        lax.all_gather(self_key, "pas", axis=0, tiled=True),
        lax.all_gather(self_value, "pas", axis=0, tiled=True),
        lax.all_gather(cross_query, "pas", axis=0, tiled=True),
        lax.all_gather(cross_key, "pas", axis=0, tiled=True),
        lax.all_gather(cross_value, "pas", axis=0, tiled=True),
        lax.all_gather(expand_weight, "pas", axis=0, tiled=True),
    )
    output_full, cross_output_full, reduce_full = (
        lax.all_gather(self_output, "pas", axis=1, tiled=True),
        lax.all_gather(cross_output, "pas", axis=1, tiled=True),
        lax.all_gather(reduce_weight, "pas", axis=1, tiled=True),
    )
    width_here = query_full.shape[1]
    heads_here = width_here // HEAD_DIM
    sequences = target_states.shape[0] // TLEN
    passage_len = passage_states.shape[1]
    bucket_count = position_bias.shape[0]
    devices = lax.axis_size("pas")
    slots_here = slot_query.shape[0]
    capacity = -(-slots_here // devices)
    buffer_rows = devices * capacity
    residual = target_states.astype(jnp.float32)
    unit_one, factor_one, normed_one = rms_forward(residual, norm_gains[0])
    self_weights = jnp.concatenate([query_full, key_full, value_full], axis=1)
    projected = jnp.dot(normed_one, self_weights, preferred_element_type=jnp.float32).astype(
        jnp.bfloat16
    )
    projected = projected.reshape(sequences, TLEN, 3, heads_here, HEAD_DIM)
    queries_self = projected[:, :, 0]
    keys_self = projected[:, :, 1]
    values_self = projected[:, :, 2]
    buckets = jnp.asarray(bucket_table(TLEN, bucket_count, MAXDIST))
    one_hot = (jnp.arange(bucket_count, dtype=jnp.int32)[:, None, None] == buckets[None]).astype(
        jnp.float32
    )
    bias_full = jnp.einsum("bij,bh->hij", one_hot, position_bias, precision=lax.Precision.HIGHEST)[
        None
    ]
    causal = jnp.asarray(np.tril(np.ones((TLEN, TLEN), dtype=bool)))
    attended_self, total_self = attend(queries_self, keys_self, values_self, causal, bias_full)
    merged_self = attended_self.reshape(sequences * TLEN, width_here)
    residual_two = residual + over_heads(
        jnp.dot(merged_self, output_full, preferred_element_type=jnp.float32)
    )
    unit_two, factor_two, normed_two = rms_forward(residual_two, norm_gains[1])
    cross_queries = jnp.dot(
        normed_two, cross_query_full, preferred_element_type=jnp.float32
    ).astype(jnp.bfloat16)
    cross_queries = cross_queries.reshape(sequences, TLEN, heads_here, HEAD_DIM)
    kv_weights = jnp.concatenate([cross_key_full, cross_value_full], axis=1)
    position, codes = send_plan(slot_query, slot_live, sequences, capacity)
    sent_codes = place_rows(codes, position, buffer_rows)
    states_full = lax.all_gather(passage_states, "mdl", axis=2, tiled=True)
    key_values = jnp.einsum(
        "tpd,dc->tpc", states_full, kv_weights, preferred_element_type=jnp.float32
    ).astype(jnp.bfloat16)
    received, got_codes = (
        lax.all_to_all(
            place_rows(key_values, position, buffer_rows),
            "pas",
            split_axis=0,
            concat_axis=0,
            tiled=True,
        ),
        lax.all_to_all(sent_codes, "pas", split_axis=0, concat_axis=0, tiled=True),
    )
    gather_index, valid_slot = arrange_plan(got_codes, sequences, PQ)
    arranged = jnp.take(received, gather_index, axis=0)
    arranged = arranged.reshape(sequences, PQ * passage_len, 2, heads_here, HEAD_DIM)
    key_rows = arranged[:, :, 0]
    value_rows = arranged[:, :, 1]
    allowed = jnp.repeat(valid_slot.reshape(sequences, PQ), passage_len, axis=1)[:, None, None, :]
    head_block = 2
    head_ranges = [
        slice(start_head, start_head + head_block)
        for start_head in range(0, heads_here, head_block)
    ]
    cross_parts = []
    cross_totals = []
    for head_range in head_ranges:
        mixed_part, total_part = attend(
            cross_queries[:, :, head_range],
            key_rows[:, :, head_range],
            value_rows[:, :, head_range],
            allowed,
            None,
        )
        cross_parts.append(mixed_part)
        cross_totals.append(total_part)
    merged_cross = jnp.concatenate(cross_parts, axis=2).reshape(sequences * TLEN, width_here)
    residual_three = residual_two + over_heads(
        jnp.dot(merged_cross, cross_output_full, preferred_element_type=jnp.float32)
    )
    unit_three, factor_three, normed_three = rms_forward(residual_three, norm_gains[2])
    before = jnp.dot(normed_three, expand_full, preferred_element_type=jnp.float32)
    hidden = jax.nn.gelu(before, approximate=True).astype(jnp.bfloat16)
    block_out = residual_three + over_heads(
        jnp.dot(hidden, reduce_full, preferred_element_type=jnp.float32)
    )
    grad_out = output_cotangent.astype(jnp.float32)
    reduce_grad = jnp.dot(hidden.T, output_cotangent, preferred_element_type=jnp.float32)
    hidden_grad = jnp.dot(output_cotangent, reduce_full.T, preferred_element_type=jnp.float32)
    unused_value, gelu_pullback = jax.vjp(partial(jax.nn.gelu, approximate=True), before)
    before_grad = gelu_pullback(hidden_grad)[0].astype(jnp.bfloat16)
    expand_grad = jnp.dot(normed_three.T, before_grad, preferred_element_type=jnp.float32)
    normed_grad = over_heads(
        jnp.dot(before_grad, expand_full.T, preferred_element_type=jnp.float32)
    )
    back_three, gain_three = rms_backward(normed_grad, unit_three, factor_three, norm_gains[2])
    grad_three = grad_out + back_three
    grad_low = grad_three.astype(jnp.bfloat16)
    cross_output_grad = jnp.dot(merged_cross.T, grad_low, preferred_element_type=jnp.float32)
    mixed_grad = jnp.dot(grad_low, cross_output_full.T, preferred_element_type=jnp.float32).astype(
        jnp.bfloat16
    )
    mixed_grad = mixed_grad.reshape(sequences, TLEN, heads_here, HEAD_DIM)
    query_parts = []
    key_parts = []
    value_parts = []
    for number, head_range in enumerate(head_ranges):
        query_part, key_part, value_part, unused_scores = attend_back(
            cross_queries[:, :, head_range],
            key_rows[:, :, head_range],
            value_rows[:, :, head_range],
            allowed,
            None,
            cross_totals[number],
            mixed_grad[:, :, head_range],
        )
        query_parts.append(query_part)
        key_parts.append(key_part)
        value_parts.append(value_part)
    cross_query_rows = (
        jnp.concatenate(query_parts, axis=2)
        .astype(jnp.bfloat16)
        .reshape(sequences * TLEN, width_here)
    )
    kv_grad = jnp.stack(
        [jnp.concatenate(key_parts, axis=2), jnp.concatenate(value_parts, axis=2)], axis=2
    )
    kv_grad = kv_grad.astype(jnp.bfloat16).reshape(sequences * PQ, passage_len, 2 * width_here)
    returned = lax.all_to_all(
        return_rows(kv_grad, gather_index, buffer_rows),
        "pas",
        split_axis=0,
        concat_axis=0,
        tiled=True,
    )
    kv_grad_here = jnp.take(returned, position, axis=0)
    kv_weight_grad = jnp.einsum(
        "tpd,tpc->dc", states_full, kv_grad_here, preferred_element_type=jnp.float32
    )
    states_grad = jnp.einsum(
        "tpc,dc->tpd", kv_grad_here, kv_weights, preferred_element_type=jnp.float32
    )
    passage_grad = lax.psum_scatter(
        states_grad.astype(jnp.bfloat16), "mdl", scatter_dimension=2, tiled=True
    )
    cross_query_grad = jnp.dot(normed_two.T, cross_query_rows, preferred_element_type=jnp.float32)
    normed_grad = over_heads(
        jnp.dot(cross_query_rows, cross_query_full.T, preferred_element_type=jnp.float32)
    )
    back_two, gain_two = rms_backward(normed_grad, unit_two, factor_two, norm_gains[1])
    grad_two = grad_three + back_two
    grad_low = grad_two.astype(jnp.bfloat16)
    self_output_grad = jnp.dot(merged_self.T, grad_low, preferred_element_type=jnp.float32)
    attended_grad = jnp.dot(grad_low, output_full.T, preferred_element_type=jnp.float32).astype(
        jnp.bfloat16
    )
    attended_grad = attended_grad.reshape(sequences, TLEN, heads_here, HEAD_DIM)
    query_grad, key_grad, value_grad, score_grad = attend_back(
        queries_self, keys_self, values_self, causal, bias_full, total_self, attended_grad
    )
    bias_grad = jnp.einsum(
        "hij,bij->bh",
        jnp.sum(score_grad.astype(jnp.float32), axis=0),
        one_hot,
        precision=lax.Precision.HIGHEST,
    )
    projected_grad = jnp.stack([query_grad, key_grad, value_grad], axis=2).astype(jnp.bfloat16)
    projected_grad = projected_grad.reshape(sequences * TLEN, 3 * width_here)
    self_weight_grad = jnp.dot(normed_one.T, projected_grad, preferred_element_type=jnp.float32)
    normed_grad = over_heads(
        jnp.dot(projected_grad, self_weights.T, preferred_element_type=jnp.float32)
    )
    back_one, gain_one = rms_backward(normed_grad, unit_one, factor_one, norm_gains[0])
    target_grad = (grad_two + back_one).astype(jnp.bfloat16)
    row_grads = (
        lax.psum_scatter(self_weight_grad[:, :width_here], "pas", scatter_dimension=0, tiled=True),
        lax.psum_scatter(
            self_weight_grad[:, width_here : 2 * width_here], "pas", scatter_dimension=0, tiled=True
        ),
        lax.psum_scatter(
            self_weight_grad[:, 2 * width_here :], "pas", scatter_dimension=0, tiled=True
        ),
        lax.psum_scatter(cross_query_grad, "pas", scatter_dimension=0, tiled=True),
        lax.psum_scatter(kv_weight_grad[:, :width_here], "pas", scatter_dimension=0, tiled=True),
        lax.psum_scatter(kv_weight_grad[:, width_here:], "pas", scatter_dimension=0, tiled=True),
        lax.psum_scatter(expand_grad, "pas", scatter_dimension=0, tiled=True),
    )
    col_grads = (
        lax.psum_scatter(self_output_grad, "pas", scatter_dimension=1, tiled=True),
        lax.psum_scatter(cross_output_grad, "pas", scatter_dimension=1, tiled=True),
        lax.psum_scatter(reduce_grad, "pas", scatter_dimension=1, tiled=True),
    )
    gains_total, bias_total = lax.psum(
        (jnp.stack([gain_one, gain_two, gain_three]), bias_grad), "pas"
    )
    return (
        block_out.astype(jnp.bfloat16),
        target_grad,
        passage_grad,
        gains_total,
        row_grads[0],
        row_grads[1],
        row_grads[2],
        col_grads[0],
        bias_total,
        row_grads[3],
        row_grads[4],
        row_grads[5],
        col_grads[1],
        row_grads[6],
        col_grads[2],
    )


def solution(mesh):
    return jax.shard_map(
        body,
        mesh=mesh,
        in_specs=(
            P("pas", None),
            P("pas", None, "mdl"),
            P("pas"),
            P("pas"),
            P(),
            P("pas", "mdl"),
            P("pas", "mdl"),
            P("pas", "mdl"),
            P("mdl", "pas"),
            P(None, "mdl"),
            P("pas", "mdl"),
            P("pas", "mdl"),
            P("pas", "mdl"),
            P("mdl", "pas"),
            P("pas", "mdl"),
            P("mdl", "pas"),
            P("pas", None),
        ),
        out_specs=(
            P("pas", None),
            P("pas", None),
            P("pas", None, "mdl"),
            P(),
            P("pas", "mdl"),
            P("pas", "mdl"),
            P("pas", "mdl"),
            P("mdl", "pas"),
            P(None, "mdl"),
            P("pas", "mdl"),
            P("pas", "mdl"),
            P("pas", "mdl"),
            P("mdl", "pas"),
            P("pas", "mdl"),
            P("mdl", "pas"),
        ),
        check_vma=False,
    )
```

profile of v0, /device:TPU:0, one launch (start us, length us, event | category | flops | bytes accessed | tf_op | source)
XLA Modules:
  0.0 2176.3 jit_solution(16589914627440885935)
XLA Ops:
  21.4 44.9 %all_gather.37 = bf16[768,384]{1,0:T(8,128)(2,1)S(1)} all-gather(bf16[48,384]{1,0:T(8,128)(2,1)} %param.32), channel_id=1, replica_groups=mesh['pas'=16,'mdl'=2] {'pas'}, dimensions={0}, use_global_device_ids=true | all-gather | bytes 626688 | tf_op jit(solution)/shard_map/all_gather | solution.py:158
  66.2 38.7 %all_gather.38 = bf16[768,384]{1,0:T(8,128)(2,1)S(1)} all-gather(bf16[48,384]{1,0:T(8,128)(2,1)S(1)} %copy-done.57), channel_id=1, replica_groups=mesh['pas'=16,'mdl'=2] {'pas'}, dimensions={0}, use_global_device_ids=true | all-gather | bytes 626688 | tf_op jit(solution)/shard_map/all_gather | solution.py:159
  115.1 12.9 scatter_fusion
  132.9 110.6 %all_gather.33 = bf16[768,384]{1,0:T(8,128)(2,1)S(1)} all-gather(bf16[48,384]{1,0:T(8,128)(2,1)S(1)} %copy-done.58), channel_id=1, replica_groups=mesh['pas'=16,'mdl'=2] {'pas'}, dimensions={0}, use_global_device_ids=true | all-gather | bytes 626688 | tf_op jit(solution)/shard_map/all_gather | solution.py:154
  243.6 48.5 %all_gather.34 = bf16[768,384]{1,0:T(8,128)(2,1)S(1)} all-gather(bf16[48,384]{1,0:T(8,128)(2,1)S(1)} %copy-done.59), channel_id=1, replica_groups=mesh['pas'=16,'mdl'=2] {'pas'}, dimensions={0}, use_global_device_ids=true | all-gather | bytes 626688 | tf_op jit(solution)/shard_map/all_gather | solution.py:155
  292.2 39.0 %all_gather.35 = bf16[768,384]{1,0:T(8,128)(2,1)S(1)} all-gather(bf16[48,384]{1,0:T(8,128)(2,1)S(1)} %copy-done.60), channel_id=1, replica_groups=mesh['pas'=16,'mdl'=2] {'pas'}, dimensions={0}, use_global_device_ids=true | all-gather | bytes 626688 | tf_op jit(solution)/shard_map/all_gather | solution.py:156
  340.5 41.0 %all_gather.36 = bf16[384,768]{0,1:T(8,128)(2,1)S(1)} all-gather(bf16[384,48]{0,1:T(8,128)(2,1)S(1)} %copy-done.61), channel_id=1, replica_groups=mesh['pas'=16,'mdl'=2] {'pas'}, dimensions={1}, use_global_device_ids=true | all-gather | bytes 626688 | tf_op jit(solution)/shard_map/all_gather | solution.py:163
  383.5 43.2 %all_gather.40 = bf16[768,384]{1,0:T(8,128)(2,1)} all-gather(bf16[48,384]{1,0:T(8,128)(2,1)S(1)} %copy-done.62), channel_id=1, replica_groups=mesh['pas'=16,'mdl'=2] {'pas'}, dimensions={0}, use_global_device_ids=true | all-gather | bytes 626688 | tf_op jit(solution)/shard_map/all_gather | solution.py:157
  426.7 44.3 %all_gather.41 = bf16[384,768]{0,1:T(8,128)(2,1)} all-gather(bf16[384,48]{0,1:T(8,128)(2,1)S(1)} %copy-done.63), channel_id=1, replica_groups=mesh['pas'=16,'mdl'=2] {'pas'}, dimensions={1}, use_global_device_ids=true | all-gather | bytes 626688 | tf_op jit(solution)/shard_map/all_gather | solution.py:164
  486.4 11.5 copy.104
  497.8 11.1 reshape.511
  526.7 10.4 all-reduce.10.cloned.1.call-done
  538.4 45.1 %all-gather.6.cloned.1.call-done = bf16[768,1536]{1,0:T(8,128)(2,1)} async-done(((bf16[48,1536]{1,0:T(8,128)(2,1)}), bf16[768,1536]{1,0:T(8,128)(2,1)}) %all-gather.6.cloned.1.call-update) | async-done | bytes 2359312 | tf_op jit(solution)/shard_map/all_gather | solution.py:160
  591.2 17.6 all-reduce.12.cloned.1.call-done
  653.2 10.7 reshape.580
  664.0 11.3 copy.111
  678.0 20.2 scatter_fusion.1
  718.6 16.5 all-reduce.14.cloned.1.call-done
  746.5 48.9 %all-to-all-done.2 = bf16[48,64,768]{2,1,0:T(8,128)(2,1)} async-done(((bf16[48,64,768]{2,1,0:T(8,128)(2,1)}), bf16[48,64,768]{2,1,0:T(8,128)(2,1)}, u32[]{:S(2)}, u32[]{:S(2)}) %all-to-all-start.2) | async-done | bytes 4718624 | tf_op jit(solution)/shard_map/all_to_all | solution.py:296
  808.0 11.5 copy.119
  819.4 11.1 reshape.597
  864.9 90.5 %all-reduce = (f32[3,768]{1,0:T(4,128)}, f32[32,6]{0,1:T(8,128)}) all-reduce(f32[3,768]{1,0:T(4,128)S(1)} %pad_maximum_fusion.4, f32[32,6]{0,1:T(8,128)S(1)} %fusion.35), channel_id=1, replica_groups=mesh['pas'=16,'mdl'=2] {'pas'}, use_global_device_ids=true, to_apply=%region_35.37 | all-reduce | flops 2496 | bytes 19968 | tf_op jit(solution)/shard_map/psum | solution.py:360
  969.6 20.2 reduce-scatter.28.cloned.1.call-done
  989.8 128.0 %reduce-scatter.26.cloned.1.call-done = f32[48,384]{1,0:T(8,128)} async-done(((f32[768,384]{1,0:T(8,128)}), f32[48,384]{1,0:T(8,128)}) %reduce-scatter.26.cloned.1.call-update) | async-done | bytes 73744 | tf_op jit(solution)/shard_map/reduce_scatter | solution.py:350
  1117.8 127.8 %reduce-scatter.24.cloned.1.call-done = f32[384,48]{0,1:T(8,128)} async-done(((f32[384,768]{0,1:T(8,128)}), f32[384,48]{0,1:T(8,128)}) %reduce-scatter.24.cloned.1.call-update) | async-done | bytes 73744 | tf_op jit(solution)/shard_map/reduce_scatter | solution.py:356
  1245.6 128.0 %reduce-scatter.18.cloned.1.call-done = f32[48,384]{1,0:T(8,128)} async-done(((f32[768,384]{1,0:T(8,128)}), f32[48,384]{1,0:T(8,128)}) %reduce-scatter.18.cloned.1.call-update) | async-done | bytes 73744 | tf_op jit(solution)/shard_map/reduce_scatter | solution.py:343
  1373.6 127.7 %reduce-scatter.20.cloned.1.call-done = f32[48,384]{1,0:T(8,128)} async-done(((f32[768,384]{1,0:T(8,128)}), f32[48,384]{1,0:T(8,128)}) %reduce-scatter.20.cloned.1.call-update) | async-done | bytes 73744 | tf_op jit(solution)/shard_map/reduce_scatter | solution.py:344
  1501.4 127.9 %reduce-scatter.22.cloned.1.call-done = f32[48,384]{1,0:T(8,128)} async-done(((f32[768,384]{1,0:T(8,128)}), f32[48,384]{1,0:T(8,128)}) %reduce-scatter.22.cloned.1.call-update) | async-done | bytes 73744 | tf_op jit(solution)/shard_map/reduce_scatter | solution.py:347
  1629.3 141.5 %reduce-scatter.30.cloned.1.call-done = f32[48,1536]{1,0:T(8,128)} async-done(((f32[768,1536]{1,0:T(8,128)}), f32[48,1536]{1,0:T(8,128)}) %reduce-scatter.30.cloned.1.call-update) | async-done | bytes 294928 | tf_op jit(solution)/shard_map/reduce_scatter | solution.py:353
  1770.7 142.4 %reduce-scatter.32.cloned.1.call-done = f32[1536,48]{0,1:T(8,128)} async-done(((f32[1536,768]{0,1:T(8,128)}), f32[1536,48]{0,1:T(8,128)}) %reduce-scatter.32.cloned.1.call-update) | async-done | bytes 294928 | tf_op jit(solution)/shard_map/reduce_scatter | solution.py:358
  1913.2 127.9 %reduce-scatter.36.cloned.1.call-done = f32[48,384]{1,0:T(8,128)} async-done(((f32[768,384]{1,0:T(8,128)}), f32[48,384]{1,0:T(8,128)}) %reduce-scatter.36.cloned.1.call-update) | async-done | bytes 73744
  2041.0 127.7 %reduce-scatter.38.cloned.1.call-done = f32[48,384]{1,0:T(8,128)} async-done(((f32[768,384]{1,0:T(8,128)}), f32[48,384]{1,0:T(8,128)}) %reduce-scatter.38.cloned.1.call-update) | async-done | bytes 73744
  (340 shorter events, 220.8 us)
Async XLA Ops:
  8.0 325.5 %copy-start = (f32[32,6]{0,1:T(8,128)S(1)}, f32[32,6]{0,1:T(8,128)}, u32[]{:S(2)}) copy-start(f32[32,6]{0,1:T(8,128)} %param.30) | copy-start | bytes 2308
  8.0 96.9 %all-gather.4.cloned.1.call-start = ((), (), s32[]{:S(2)}) async-start(), calls=%async_computation.15 | async-start | bytes 5898240 | tf_op jit(solution)/shard_map/all_gather | solution.py:207
  11.5 103.6 %copy-start.65 = (s32[40]{0:T(128)}, s32[40]{0:T(128)S(1)}, u32[]{:S(2)}) copy-start(s32[40]{0:T(128)S(1)} %get-tuple-element.92) | copy-start | bytes 484
  13.1 115.0 %all-to-all-start.1 = ((bf16[16,3,1]{1,2,0:T(2,128)(2,1)}), bf16[16,3,1]{1,2,0:T(2,128)(2,1)S(1)}, u32[]{:S(2)}, u32[]{:S(2)}) async-start(bf16[16,3,1]{1,2,0:T(2,128)(2,1)} %all_to_all.16), calls=%async_computation.1 | async-start | bytes 16384 | tf_op jit(solution)/shard_map/all_to_all | solution.py:219
  128.1 115.5 %copy-start.59 = (bf16[48,384]{1,0:T(8,128)(2,1)S(1)}, bf16[48,384]{1,0:T(8,128)(2,1)}, u32[]{:S(2)}) copy-start(bf16[48,384]{1,0:T(8,128)(2,1)} %param.27) | copy-start | bytes 110596
  128.1 348.4 %all-to-all-start = ((bf16[48,64,768]{2,1,0:T(8,128)(2,1)}), bf16[48,64,768]{2,1,0:T(8,128)(2,1)}, u32[]{:S(2)}, u32[]{:S(2)}) async-start(bf16[48,64,768]{2,1,0:T(8,128)(2,1)} %scatter_fusion), calls=%async_computation | async-start | bytes 9437184 | tf_op jit(solution)/shard_map/all_to_all | solution.py:212
  132.8 159.4 %copy-start.60 = (bf16[48,384]{1,0:T(8,128)(2,1)S(1)}, bf16[48,384]{1,0:T(8,128)(2,1)}, u32[]{:S(2)}) copy-start(bf16[48,384]{1,0:T(8,128)(2,1)} %param.28) | copy-start | bytes 110596
  132.8 340.7 %all-reduce.8.cloned.1.call-start = ((), (), s32[]{:S(2)}) async-start(), calls=%async_computation.14 | async-start | bytes 1572864 | tf_op jit(solution)/shard_map/psum | solution.py:45
  243.5 87.8 %copy-start.21 = (bf16[256,768]{1,0:T(8,128)(2,1)S(1)}, bf16[256,768]{1,0:T(8,128)(2,1)}, u32[]{:S(2)}) copy-start(bf16[256,768]{1,0:T(8,128)(2,1)} %param.21) | copy-start | bytes 1179652
  340.5 86.2 %copy-start.63 = (bf16[384,48]{0,1:T(8,128)(2,1)S(1)}, bf16[384,48]{0,1:T(8,128)(2,1)}, u32[]{:S(2)}) copy-start(bf16[384,48]{0,1:T(8,128)(2,1)} %param.34) | copy-start | bytes 110596
  381.5 93.3 %copy-start.23 = (bf16[384,768]{0,1:T(8,128)(2,1)}, bf16[384,768]{0,1:T(8,128)(2,1)S(1)}, u32[]{:S(2)}) copy-start(bf16[384,768]{0,1:T(8,128)(2,1)S(1)} %all_gather.36) | copy-start | bytes 1769476
  382.8 139.9 %all-gather.8.cloned.1.call-start = ((), (), s32[]{:S(2)}) async-start(), calls=%async_computation.18 | async-start | bytes 2506752 | tf_op jit(solution)/shard_map/all_gather | solution.py:165
  383.4 153.7 %all-reduce.10.cloned.1.call-start = ((), (), s32[]{:S(2)}) async-start(), calls=%async_computation.16 | async-start | bytes 1572864 | tf_op jit(solution)/shard_map/psum | solution.py:45
  521.7 61.9 %all-gather.6.cloned.1.call-start = ((), (), s32[]{:S(2)}) async-start(), calls=%async_computation.17 | async-start | bytes 2506752 | tf_op jit(solution)/shard_map/all_gather | solution.py:160
  522.3 86.5 %all-reduce.12.cloned.1.call-start = ((), (), s32[]{:S(2)}) async-start(), calls=%async_computation.19 | async-start | bytes 1572864 | tf_op jit(solution)/shard_map/psum | solution.py:45
  698.2 97.2 %all-to-all-start.2 = ((bf16[48,64,768]{2,1,0:T(8,128)(2,1)}), bf16[48,64,768]{2,1,0:T(8,128)(2,1)}, u32[]{:S(2)}, u32[]{:S(2)}) async-start(bf16[48,64,768]{2,1,0:T(8,128)(2,1)} %scatter_fusion.1), calls=%async_computation.2 | async-start | bytes 9437184 | tf_op jit(solution)/shard_map/all_to_all | solution.py:296
  705.1 29.9 %all-reduce.14.cloned.1.call-start = ((), (), s32[]{:S(2)}) async-start(), calls=%async_computation.20 | async-start | bytes 1572864 | tf_op jit(solution)/shard_map/psum | solution.py:45
  714.4 149.0 %all-reduce.16.cloned.1.call-start = ((), (), s32[]{:S(2)}) async-start(), calls=%async_computation.32 | async-start | bytes 3145728 | tf_op jit(solution)/shard_map/psum | solution.py:45
  738.2 96.6 %copy-start.15 = (f32[256,768]{1,0:T(8,128)}, f32[256,768]{1,0:T(8,128)S(1)}, u32[]{:S(2)}) copy-start(f32[256,768]{1,0:T(8,128)S(1)} %multiply_add_fusion) | copy-start | bytes 2359300
  746.2 211.7 %reduce-scatter.34.cloned.1.call-start = ((), (), s32[]{:S(2)}) async-start(), calls=%async_computation.29 | async-start | bytes 5898240
  830.6 159.2 %reduce-scatter.28.cloned.1.call-start = ((), (), s32[]{:S(2)}) async-start(), calls=%async_computation.26 | async-start | bytes 1253376 | tf_op jit(solution)/shard_map/reduce_scatter | solution.py:357
  833.2 284.6 %reduce-scatter.26.cloned.1.call-start = ((), (), s32[]{:S(2)}) async-start(), calls=%async_computation.25 | async-start | bytes 1253376 | tf_op jit(solution)/shard_map/reduce_scatter | solution.py:350
  834.8 410.8 %reduce-scatter.24.cloned.1.call-start = ((), (), s32[]{:S(2)}) async-start(), calls=%async_computation.24 | async-start | bytes 1253376 | tf_op jit(solution)/shard_map/reduce_scatter | solution.py:356
  836.3 537.3 %reduce-scatter.18.cloned.1.call-start = ((), (), s32[]{:S(2)}) async-start(), calls=%async_computation.21 | async-start | bytes 1253376 | tf_op jit(solution)/shard_map/reduce_scatter | solution.py:343
  839.1 662.3 %reduce-scatter.20.cloned.1.call-start = ((), (), s32[]{:S(2)}) async-start(), calls=%async_computation.22 | async-start | bytes 1253376 | tf_op jit(solution)/shard_map/reduce_scatter | solution.py:344
  839.7 789.6 %reduce-scatter.22.cloned.1.call-start = ((), (), s32[]{:S(2)}) async-start(), calls=%async_computation.23 | async-start | bytes 1253376 | tf_op jit(solution)/shard_map/reduce_scatter | solution.py:347
  840.4 930.3 %reduce-scatter.30.cloned.1.call-start = ((), (), s32[]{:S(2)}) async-start(), calls=%async_computation.27 | async-start | bytes 5013504 | tf_op jit(solution)/shard_map/reduce_scatter | solution.py:353
  843.5 1069.6 %reduce-scatter.32.cloned.1.call-start = ((), (), s32[]{:S(2)}) async-start(), calls=%async_computation.28 | async-start | bytes 5013504 | tf_op jit(solution)/shard_map/reduce_scatter | solution.py:358
  848.1 1192.9 %reduce-scatter.36.cloned.1.call-start = ((), (), s32[]{:S(2)}) async-start(), calls=%async_computation.30 | async-start | bytes 1253376
  859.5 1309.3 %reduce-scatter.38.cloned.1.call-start = ((), (), s32[]{:S(2)}) async-start(), calls=%async_computation.31 | async-start | bytes 1253376
  862.0 93.5 %copy-start.16 = (f32[256,768]{1,0:T(8,128)S(1)}, f32[256,768]{1,0:T(8,128)}, u32[]{:S(2)}) copy-start(f32[256,768]{1,0:T(8,128)} %copy-done.15) | copy-start | bytes 2359300
  963.9 1204.9 %copy-start.1 = (f32[32,6]{0,1:T(8,128)S(1)}, f32[32,6]{0,1:T(8,128)}, u32[]{:S(2)}) copy-start(f32[32,6]{0,1:T(8,128)} %param.30) | copy-start | bytes 2308
  (68 other events, 660.3 us)
Sparse Core Ops, SparseCore 0:
  10.4 15.8 all-gather.3
  383.0 15.0 all-reduce.7
  521.8 15.2 all-reduce.9
  591.3 17.4 all-reduce.11
  714.5 20.4 all-reduce.13
  746.3 21.6 all-reduce.15
  830.7 29.0 reduce-scatter.33
  865.1 124.7 reduce-scatter.27
  995.2 122.5 reduce-scatter.25
  1123.0 122.5 reduce-scatter.23
  1250.9 122.6 reduce-scatter.17
  1378.8 122.5 reduce-scatter.19
  1506.7 122.5 reduce-scatter.21
  1634.9 135.8 reduce-scatter.29
  1777.1 135.9 reduce-scatter.31
  1918.3 122.6 reduce-scatter.35
  2046.2 122.5 reduce-scatter.37
Sparse Core Ops, SparseCore 1:
  386.1 61.5 all-gather.7
  525.0 58.5 all-gather.5
where the time goes:
time: 2190 us; the launch traced here: 2180 us
  waiting for transfers between devices  1340 us (61%)
  blocking collectives  501 us (23%)
  local copies, waits for them, and re-layouts  136 us (6%)
  matrix products  105 us (5%)
  other arithmetic  55.5 us (3%)
    unnamed x22, waiting for transfers between devices  259 us
    reduce_scatter x1, waiting for transfers between devices, body(): lax.psum_scatter(reduce_grad, 'pas', scatter_dimension=1, tiled=True)  142 us
    reduce_scatter x1, waiting for transfers between devices, body(): lax.psum_scatter(expand_grad, 'pas', scatter_dimension=0, tiled=True)  141 us
    reduce_scatter x1, waiting for transfers between devices, body(): lax.psum_scatter(self_weight_grad[:, :width_here], 'pas', scatter_dimensi...  128 us
    reduce_scatter x1, waiting for transfers between devices, body(): lax.psum_scatter(cross_query_grad, 'pas', scatter_dimension=0, tiled=True)  128 us
    reduce_scatter x1, waiting for transfers between devices, body(): lax.psum_scatter(self_weight_grad[:, 2 * width_here:], 'pas', scatter_dim...  128 us
    reduce_scatter x1, waiting for transfers between devices, body(): lax.psum_scatter(self_output_grad, 'pas', scatter_dimension=1, tiled=True)  128 us
    reduce_scatter x1, waiting for transfers between devices, body(): lax.psum_scatter(self_weight_grad[:, width_here:2 * width_here], 'pas', s...  128 us
  transfers between devices with their start and end apart: 22, of which 15 were waited for; matrix products, arithmetic and copies ran while one was open for 9% of the time, Pallas kernels for 0%

commit v1 on v0

--- a/solution.py
+++ b/solution.py
@@ -5,6 +5,8 @@
 import jax.numpy as jnp
 import numpy as np
 from jax import lax
+from jax.experimental import pallas as pl
+from jax.experimental.pallas import tpu as pltpu
 from jax.sharding import PartitionSpec as P
 
 HEAD_DIM = 64
@@ -123,7 +125,7 @@
     return jnp.zeros((total_rows,) + rows.shape[1:], rows.dtype).at[gather_index].add(rows)
 
 
-def body(
+def body_any(
     target_states,
     passage_states,
     slot_query,
@@ -379,9 +381,702 @@
     )
 
 
+CHIPS = 16
+RANKS = 3
+FLAG_ROWS = 16
+MESH_ID = pl.DeviceIdType.MESH
+VMEM_LIMIT = 56 * 2**20
+
+
+def fits(mesh):
+    return mesh.shape["pas"] == CHIPS and mesh.shape["mdl"] == 2
+
+
+def places():
+    me, core = lax.axis_index("pas"), lax.axis_index("mdl")
+    x, y, z = me % 2, (me // 2) % 2, me // 4
+    across_x, across_y = me + 1 - 2 * x, me + 2 - 4 * y
+    near = across_y + (across_x - across_y) * core
+    far = across_x + (across_y - across_x) * core
+    return me, core, x, y, z, near, far
+
+
+def remote(src, dst, send_sem, recv_sem, device):
+    return pltpu.make_async_remote_copy(
+        src_ref=src,
+        dst_ref=dst,
+        send_sem=send_sem,
+        recv_sem=recv_sem,
+        device_id=device,
+        device_id_type=MESH_ID,
+    )
+
+
+def greet_all(me, core):
+    barrier = pltpu.get_barrier_semaphore()
+    for k in range(1, CHIPS):
+        pl.semaphore_signal(
+            barrier, inc=1, device_id=((me + k) % CHIPS, core), device_id_type=MESH_ID
+        )
+    pl.semaphore_signal(barrier, inc=1, device_id=(me, 1 - core), device_id_type=MESH_ID)
+    pl.semaphore_wait(barrier, CHIPS)
+
+
+def gather_kernel(
+    index_ref,
+    shard_ref,
+    passage_ref,
+    flag_ref,
+    full_ref,
+    states_ref,
+    outgoing,
+    own_sem,
+    z_send,
+    z_recv,
+    near_send,
+    near_recv,
+    far_send,
+    far_recv,
+    slot_send,
+    slot_recv,
+    core_send,
+    core_recv,
+    slot_own,
+):
+    me, core, x, y, z, near, far = places()
+    groups = shard_ref.shape[0]
+    greet_all(me, core)
+
+    def z_copy(g, k):
+        return remote(
+            shard_ref.at[g],
+            full_ref.at[g, z, y, x],
+            z_send.at[g, k - 1],
+            z_recv.at[g, k - 1],
+            ((me + 4 * k) % CHIPS, core),
+        )
+
+    def near_copy(g):
+        block = full_ref.at[g, :, y, x]
+        return remote(block, block, near_send.at[g], near_recv.at[g], (near, core))
+
+    def far_copy(g, across_x):
+        block = full_ref.at[g, :, :, x] if across_x else full_ref.at[g, :, y, :]
+        return remote(block, block, far_send.at[g], far_recv.at[g], (far, core))
+
+    def own_copy(g):
+        return pltpu.make_async_copy(shard_ref.at[g], full_ref.at[g, z, y, x], own_sem.at[g])
+
+    def slot_copy(k):
+        to = (me + k) % CHIPS
+        return remote(
+            outgoing.at[to],
+            states_ref.at[core, me],
+            slot_send.at[k - 1],
+            slot_recv.at[k - 1],
+            (to, core),
+        )
+
+    def core_copy(k):
+        block = states_ref.at[core, (me + CHIPS - k) % CHIPS]
+        return remote(block, block, core_send.at[k], core_recv.at[k], (me, 1 - core))
+
+    for g in range(groups):
+        own_copy(g).start()
+        for k in range(1, 4):
+            z_copy(g, k).start()
+
+    def fill(to, carry):
+        for rank in range(RANKS):
+            rows = passage_ref.shape[1]
+            outgoing[to, rank * rows : (rank + 1) * rows, :] = passage_ref[
+                index_ref[to * RANKS + rank]
+            ]
+        outgoing[to, RANKS * passage_ref.shape[1] :, :] = flag_ref[to]
+        return carry
+
+    lax.fori_loop(0, CHIPS, fill, 0)
+    for k in range(1, CHIPS):
+        slot_copy(k).start()
+    mine = pltpu.make_async_copy(outgoing.at[me], states_ref.at[core, me], slot_own)
+    mine.start()
+
+    def second(g):
+        own_copy(g).wait()
+        for k in range(1, 4):
+            z_copy(g, k).wait_recv()
+        near_copy(g).start()
+
+    def third(g):
+        near_copy(g).wait_recv()
+
+        @pl.when(core == 0)
+        def _():
+            far_copy(g, True).start()
+
+        @pl.when(core == 1)
+        def _():
+            far_copy(g, False).start()
+
+    second(0)
+    second(1)
+    third(0)
+    second(2)
+    third(1)
+    second(3)
+    third(2)
+    third(3)
+    mine.wait()
+    core_copy(0).start()
+    for k in range(1, CHIPS):
+        slot_copy(k).wait_recv()
+        core_copy(k).start()
+    for g in range(groups):
+        far_copy(g, True).wait_recv()
+    for k in range(CHIPS):
+        core_copy(k).wait()
+    for k in range(1, CHIPS):
+        slot_copy(k).wait_send()
+    for g in range(groups):
+        for k in range(1, 4):
+            z_copy(g, k).wait_send()
+        near_copy(g).wait_send()
+        far_copy(g, True).wait_send()
+
+
+ANY = pl.BlockSpec(memory_space=pl.ANY)
+IN_VMEM = pl.BlockSpec(memory_space=pltpu.VMEM)
+IN_SMEM = pl.BlockSpec(memory_space=pltpu.SMEM)
+DMA = pltpu.SemaphoreType.DMA
+
+
+def gather_everything(index, shards, passages, flags):
+    groups, rows, columns = shards.shape
+    passage_len, half = passages.shape[1:]
+    block_rows = RANKS * passage_len + FLAG_ROWS
+    return pl.pallas_call(
+        gather_kernel,
+        out_shape=(
+            jax.ShapeDtypeStruct((groups, 4, 2, 2, rows, columns), jnp.bfloat16),
+            jax.ShapeDtypeStruct((2, CHIPS, block_rows, half), jnp.bfloat16),
+        ),
+        in_specs=[IN_SMEM, ANY, IN_VMEM, IN_VMEM],
+        out_specs=(ANY, ANY),
+        scratch_shapes=[
+            pltpu.VMEM((CHIPS, block_rows, half), jnp.bfloat16),
+            DMA((groups,)),
+            DMA((groups, 3)),
+            DMA((groups, 3)),
+            DMA((groups,)),
+            DMA((groups,)),
+            DMA((groups,)),
+            DMA((groups,)),
+            DMA((CHIPS - 1,)),
+            DMA((CHIPS - 1,)),
+            DMA((CHIPS,)),
+            DMA((CHIPS,)),
+            DMA,
+        ],
+        compiler_params=pltpu.CompilerParams(
+            collective_id=0, has_side_effects=True, vmem_limit_bytes=VMEM_LIMIT
+        ),
+    )(index, shards, passages, flags)
+
+
+def pair_kernel(mine_ref, sum_ref, other, send_sem, recv_sem):
+    partner = (lax.axis_index("pas"), 1 - lax.axis_index("mdl"))
+    barrier = pltpu.get_barrier_semaphore()
+    pl.semaphore_signal(barrier, inc=1, device_id=partner, device_id_type=MESH_ID)
+    pl.semaphore_wait(barrier, 1)
+    copy = remote(mine_ref, other, send_sem, recv_sem, partner)
+    copy.start()
+    copy.wait()
+    sum_ref[...] = mine_ref[...] + other[...]
+
+
+def over_pair(partial_rows):
+    return pl.pallas_call(
+        pair_kernel,
+        out_shape=jax.ShapeDtypeStruct(partial_rows.shape, partial_rows.dtype),
+        in_specs=[IN_VMEM],
+        out_specs=IN_VMEM,
+        scratch_shapes=[pltpu.VMEM(partial_rows.shape, partial_rows.dtype), DMA, DMA],
+        compiler_params=pltpu.CompilerParams(
+            collective_id=1, has_side_effects=True, vmem_limit_bytes=VMEM_LIMIT
+        ),
+    )(partial_rows)
+
+
+def scatter_kernel(
+    position_ref,
+    grads_ref,
+    passage_ref,
+    small_ref,
+    shard_ref,
+    slots_ref,
+    total_ref,
+    far_got,
+    far_sum,
+    near_got,
+    near_sum,
+    z_got,
+    pair_got,
+    pair_sum,
+    slot_got,
+    small_got,
+    small_sum,
+    far_send,
+    far_recv,
+    near_send,
+    near_recv,
+    z_send,
+    z_recv,
+    pair_send,
+    pair_recv,
+    slot_send,
+    slot_recv,
+    small_send,
+    small_recv,
+):
+    me, core, x, y, z, near, far = places()
+    groups = grads_ref.shape[0]
+    across_x, across_y = me + 1 - 2 * x, me + 2 - 4 * y
+    kept = (1 - core) * y + core * x
+    greet_all(me, core)
+
+    def far_copy(g, over_x):
+        block = grads_ref.at[g, :, :, 1 - x] if over_x else grads_ref.at[g, :, 1 - y, :]
+        return remote(block, far_got.at[g], far_send.at[g], far_recv.at[g], (far, core))
+
+    def near_copy(g):
+        return remote(
+            far_sum.at[g, :, 1 - kept], near_got.at[g], near_send.at[g], near_recv.at[g], (near, core)
+        )
+
+    def z_copy(g, k):
+        return remote(
+            near_sum.at[g, (z + k) % 4],
+            z_got.at[g, k - 1],
+            z_send.at[g, k - 1],
+            z_recv.at[g, k - 1],
+            ((me + 4 * k) % CHIPS, core),
+        )
+
+    def pair_copy(k):
+        to = (me + k) % CHIPS
+        return remote(
+            passage_ref.at[1 - core, to],
+            pair_got.at[to],
+            pair_send.at[k],
+            pair_recv.at[k],
+            (me, 1 - core),
+        )
+
+    def slot_copy(k):
+        to = (me + k) % CHIPS
+        return remote(
+            pair_sum.at[to],
+            slot_got.at[me],
+            slot_send.at[k - 1],
+            slot_recv.at[k - 1],
+            (to, core),
+        )
+
+    def small_copy(step):
+        if step == 0:
+            return remote(
+                small_ref, small_got.at[0], small_send.at[0], small_recv.at[0], (across_x, core)
+            )
+        if step == 1:
+            return remote(
+                small_sum.at[0],
+                small_got.at[1],
+                small_send.at[1],
+                small_recv.at[1],
+                (across_y, core),
+            )
+        return remote(
+            small_sum.at[1],
+            small_got.at[2 + z],
+            small_send.at[step],
+            small_recv.at[step],
+            ((me + 4 * (step - 1)) % CHIPS, core),
+        )
+
+    for k in range(CHIPS):
+        pair_copy(k).start()
+    small_copy(0).start()
+    for g in range(groups):
+
+        @pl.when(core == 0)
+        def _():
+            far_copy(g, True).start()
+
+        @pl.when(core == 1)
+        def _():
+            far_copy(g, False).start()
+
+    for k in list(range(1, CHIPS)) + [0]:
+        to = (me + k) % CHIPS
+        pair_copy(k).wait_recv()
+        pair_sum[to] = (
+            passage_ref[core, to].astype(jnp.float32) + pair_got[to].astype(jnp.float32)
+        ).astype(jnp.bfloat16)
+        if k:
+            slot_copy(k).start()
+    slot_got[me] = pair_sum[me]
+    small_copy(0).wait_recv()
+    small_sum[0] = small_ref[...] + small_got[0]
+    small_copy(1).start()
+
+    def far_add(g):
+        far_copy(g, True).wait_recv()
+
+        def step(i, carry):
+            zi, o = i // 2, i % 2
+            mine = grads_ref[g, zi, (1 - core) * o + core * y, (1 - core) * x + core * o]
+            far_sum[g, zi, o] = (
+                mine.astype(jnp.float32) + far_got[g, zi, o].astype(jnp.float32)
+            ).astype(jnp.bfloat16)
+            return carry
+
+        lax.fori_loop(0, 8, step, 0)
+        near_copy(g).start()
+
+    def near_add(g):
+        near_copy(g).wait_recv()
+
+        def step(zi, carry):
+            near_sum[g, zi] = (
+                far_sum[g, zi, kept].astype(jnp.float32) + near_got[g, zi].astype(jnp.float32)
+            ).astype(jnp.bfloat16)
+            return carry
+
+        lax.fori_loop(0, 4, step, 0)
+        for k in range(1, 4):
+            z_copy(g, k).start()
+
+    def z_add(g):
+        for k in range(1, 4):
+            z_copy(g, k).wait_recv()
+        total = near_sum[g, z].astype(jnp.float32)
+        for k in range(3):
+            total = total + z_got[g, k].astype(jnp.float32)
+        shard_ref[g] = total
+
+    far_add(0)
+    small_copy(1).wait_recv()
+    small_sum[1] = small_sum[0] + small_got[1]
+    for step in range(2, 5):
+        small_copy(step).start()
+    small_got[2 + z] = small_sum[1]
+    far_add(1)
+    near_add(0)
+    far_add(2)
+    near_add(1)
+    z_add(0)
+    far_add(3)
+    near_add(2)
+    z_add(1)
+    near_add(3)
+    z_add(2)
+    z_add(3)
+    for step in range(2, 5):
+        small_copy(step).wait_recv()
+    total_ref[...] = small_got[2] + small_got[3] + small_got[4] + small_got[5]
+    for k in range(1, CHIPS):
+        slot_copy(k).wait_recv()
+    rows = slots_ref.shape[1]
+
+    def pick(slot, carry):
+        at = position_ref[slot]
+        slots_ref[slot] = slot_got[at // RANKS, pl.ds(at % RANKS * rows, rows), :]
+        return carry
+
+    lax.fori_loop(0, slots_ref.shape[0], pick, 0)
+    for g in range(groups):
+        far_copy(g, True).wait_send()
+        near_copy(g).wait_send()
+        for k in range(1, 4):
+            z_copy(g, k).wait_send()
+    for k in range(CHIPS):
+        pair_copy(k).wait_send()
+    for k in range(1, CHIPS):
+        slot_copy(k).wait_send()
+    for step in range(5):
+        small_copy(step).wait_send()
+
+
+def scatter_everything(position, grads, passage_parts, small, slots):
+    groups, _, _, _, rows, columns = grads.shape
+    _, _, block_rows, half = passage_parts.shape
+    low = jnp.bfloat16
+    return pl.pallas_call(
+        scatter_kernel,
+        out_shape=(
+            jax.ShapeDtypeStruct((groups, rows, columns), jnp.float32),
+            jax.ShapeDtypeStruct((slots, block_rows // RANKS, half), low),
+            jax.ShapeDtypeStruct(small.shape, jnp.float32),
+        ),
+        in_specs=[IN_SMEM, IN_VMEM, IN_VMEM, IN_VMEM],
+        out_specs=(IN_VMEM, IN_VMEM, IN_VMEM),
+        scratch_shapes=[
+            pltpu.VMEM((groups, 4, 2, rows, columns), low),
+            pltpu.VMEM((groups, 4, 2, rows, columns), low),
+            pltpu.VMEM((groups, 4, rows, columns), low),
+            pltpu.VMEM((groups, 4, rows, columns), low),
+            pltpu.VMEM((groups, 3, rows, columns), low),
+            pltpu.VMEM((CHIPS, block_rows, half), low),
+            pltpu.VMEM((CHIPS, block_rows, half), low),
+            pltpu.VMEM((CHIPS, block_rows, half), low),
+            pltpu.VMEM((6,) + small.shape, jnp.float32),
+            pltpu.VMEM((2,) + small.shape, jnp.float32),
+            DMA((groups,)),
+            DMA((groups,)),
+            DMA((groups,)),
+            DMA((groups,)),
+            DMA((groups, 3)),
+            DMA((groups, 3)),
+            DMA((CHIPS,)),
+            DMA((CHIPS,)),
+            DMA((CHIPS - 1,)),
+            DMA((CHIPS - 1,)),
+            DMA((5,)),
+            DMA((5,)),
+        ],
+        compiler_params=pltpu.CompilerParams(
+            collective_id=2, has_side_effects=True, vmem_limit_bytes=VMEM_LIMIT
+        ),
+    )(position, grads, passage_parts, small)
+
+
+def rows_nt(left, right):
+    return lax.dot_general(
+        left, right, (((1,), (1,)), ((), ())), preferred_element_type=jnp.float32
+    )
+
+
+def rows_tn(left, right):
+    return lax.dot_general(
+        left, right, (((0,), (0,)), ((), ())), preferred_element_type=jnp.float32
+    )
+
+
+def route(slot_query, slot_live):
+    matching = slot_query[:, None] == slot_query[None, :]
+    earlier = jnp.tril(jnp.ones(matching.shape, jnp.bool_), -1)
+    position = slot_query * RANKS + jnp.sum(jnp.logical_and(matching, earlier), axis=1).astype(
+        jnp.int32
+    )
+    here = position[None, :] == jnp.arange(CHIPS * RANKS, dtype=jnp.int32)[:, None]
+    slots = slot_query.shape[0]
+    index = jnp.sum(jnp.where(here, jnp.arange(slots, dtype=jnp.int32)[None, :], 0), axis=1)
+    live = jnp.sum(jnp.where(here, slot_live[None, :], 0), axis=1)
+    return position, index, live
+
+
+def body(
+    target_states,
+    passage_states,
+    slot_query,
+    slot_live,
+    norm_gains,
+    self_query,
+    self_key,
+    self_value,
+    self_output,
+    position_bias,
+    cross_query,
+    cross_key,
+    cross_value,
+    cross_output,
+    expand_weight,
+    reduce_weight,
+    output_cotangent,
+):
+    low = jnp.bfloat16
+    width_here = self_query.shape[1]
+    heads_here = width_here // HEAD_DIM
+    slots_here, passage_len, half = passage_states.shape
+    bucket_count = position_bias.shape[0]
+    shards = jnp.stack(
+        [
+            jnp.concatenate([self_query, self_key, self_value, self_output.T], axis=1),
+            jnp.concatenate([cross_query, cross_key, cross_value, cross_output.T], axis=1),
+            expand_weight,
+            reduce_weight.T,
+        ]
+    )
+    position, index, live = route(slot_query, slot_live)
+    flags = jnp.repeat(live.reshape(CHIPS, RANKS), passage_len, axis=1).astype(low)
+    flags = jnp.pad(flags, ((0, 0), (0, half - RANKS * passage_len)))
+    flags = jnp.broadcast_to(flags[:, None, :], (CHIPS, FLAG_ROWS, half))
+    full, states = gather_everything(index, shards, passage_states, flags)
+    full = full.reshape(4, -1, full.shape[-1])
+    w = width_here
+    self_in, output_t = full[0, :, : 3 * w], full[0, :, 3 * w :]
+    cross_query_full = full[1, :, :w]
+    kv_weights = full[1, :, w : 3 * w]
+    cross_output_t = full[1, :, 3 * w :]
+    expand_full, reduce_t = full[2], full[3]
+    key_rows_n = CHIPS * RANKS * passage_len
+    live_keys = states[0, :, RANKS * passage_len, : RANKS * passage_len].reshape(1, key_rows_n)
+    allowed = (live_keys > 0)[:, None, None, :]
+    states = states[:, :, : RANKS * passage_len].reshape(2, key_rows_n, half)
+
+    residual = target_states.astype(jnp.float32)
+    unit_one, factor_one, normed_one = rms_forward(residual, norm_gains[0])
+    projected = jnp.dot(normed_one, self_in, preferred_element_type=jnp.float32).astype(low)
+    projected = projected.reshape(1, TLEN, 3, heads_here, HEAD_DIM)
+    queries_self = projected[:, :, 0]
+    keys_self = projected[:, :, 1]
+    values_self = projected[:, :, 2]
+    buckets = jnp.asarray(bucket_table(TLEN, bucket_count, MAXDIST))
+    one_hot = (jnp.arange(bucket_count, dtype=jnp.int32)[:, None, None] == buckets[None]).astype(
+        jnp.float32
+    )
+    bias_full = jnp.einsum("bij,bh->hij", one_hot, position_bias, precision=lax.Precision.HIGHEST)[
+        None
+    ]
+    causal = jnp.asarray(np.tril(np.ones((TLEN, TLEN), dtype=bool)))
+    attended_self, total_self = attend(queries_self, keys_self, values_self, causal, bias_full)
+    merged_self = attended_self.reshape(TLEN, w)
+    residual_two = residual + over_pair(rows_nt(merged_self, output_t))
+    unit_two, factor_two, normed_two = rms_forward(residual_two, norm_gains[1])
+    cross_queries = jnp.dot(
+        normed_two, cross_query_full, preferred_element_type=jnp.float32
+    ).astype(low)
+    cross_queries = cross_queries.reshape(1, TLEN, heads_here, HEAD_DIM)
+    key_values = jnp.dot(states[0], kv_weights[:half], preferred_element_type=jnp.float32) + jnp.dot(
+        states[1], kv_weights[half:], preferred_element_type=jnp.float32
+    )
+    key_values = key_values.astype(low).reshape(1, key_rows_n, 2, heads_here, HEAD_DIM)
+    key_rows = key_values[:, :, 0]
+    value_rows = key_values[:, :, 1]
+    head_block = 2
+    head_ranges = [
+        slice(start_head, start_head + head_block)
+        for start_head in range(0, heads_here, head_block)
+    ]
+    cross_parts = []
+    cross_totals = []
+    for head_range in head_ranges:
+        mixed_part, total_part = attend(
+            cross_queries[:, :, head_range],
+            key_rows[:, :, head_range],
+            value_rows[:, :, head_range],
+            allowed,
+            None,
+        )
+        cross_parts.append(mixed_part)
+        cross_totals.append(total_part)
+    merged_cross = jnp.concatenate(cross_parts, axis=2).reshape(TLEN, w)
+    residual_three = residual_two + over_pair(rows_nt(merged_cross, cross_output_t))
+    unit_three, factor_three, normed_three = rms_forward(residual_three, norm_gains[2])
+    before = jnp.dot(normed_three, expand_full, preferred_element_type=jnp.float32)
+    hidden = jax.nn.gelu(before, approximate=True).astype(low)
+    block_out = residual_three + over_pair(rows_nt(hidden, reduce_t))
+    grad_out = output_cotangent.astype(jnp.float32)
+    reduce_grad_t = rows_tn(output_cotangent, hidden)
+    hidden_grad = jnp.dot(output_cotangent, reduce_t, preferred_element_type=jnp.float32)
+    unused_value, gelu_pullback = jax.vjp(partial(jax.nn.gelu, approximate=True), before)
+    before_grad = gelu_pullback(hidden_grad)[0].astype(low)
+    expand_grad = rows_tn(normed_three, before_grad)
+    normed_grad = over_pair(rows_nt(before_grad, expand_full))
+    back_three, gain_three = rms_backward(normed_grad, unit_three, factor_three, norm_gains[2])
+    grad_three = grad_out + back_three
+    grad_low = grad_three.astype(low)
+    cross_output_grad_t = rows_tn(grad_low, merged_cross)
+    mixed_grad = jnp.dot(grad_low, cross_output_t, preferred_element_type=jnp.float32).astype(low)
+    mixed_grad = mixed_grad.reshape(1, TLEN, heads_here, HEAD_DIM)
+    query_parts = []
+    key_parts = []
+    value_parts = []
+    for number, head_range in enumerate(head_ranges):
+        query_part, key_part, value_part, unused_scores = attend_back(
+            cross_queries[:, :, head_range],
+            key_rows[:, :, head_range],
+            value_rows[:, :, head_range],
+            allowed,
+            None,
+            cross_totals[number],
+            mixed_grad[:, :, head_range],
+        )
+        query_parts.append(query_part)
+        key_parts.append(key_part)
+        value_parts.append(value_part)
+    cross_query_rows = jnp.concatenate(query_parts, axis=2).astype(low).reshape(TLEN, w)
+    kv_grad = jnp.stack(
+        [jnp.concatenate(key_parts, axis=2), jnp.concatenate(value_parts, axis=2)], axis=2
+    )
+    kv_grad = kv_grad.astype(low).reshape(key_rows_n, 2 * w)
+    kv_weight_grad = jnp.concatenate([rows_tn(states[0], kv_grad), rows_tn(states[1], kv_grad)])
+    passage_parts = jnp.stack(
+        [rows_nt(kv_grad, kv_weights[:half]), rows_nt(kv_grad, kv_weights[half:])]
+    ).astype(low)
+    passage_parts = passage_parts.reshape(2, CHIPS, RANKS * passage_len, half)
+    cross_query_grad = rows_tn(normed_two, cross_query_rows)
+    normed_grad = over_pair(rows_nt(cross_query_rows, cross_query_full))
+    back_two, gain_two = rms_backward(normed_grad, unit_two, factor_two, norm_gains[1])
+    grad_two = grad_three + back_two
+    grad_low = grad_two.astype(low)
+    self_output_grad_t = rows_tn(grad_low, merged_self)
+    attended_grad = jnp.dot(grad_low, output_t, preferred_element_type=jnp.float32).astype(low)
+    attended_grad = attended_grad.reshape(1, TLEN, heads_here, HEAD_DIM)
+    query_grad, key_grad, value_grad, score_grad = attend_back(
+        queries_self, keys_self, values_self, causal, bias_full, total_self, attended_grad
+    )
+    bias_grad = jnp.einsum(
+        "hij,bij->bh",
+        jnp.sum(score_grad.astype(jnp.float32), axis=0),
+        one_hot,
+        precision=lax.Precision.HIGHEST,
+    )
+    projected_grad = jnp.stack([query_grad, key_grad, value_grad], axis=2).astype(low)
+    projected_grad = projected_grad.reshape(TLEN, 3 * w)
+    self_weight_grad = rows_tn(normed_one, projected_grad)
+    normed_grad = over_pair(rows_nt(projected_grad, self_in))
+    back_one, gain_one = rms_backward(normed_grad, unit_one, factor_one, norm_gains[0])
+    target_grad = (grad_two + back_one).astype(low)
+
+    grads = jnp.stack(
+        [
+            jnp.concatenate([self_weight_grad, self_output_grad_t], axis=1),
+            jnp.concatenate([cross_query_grad, kv_weight_grad, cross_output_grad_t], axis=1),
+            expand_grad,
+            reduce_grad_t,
+        ]
+    ).astype(low)
+    grads = grads.reshape((4, 4, 2, 2) + shards.shape[1:])
+    bias_row = jnp.pad(bias_grad.reshape(-1), (0, norm_gains.shape[1] - bias_grad.size))
+    small = jnp.stack([gain_one, gain_two, gain_three, bias_row])
+    small = jnp.pad(small, ((0, 4), (0, 0)))
+    shard_grads, passage_grad, small_total = scatter_everything(
+        position, grads, passage_parts, small, slots_here
+    )
+    first, second = shard_grads[0], shard_grads[1]
+    return (
+        block_out.astype(low),
+        target_grad,
+        passage_grad,
+        small_total[:3],
+        first[:, :w],
+        first[:, w : 2 * w],
+        first[:, 2 * w : 3 * w],
+        first[:, 3 * w :].T,
+        small_total[3, : bias_grad.size].reshape(bias_grad.shape),
+        second[:, :w],
+        second[:, w : 2 * w],
+        second[:, 2 * w : 3 * w],
+        second[:, 3 * w :].T,
+        shard_grads[2],
+        shard_grads[3].T,
+    )
+
+
 def solution(mesh):
     return jax.shard_map(
-        body,
+        body if fits(mesh) else body_any,
         mesh=mesh,
         in_specs=(
             P("pas", None),

time: 2190 us -> 548 us (0.25)
  the two profiles are of different devices: /device:TPU:0 before, /device:TPU:25 now
where the time goes in v1:
time: 548 us; the launch traced here: 537 us
  Pallas kernels  314 us (57%)
  matrix products  114 us (21%)
  local copies, waits for them, and re-layouts  56.1 us (10%)
  other arithmetic  51.5 us (9%)
    pallas_call x1, Pallas kernels, scatter_everything(): pl.pallas_call(scatter_kernel, out_shape=(jax.ShapeDtypeStruct((groups, r...  158 us
    pallas_call x1, Pallas kernels, gather_everything(): pl.pallas_call(gather_kernel, out_shape=(jax.ShapeDtypeStruct((groups, 4,...  130 us
    pallas_call x6, Pallas kernels, over_pair(): pl.pallas_call(pair_kernel, out_shape=jax.ShapeDtypeStruct(partial_rows.s...  26.6 us
    dot_general x8, matrix products, rows_nt(): lax.dot_general(left, right, (((1,), (1,)), ((), ())), preferred_element_...  25.2 us
    dot_general x4, matrix products, attend_back(): jnp.einsum('sihe,sjhe->shij', out_grad, values, preferred_element_type=jn...  20.1 us
    convert_element_type x2, local copies, waits for them, and re-layouts, body(): kv_grad = kv_grad.astype(low).reshape(key_rows_n, 2 * w)  20 us
    convert_element_type x2, other arithmetic, attend_back(): score_grad = (probability * (prob_grad - centered)).astype(jnp.bfloat16)  18.1 us
    dot_general x8, matrix products, rows_tn(): lax.dot_general(left, right, (((0,), (0,)), ((), ())), preferred_element_...  14.3 us

profile of v1, /device:TPU:25, one launch (start us, length us, event | category | flops | bytes accessed | tf_op | source)
XLA Modules:
  0.0 537.3 jit_solution(11868342846195136233)
XLA Ops:
  7.3 129.7 %shard_map.298 = (bf16[4,4,2,2,48,1536]{5,4,3,2,1,0:T(8,128)(2,1)}, bf16[2,16,208,384]{3,2,1,0:T(8,128)(2,1)}) custom-call(s32[48]{0:T(128)} %get-tuple-element.88.index_ref, bf16[4,48,1536]{2,1,0:T(8,128)(2,1)} %pad_maximum_fusion.5.shard_ref, bf16[40,64,384]{2,1,0:T(8,128)(2,1)} %passage_ref.1, bf16[16,16,384]{2,1,0:T(8,128)(2,1)} %broadcast_in_dim.104.flag_ref), custom_call_target="tpu_custom_call" | custom-call | tf_op jit(solution)/shard_map/pallas_call | solution.py:557
  137.1 5.1 fusion.82
  142.2 2.7 fusion.1
  153.8 4.4 shard_map.299
  159.6 2.9 fusion.83
  162.4 4.2 fusion.48
  166.7 4.4 add_convert_fusion
  171.1 2.6 slice_bitcast_fusion
  175.4 4.8 fusion.44
  184.2 4.2 exponential_reduce_fusion.2
  195.8 2.5 fusion.52.mine_ref
  198.3 4.4 shard_map.300
  209.4 4.4 shard_map.302
  215.2 3.5 fusion.81.mine_ref
  218.7 4.4 shard_map.301
  232.6 5.3 fusion.43
  238.0 11.0 %multiply_reduce_fusion.2 = (f32[2,256]{1,0:T(2,128)S(1)}, f32[2,256]{1,0:T(2,128)S(1)}, f32[2,256]{1,0:T(2,128)S(1)}, f32[2,256,3072]{2,1,0:T(8,128)}) fusion(f32[2,256,3072]{2,1,0:T(8,128)} %copy-done.3, f32[2,256]{1,0:T(2,128)S(1)} %log_add_fusion.3, pred[3072]{0:T(1024)(128)(4,1)S(1)} %gt.17, f32[2,256,3072]{2,1,0:T(8,128)S(1)} %fusion.41, ...), kind=kOutput, calls=%fused_computation.10 | convolution fusion | flops 220199424 | bytes 38616064 | tf_op jit(solution)/shard_map/sihe,sjhe->shij/dot_general | solution.py:74
  248.9 17.7 %multiply_convert_fusion.2 = (bf16[2,256,3072]{2,1,0:T(8,128)(2,1)S(1)}, bf16[2,256,3072]{2,1,0:T(8,128)(2,1)}, bf16[2,256,3072]{2,1,0:T(8,128)(2,1)}) fusion(f32[2,256,3072]{2,1,0:T(8,128)} %get-tuple-element.121, f32[2,256,3072]{2,1,0:T(8,128)} %copy-done.3, f32[2,256]{1,0:T(2,128)S(1)} %get-tuple-element.79, f32[2,256]{1,0:T(2,128)S(1)} %log_add_fusion.3, ...), kind=kLoop, calls=%fused_computation.9 | loop fusion | flops 23592960 | bytes 47201280 | tf_op jit(solution)/shard_map/convert_element_type | solution.py:76
  266.6 4.4 convolution_bitcast_fusion.4
  275.5 2.5 fusion.51.mine_ref
  278.0 4.4 shard_map.303
  291.5 3.4 fusion.21.mine_ref
  294.9 4.6 shard_map.304
  319.5 3.0 convolution_convert_fusion.13
  322.4 3.0 convolution_convert_fusion.14
  332.4 4.2 pad_maximum_fusion.grads_ref
  336.6 11.1 %convert_element_type.271 = bf16[16,192,768]{1,0,2:T(8,128)(2,1)} reshape(bf16[1,3072,2,6,64]{1,4,3,2,0:T(8,128)(2,1)} %copy-done.15) | data formatting | bytes 9437184 | tf_op jit(solution)/shard_map/convert_element_type | solution.py:1012
  347.8 8.9 %copy.89 = bf16[16,192,768]{2,1,0:T(8,128)(2,1)} copy(bf16[16,192,768]{1,0,2:T(8,128)(2,1)} %convert_element_type.271) | data formatting | bytes 9437184 | tf_op jit(solution)/shard_map/convert_element_type | solution.py:1012
  356.6 5.3 convert_bitcast_fusion
  361.9 3.9 convert_bitcast_fusion.1
  365.9 2.6 pad_maximum_fusion.2.passage_ref
  371.6 157.7 %shard_map.305 = (f32[4,48,1536]{2,1,0:T(8,128)}, bf16[40,64,384]{2,1,0:T(8,128)(2,1)}, f32[8,768]{1,0:T(8,128)}) custom-call(s32[40]{0:T(128)} %copy-done.60, bf16[4,4,2,2,48,1536]{5,4,3,2,1,0:T(8,128)(2,1)} %pad_maximum_fusion.grads_ref, bf16[2,16,192,384]{3,2,1,0:T(8,128)(2,1)} %pad_maximum_fusion.2.passage_ref, f32[8,768]{1,0:T(8,128)} %select_maximum_fusion.small_ref), custom_call_target="tpu_custom_call" | custom-call | tf_op jit(solution)/shard_map/pallas_call | solution.py:814
  (244 shorter events, 98.1 us)
Async XLA Ops:
  0.6 141.5 %copy-start = (f32[32,6]{0,1:T(8,128)S(1)}, f32[32,6]{0,1:T(8,128)}, u32[]{:S(2)}) copy-start(f32[32,6]{0,1:T(8,128)} %param.28) | copy-start | bytes 2308
  137.1 5.1 copy-start.56
  142.2 4.3 copy-start.59
  142.2 4.4 copy-start.25
  162.4 4.2 copy-start.16
  183.6 10.9 %copy-start.3 = (f32[2,256,3072]{2,1,0:T(8,128)}, f32[2,256,3072]{2,1,0:T(8,128)S(1)}, u32[]{:S(2)}) copy-start(f32[2,256,3072]{2,1,0:T(8,128)S(1)} %get-tuple-element.119) | copy-start | bytes 18874372
  188.4 4.7 copy-start.4
  195.7 8.5 %copy-start.29 = (bf16[1,4,2,2,48,1536]{5,4,3,2,1,0:T(8,128)(2,1)S(1)}, bf16[1,4,2,2,48,1536]{5,4,3,2,1,0:T(8,128)(2,1)}, u32[]{:S(2)}) copy-start(bf16[1,4,2,2,48,1536]{5,4,3,2,1,0:T(8,128)(2,1)} %get-tuple-element.93) | copy-start | bytes 7077892
  204.2 18.9 %copy-start.13 = (f32[256,768]{1,0:T(8,128)}, f32[256,768]{1,0:T(8,128)S(1)}, u32[]{:S(2)}) copy-start(f32[256,768]{1,0:T(8,128)S(1)} %get-tuple-element.90) | copy-start | bytes 2359300
  207.7 7.6 %copy-start.52 = (bf16[256,1536]{1,0:T(8,128)(2,1)}, bf16[256,1536]{1,0:T(8,128)(2,1)S(1)}, u32[]{:S(2)}) copy-start(bf16[256,1536]{1,0:T(8,128)(2,1)S(1)} %fusion.19) | copy-start | bytes 2359300
  215.2 7.9 %copy-start.31 = (f32[256,768]{1,0:T(8,128)S(1)}, f32[256,768]{1,0:T(8,128)}, u32[]{:S(2)}) copy-start(f32[256,768]{1,0:T(8,128)} %shard_map.302) | copy-start | bytes 2359300
  226.2 11.7 %slice-start = ((s8[6291456]{0:T(1024)(128)(4,1)}), s8[2097152]{0:T(1024)(128)(4,1)S(1)}, s32[]{:S(2)}) async-start(s8[6291456]{0:T(1024)(128)(4,1)} %bitcast.285), calls=%async_computation | async-start | bytes 4194304
  230.3 7.7 %slice-start.1 = ((s8[6291456]{0:T(1024)(128)(4,1)}), s8[4194304]{0:T(1024)(128)(4,1)S(1)}, s32[]{:S(2)}) async-start(s8[6291456]{0:T(1024)(128)(4,1)} %bitcast.285), calls=%async_computation.1 | async-start | bytes 8388608
  232.6 5.4 copy-start.5
  266.6 6.6 %copy-start.8 = (bf16[2,256,3072]{2,1,0:T(8,128)(2,1)}, bf16[2,256,3072]{2,1,0:T(8,128)(2,1)S(1)}, u32[]{:S(2)}) copy-start(bf16[2,256,3072]{2,1,0:T(8,128)(2,1)S(1)} %get-tuple-element.113) | copy-start | bytes 9437188
  266.6 4.4 copy-start.10
  275.4 8.6 %copy-start.23 = (f32[256,768]{1,0:T(8,128)S(1)}, f32[256,768]{1,0:T(8,128)}, u32[]{:S(2)}) copy-start(f32[256,768]{1,0:T(8,128)} %copy-done.22) | copy-start | bytes 2359300
  275.5 9.9 %copy-start.46 = (bf16[1,256,6,64]{1,3,2,0:T(8,128)(2,1)}, bf16[1,256,6,64]{1,3,2,0:T(8,128)(2,1)S(1)}, u32[]{:S(2)}) copy-start(bf16[1,256,6,64]{1,3,2,0:T(8,128)(2,1)S(1)} %maximum_convert_fusion.1) | copy-start | bytes 589828
  282.4 5.5 %copy-start.7 = (f32[6,256,256]{1,2,0:T(8,128)S(1)}, f32[6,256,256]{1,2,0:T(8,128)}, u32[]{:S(2)}) copy-start(f32[6,256,256]{1,2,0:T(8,128)} %copy-done.6) | copy-start | bytes 4718596
  291.5 9.6 %copy-start.38 = (bf16[1,256,3,6,64]{1,4,3,2,0:T(8,128)(2,1)}, bf16[1,256,3,6,64]{1,4,3,2,0:T(8,128)(2,1)S(1)}, u32[]{:S(2)}) copy-start(bf16[1,256,3,6,64]{1,4,3,2,0:T(8,128)(2,1)S(1)} %maximum_convert_fusion) | copy-start | bytes 1769476
  291.5 9.6 %copy-start.21 = (f32[256,768]{1,0:T(8,128)S(1)}, f32[256,768]{1,0:T(8,128)}, u32[]{:S(2)}) copy-start(f32[256,768]{1,0:T(8,128)} %copy-done.20) | copy-start | bytes 2359300
  294.9 8.4 %copy-start.51 = (f32[256,1536]{1,0:T(8,128)S(1)}, f32[256,1536]{1,0:T(8,128)}, u32[]{:S(2)}) copy-start(f32[256,1536]{1,0:T(8,128)} %copy-done.50) | copy-start | bytes 4718596
  294.9 8.4 %copy-start.55 = (bf16[256,768]{1,0:T(8,128)(2,1)S(1)}, bf16[256,768]{1,0:T(8,128)(2,1)}, u32[]{:S(2)}) copy-start(bf16[256,768]{1,0:T(8,128)(2,1)} %param.35) | copy-start | bytes 1179652
  299.5 9.8 %slice-start.2 = ((s8[6291456]{0:T(1024)(128)(4,1)}), s8[4194304]{0:T(1024)(128)(4,1)S(1)}, s32[]{:S(2)}) async-start(s8[6291456]{0:T(1024)(128)(4,1)} %bitcast.287), calls=%async_computation.2 | async-start | bytes 8388608
  303.3 6.0 %slice-start.3 = ((s8[6291456]{0:T(1024)(128)(4,1)}), s8[2097152]{0:T(1024)(128)(4,1)S(1)}, s32[]{:S(2)}) async-start(s8[6291456]{0:T(1024)(128)(4,1)} %bitcast.287), calls=%async_computation.3 | async-start | bytes 4194304
  303.3 7.3 %slice-start.6 = ((s8[6291456]{0:T(1024)(128)(4,1)}), s8[4194304]{0:T(1024)(128)(4,1)S(1)}, s32[]{:S(2)}) async-start(s8[6291456]{0:T(1024)(128)(4,1)} %bitcast.291), calls=%async_computation.6 | async-start | bytes 8388608
  305.7 4.9 slice-start.7
  305.7 6.2 %slice-start.4 = ((s8[6291456]{0:T(1024)(128)(4,1)}), s8[4194304]{0:T(1024)(128)(4,1)S(1)}, s32[]{:S(2)}) async-start(s8[6291456]{0:T(1024)(128)(4,1)} %bitcast.289), calls=%async_computation.4 | async-start | bytes 8388608
  317.7 4.8 copy-start.15
  356.6 5.3 copy-start.35
  529.3 6.6 %copy-start.41 = (bf16[40,64,384]{2,1,0:T(8,128)(2,1)S(1)}, bf16[40,64,384]{2,1,0:T(8,128)(2,1)}, u32[]{:S(2)}) copy-start(bf16[40,64,384]{2,1,0:T(8,128)(2,1)} %get-tuple-element.143) | copy-start | bytes 5898244
  530.8 6.3 %copy-start.1 = (f32[32,6]{0,1:T(8,128)S(1)}, f32[32,6]{0,1:T(8,128)}, u32[]{:S(2)}) copy-start(f32[32,6]{0,1:T(8,128)} %param.28) | copy-start | bytes 2308
  (37 other events, 89.1 us)

commit v2 on v1

--- a/solution.py
+++ b/solution.py
@@ -607,24 +607,128 @@
     )(partial_rows)
 
 
-def scatter_kernel(
+def rows_nt(left, right):
+    return lax.dot_general(
+        left, right, (((1,), (1,)), ((), ())), preferred_element_type=jnp.float32
+    )
+
+
+def rows_tn(left, right):
+    return lax.dot_general(
+        left, right, (((0,), (0,)), ((), ())), preferred_element_type=jnp.float32
+    )
+
+
+TILE = 2
+
+
+def mm(left, right):
+    return jnp.dot(left, right, preferred_element_type=jnp.float32)
+
+
+def halves_of_pair(rows, head):
+    lane = lax.broadcasted_iota(jnp.int32, (rows.shape[0], 2 * HEAD_DIM), 1)
+    at = head // 2 * 2 * HEAD_DIM
+    return jnp.where(lane // HEAD_DIM == head % 2, rows[:, at : at + 2 * HEAD_DIM], 0.0).astype(
+        jnp.bfloat16
+    )
+
+
+def halves_of_rows(rows, head):
+    row = lax.broadcasted_iota(jnp.int32, (2 * HEAD_DIM, rows.shape[1]), 0)
+    at = head // 2 * 2 * HEAD_DIM
+    return jnp.where(row // HEAD_DIM == head % 2, rows[at : at + 2 * HEAD_DIM], 0.0).astype(
+        jnp.bfloat16
+    )
+
+
+def unit_of(values):
+    factor = lax.rsqrt(jnp.mean(values * values, axis=-1, keepdims=True) + EPSILON)
+    return values * factor, factor
+
+
+def prepare_heads(heads, query_ref, grad, mixed, q_pair, o_pair, o_rows, centre):
+    grad = grad.astype(jnp.float32)
+    grad_t = grad.T
+    product = (grad * mixed.astype(jnp.float32)).T
+    queries = query_ref[...].astype(jnp.float32)
+    for h in range(heads):
+        q_pair[h] = halves_of_pair(queries, h)
+        o_pair[h] = halves_of_pair(grad, h)
+        o_rows[h] = halves_of_rows(grad_t, h)
+        centre[h : h + 1, :] = jnp.sum(
+            product[h * HEAD_DIM : (h + 1) * HEAD_DIM], axis=0, keepdims=True
+        )
+
+
+def head_pair_back(p, keys, values, prob, q_pair, o_pair, o_rows, centre, keep_scores):
+    low = jnp.bfloat16
+    keys_t = keys.T
+    query_parts = []
+    for a in range(2):
+        h = 2 * p + a
+        prob_grad = mm(values, o_rows[h])
+        weights = prob(h)
+        score_grad = (weights * (prob_grad - centre[h : h + 1, :])).astype(low)
+        if keep_scores is not None:
+            keep_scores(h, score_grad)
+        key_part = mm(score_grad, q_pair[h])
+        value_part = mm(weights.astype(low), o_pair[h])
+        key_grad = key_part if a == 0 else key_grad + key_part
+        value_grad = value_part if a == 0 else value_grad + value_part
+        query_parts.append(mm(keys_t[a * HEAD_DIM : (a + 1) * HEAD_DIM], score_grad))
+    return key_grad.astype(low), value_grad.astype(low), query_parts
+
+
+def backward_kernel(
     position_ref,
-    grads_ref,
-    passage_ref,
-    small_ref,
+    exps_ref,
+    scale_ref,
+    kv_ref,
+    states_ref,
+    query_ref,
+    mixed_ref,
+    self_w_ref,
+    cross_w_ref,
+    ff_ref,
+    grad_ref,
+    residual_ref,
+    target_ref,
+    gains_ref,
+    qkv_ref,
+    self_mixed_ref,
+    self_exps_ref,
+    self_scale_ref,
+    bucket_ref,
+    gain_ref,
     shard_ref,
     slots_ref,
-    total_ref,
+    small_ref,
+    target_grad_ref,
+    exps,
+    keys,
+    grads,
     far_got,
-    far_sum,
     near_got,
-    near_sum,
     z_got,
+    dkv,
+    outgoing,
+    kept_sum,
     pair_got,
-    pair_sum,
     slot_got,
+    small,
     small_got,
-    small_sum,
+    q_pair,
+    o_pair,
+    o_rows,
+    centre,
+    dq_t,
+    row_sent,
+    row_got,
+    upper_grad,
+    self_scores,
+    exps_sem,
+    keys_sem,
     far_send,
     far_recv,
     near_send,
@@ -637,155 +741,349 @@
     slot_recv,
     small_send,
     small_recv,
+    row_send,
+    row_recv,
 ):
+    low, wide = jnp.bfloat16, jnp.float32
     me, core, x, y, z, near, far = places()
-    groups = grads_ref.shape[0]
+    groups = shard_ref.shape[0]
     across_x, across_y = me + 1 - 2 * x, me + 2 - 4 * y
     kept = (1 - core) * y + core * x
+    partner = (me, 1 - core)
+    width = query_ref.shape[1]
+    pairs = width // (2 * HEAD_DIM)
+    heads = 2 * pairs
+    block_rows = states_ref.shape[1] // CHIPS
+    tile_rows = TILE * block_rows
+    tiles = CHIPS // TILE
+    half = states_ref.shape[2]
+
+    def tile_at(t):
+        return (t + me // TILE) % tiles
+
+    def exps_copy(t):
+        rows = pl.ds(tile_at(t) * tile_rows, tile_rows)
+        return pltpu.make_async_copy(exps_ref.at[:, rows], exps.at[t % 2], exps_sem.at[t % 2])
+
+    def keys_copy(t):
+        rows = pl.ds(tile_at(t) * tile_rows, tile_rows)
+        return pltpu.make_async_copy(kv_ref.at[rows], keys.at[t % 2], keys_sem.at[t % 2])
+
+    exps_copy(0).start()
+    keys_copy(0).start()
     greet_all(me, core)
 
+    def source(g):
+        return ff_ref.at[g - 2] if g >= 2 else grads.at[g]
+
     def far_copy(g, over_x):
-        block = grads_ref.at[g, :, :, 1 - x] if over_x else grads_ref.at[g, :, 1 - y, :]
+        block = source(g).at[:, :, 1 - x] if over_x else source(g).at[:, 1 - y, :]
         return remote(block, far_got.at[g], far_send.at[g], far_recv.at[g], (far, core))
+
+    def far_start(g):
+        @pl.when(core == 0)
+        def _():
+            far_copy(g, True).start()
+
+        @pl.when(core == 1)
+        def _():
+            far_copy(g, False).start()
 
     def near_copy(g):
         return remote(
-            far_sum.at[g, :, 1 - kept], near_got.at[g], near_send.at[g], near_recv.at[g], (near, core)
+            far_got.at[g, :, 1 - kept], near_got.at[g], near_send.at[g], near_recv.at[g], (near, core)
         )
 
     def z_copy(g, k):
         return remote(
-            near_sum.at[g, (z + k) % 4],
+            near_got.at[g, (z + k) % 4],
             z_got.at[g, k - 1],
             z_send.at[g, k - 1],
             z_recv.at[g, k - 1],
             ((me + 4 * k) % CHIPS, core),
         )
 
-    def pair_copy(k):
-        to = (me + k) % CHIPS
+    def far_add(g):
+        far_copy(g, True).wait_recv()
+
+        def step(i, carry):
+            zi, o = i // 2, i % 2
+            mine = source(g)[zi, (1 - core) * o + core * y, (1 - core) * x + core * o]
+            far_got[g, zi, o] = (mine.astype(wide) + far_got[g, zi, o].astype(wide)).astype(low)
+            return carry
+
+        lax.fori_loop(0, 8, step, 0)
+        near_copy(g).start()
+
+    def near_add(g):
+        near_copy(g).wait_recv()
+
+        def step(zi, carry):
+            near_got[g, zi] = (
+                far_got[g, zi, kept].astype(wide) + near_got[g, zi].astype(wide)
+            ).astype(low)
+            return carry
+
+        lax.fori_loop(0, 4, step, 0)
+        for k in range(1, 4):
+            z_copy(g, k).start()
+
+    def z_add(g):
+        for k in range(1, 4):
+            z_copy(g, k).wait_recv()
+        total = near_got[g, z].astype(wide)
+        for k in range(3):
+            total = total + z_got[g, k].astype(wide)
+        shard_ref[g] = total
+
+    def pair_copy(t):
         return remote(
-            passage_ref.at[1 - core, to],
-            pair_got.at[to],
-            pair_send.at[k],
-            pair_recv.at[k],
-            (me, 1 - core),
+            outgoing.at[t % 2],
+            pair_got.at[tile_at(t)],
+            pair_send.at[t % 2],
+            pair_recv.at[t],
+            partner,
         )
 
-    def slot_copy(k):
-        to = (me + k) % CHIPS
+    def slot_copy(to):
         return remote(
-            pair_sum.at[to],
-            slot_got.at[me],
-            slot_send.at[k - 1],
-            slot_recv.at[k - 1],
-            (to, core),
+            kept_sum.at[to], slot_got.at[me], slot_send.at[to], slot_recv.at[me], (to, core)
         )
+
+    def slot_arrival(k):
+        came = (me + k) % CHIPS
+        return remote(
+            kept_sum.at[came], slot_got.at[came], slot_send.at[came], slot_recv.at[came], (came, core)
+        )
+
+    def finish_tile(t):
+        tile = tile_at(t)
+        pair_copy(t).wait_recv()
+        for j in range(TILE):
+            to = tile * TILE + j
+            rows = slice(j * block_rows, (j + 1) * block_rows)
+            kept_sum[to] = (
+                kept_sum[to].astype(wide) + pair_got[tile, rows].astype(wide)
+            ).astype(low)
+
+            @pl.when(to != me)
+            def _():
+                slot_copy(to).start()
+
+            @pl.when(to == me)
+            def _():
+                slot_got[me] = kept_sum[me]
+
+    def row_copy(i):
+        return remote(row_sent.at[i], row_got.at[i], row_send.at[i], row_recv.at[i], partner)
+
+    def store_grad(g, first, value):
+        blocks = value.astype(low).reshape(grads.shape[1:5] + (value.shape[1],))
+        grads[g, :, :, :, :, first : first + value.shape[1]] = blocks
+
+    far_start(2)
+    far_start(3)
+
+    upper_grad[...] = grad_ref[...]
+    grad_low = upper_grad[...].astype(low)
+    store_grad(1, 3 * width, rows_tn(grad_low, mixed_ref[...]))
+    mixed_grad = mm(grad_low, cross_w_ref[:, 3 * width :]).astype(low)
+    prepare_heads(heads, query_ref, mixed_grad, mixed_ref[...], q_pair, o_pair, o_rows, centre)
+    dq_t[...] = jnp.zeros_like(dq_t)
+
+    def tile_step(t, carry):
+        tile = tile_at(t)
+        rows = pl.ds(pl.multiple_of(tile * tile_rows, tile_rows), tile_rows)
+
+        @pl.when(t + 1 < tiles)
+        def _():
+            exps_copy(t + 1).start()
+            keys_copy(t + 1).start()
+
+        exps_copy(t).wait()
+        keys_copy(t).wait()
+
+        def prob(h):
+            return exps[t % 2, h].astype(wide) * scale_ref[tile, h : h + 1, :]
+
+        for p in range(pairs):
+            at = 2 * HEAD_DIM * p
+            key_grad, value_grad, query_parts = head_pair_back(
+                p,
+                keys[t % 2, :, at : at + 2 * HEAD_DIM],
+                keys[t % 2, :, width + at : width + at + 2 * HEAD_DIM],
+                prob,
+                q_pair,
+                o_pair,
+                o_rows,
+                centre,
+                None,
+            )
+            dkv[rows, at : at + 2 * HEAD_DIM] = key_grad
+            dkv[rows, width + at : width + at + 2 * HEAD_DIM] = value_grad
+            for a in range(2):
+                first = at + a * HEAD_DIM
+                dq_t[first : first + HEAD_DIM, :] += query_parts[a]
+        here = dkv[rows, :]
+
+        @pl.when(t >= 2)
+        def _():
+            pair_copy(t - 2).wait_send()
+
+        weights = cross_w_ref[pl.ds((1 - core) * half, half), width : 3 * width]
+        outgoing[t % 2] = rows_nt(here, weights).astype(low)
+        pair_copy(t).start()
+        weights = cross_w_ref[pl.ds(core * half, half), width : 3 * width]
+        mine = rows_nt(here, weights).astype(low)
+        for j in range(TILE):
+            kept_sum[tile * TILE + j] = mine[j * block_rows : (j + 1) * block_rows]
+
+        @pl.when(t >= 1)
+        def _():
+            finish_tile(t - 1)
+
+        @pl.when(t == 5)
+        def _():
+            far_add(2)
+
+        return carry
+
+    lax.fori_loop(0, tiles, tile_step, 0)
+    dq = dq_t[...].T.astype(low)
+    row_sent[0] = rows_nt(dq, cross_w_ref[:, :width])
+    row_copy(0).start()
+    finish_tile(tiles - 1)
+    far_add(3)
+    unit_two, factor_two = unit_of(residual_ref[...])
+    normed_two = (unit_two * gains_ref[1:2, :]).astype(low)
+    store_grad(1, 0, rows_tn(normed_two, dq))
+
+    for n in range(2 * width // 256):
+        columns = slice(n * 256, (n + 1) * 256)
+        parts = [rows_tn(states_ref[i], dkv[:, columns]) for i in range(2)]
+        store_grad(1, width + n * 256, jnp.concatenate(parts))
+    far_start(1)
+    near_add(2)
+
+    row_copy(0).wait_recv()
+    normed_grad = row_sent[0] + row_got[0]
+    back, gain_two = rms_backward(normed_grad, unit_two, factor_two, gains_ref[1:2, :])
+    upper_grad[...] += back
+
+    grad_low = upper_grad[...].astype(low)
+    store_grad(0, 3 * width, rows_tn(grad_low, self_mixed_ref[...]))
+    mixed_grad = mm(grad_low, self_w_ref[:, 3 * width :]).astype(low)
+    prepare_heads(
+        heads,
+        qkv_ref.at[:, :width],
+        mixed_grad,
+        self_mixed_ref[...],
+        q_pair,
+        o_pair,
+        o_rows,
+        centre,
+    )
+
+    def self_prob(h):
+        return self_exps_ref[h].astype(wide) * self_scale_ref[h : h + 1, :]
+
+    def keep_scores(h, score_grad):
+        self_scores[h] = score_grad
+
+    query_rows, key_columns, value_columns = [], [], []
+    for p in range(pairs):
+        at = 2 * HEAD_DIM * p
+        key_grad, value_grad, query_parts = head_pair_back(
+            p,
+            qkv_ref[:, width + at : width + at + 2 * HEAD_DIM],
+            qkv_ref[:, 2 * width + at : 2 * width + at + 2 * HEAD_DIM],
+            self_prob,
+            q_pair,
+            o_pair,
+            o_rows,
+            centre,
+            keep_scores,
+        )
+        key_columns.append(key_grad)
+        value_columns.append(value_grad)
+        query_rows.extend(query_parts)
+    dq = jnp.concatenate(query_rows, axis=0).T.astype(low)
+    dqkv = jnp.concatenate([dq] + key_columns + value_columns, axis=1)
+    row_sent[1] = rows_nt(dqkv, self_w_ref[:, : 3 * width])
+    row_copy(1).start()
+    unit_one, factor_one = unit_of(target_ref[...].astype(wide))
+    normed_one = (unit_one * gains_ref[0:1, :]).astype(low)
+    store_grad(0, 0, rows_tn(normed_one, dqkv))
+    far_start(0)
+    near_add(3)
+
+    length = self_scores.shape[1]
+
+    def diagonal_step(i, total):
+        rows = self_scores[:, pl.ds(pl.multiple_of(16 * i, 16), 16), :].astype(wide)
+        rows = rows.reshape(heads * 16, length)
+        return total + pltpu.roll(rows, (length - 16 * i) % length, 1)
+
+    total = lax.fori_loop(
+        0, length // 16, diagonal_step, jnp.zeros((heads * 16, length), wide)
+    ).reshape(heads, 16, length)
+    small[...] = jnp.zeros_like(small)
+    for h in range(heads):
+        line = total[h, 0:1]
+        for s in range(1, 16):
+            line = line + pltpu.roll(total[h, s : s + 1], length - s, 1)
+        small[8 + h : 9 + h, :length] = line
+    by_bucket = jnp.dot(
+        small[8:16, :length], bucket_ref[...], precision=lax.Precision.HIGHEST,
+        preferred_element_type=wide,
+    )
+    small[8:16, :length] = jnp.zeros((8, length), wide)
+    small[8:16, : bucket_ref.shape[1]] = by_bucket
+
+    row_copy(1).wait_recv()
+    normed_grad = row_sent[1] + row_got[1]
+    back, gain_one = rms_backward(normed_grad, unit_one, factor_one, gains_ref[0:1, :])
+    target_grad_ref[...] = (upper_grad[...] + back).astype(low)
+    small[0:1, :] = gain_one[None, :]
+    small[1:2, :] = gain_two[None, :]
+    small[2:3, :] = gain_ref[...]
 
     def small_copy(step):
         if step == 0:
-            return remote(
-                small_ref, small_got.at[0], small_send.at[0], small_recv.at[0], (across_x, core)
-            )
+            return remote(small, small_got.at[0], small_send.at[0], small_recv.at[0], (across_x, core))
         if step == 1:
             return remote(
-                small_sum.at[0],
-                small_got.at[1],
-                small_send.at[1],
-                small_recv.at[1],
-                (across_y, core),
+                small_got.at[6], small_got.at[1], small_send.at[1], small_recv.at[1], (across_y, core)
             )
         return remote(
-            small_sum.at[1],
+            small_got.at[7],
             small_got.at[2 + z],
             small_send.at[step],
             small_recv.at[step],
             ((me + 4 * (step - 1)) % CHIPS, core),
         )
 
-    for k in range(CHIPS):
-        pair_copy(k).start()
     small_copy(0).start()
-    for g in range(groups):
-
-        @pl.when(core == 0)
-        def _():
-            far_copy(g, True).start()
-
-        @pl.when(core == 1)
-        def _():
-            far_copy(g, False).start()
-
-    for k in list(range(1, CHIPS)) + [0]:
-        to = (me + k) % CHIPS
-        pair_copy(k).wait_recv()
-        pair_sum[to] = (
-            passage_ref[core, to].astype(jnp.float32) + pair_got[to].astype(jnp.float32)
-        ).astype(jnp.bfloat16)
-        if k:
-            slot_copy(k).start()
-    slot_got[me] = pair_sum[me]
+    far_add(1)
     small_copy(0).wait_recv()
-    small_sum[0] = small_ref[...] + small_got[0]
+    small_got[6] = small[...] + small_got[0]
     small_copy(1).start()
-
-    def far_add(g):
-        far_copy(g, True).wait_recv()
-
-        def step(i, carry):
-            zi, o = i // 2, i % 2
-            mine = grads_ref[g, zi, (1 - core) * o + core * y, (1 - core) * x + core * o]
-            far_sum[g, zi, o] = (
-                mine.astype(jnp.float32) + far_got[g, zi, o].astype(jnp.float32)
-            ).astype(jnp.bfloat16)
-            return carry
-
-        lax.fori_loop(0, 8, step, 0)
-        near_copy(g).start()
-
-    def near_add(g):
-        near_copy(g).wait_recv()
-
-        def step(zi, carry):
-            near_sum[g, zi] = (
-                far_sum[g, zi, kept].astype(jnp.float32) + near_got[g, zi].astype(jnp.float32)
-            ).astype(jnp.bfloat16)
-            return carry
-
-        lax.fori_loop(0, 4, step, 0)
-        for k in range(1, 4):
-            z_copy(g, k).start()
-
-    def z_add(g):
-        for k in range(1, 4):
-            z_copy(g, k).wait_recv()
-        total = near_sum[g, z].astype(jnp.float32)
-        for k in range(3):
-            total = total + z_got[g, k].astype(jnp.float32)
-        shard_ref[g] = total
-
-    far_add(0)
+    z_add(2)
+    near_add(1)
     small_copy(1).wait_recv()
-    small_sum[1] = small_sum[0] + small_got[1]
+    small_got[7] = small_got[6] + small_got[1]
     for step in range(2, 5):
         small_copy(step).start()
-    small_got[2 + z] = small_sum[1]
-    far_add(1)
+    small_got[2 + z] = small_got[7]
+    far_add(0)
+    z_add(3)
+    z_add(1)
     near_add(0)
-    far_add(2)
-    near_add(1)
-    z_add(0)
-    far_add(3)
-    near_add(2)
-    z_add(1)
-    near_add(3)
-    z_add(2)
-    z_add(3)
     for step in range(2, 5):
         small_copy(step).wait_recv()
-    total_ref[...] = small_got[2] + small_got[3] + small_got[4] + small_got[5]
+    small_ref[...] = small_got[2] + small_got[3] + small_got[4] + small_got[5]
     for k in range(1, CHIPS):
-        slot_copy(k).wait_recv()
+        slot_arrival(k).wait_recv()
     rows = slots_ref.shape[1]
 
     def pick(slot, carry):
@@ -794,71 +1092,130 @@
         return carry
 
     lax.fori_loop(0, slots_ref.shape[0], pick, 0)
+    z_add(0)
     for g in range(groups):
         far_copy(g, True).wait_send()
         near_copy(g).wait_send()
         for k in range(1, 4):
             z_copy(g, k).wait_send()
-    for k in range(CHIPS):
-        pair_copy(k).wait_send()
+    for t in range(tiles - 2, tiles):
+        pair_copy(t).wait_send()
     for k in range(1, CHIPS):
-        slot_copy(k).wait_send()
+        slot_copy((me + k) % CHIPS).wait_send()
     for step in range(5):
         small_copy(step).wait_send()
-
-
-def scatter_everything(position, grads, passage_parts, small, slots):
-    groups, _, _, _, rows, columns = grads.shape
-    _, _, block_rows, half = passage_parts.shape
-    low = jnp.bfloat16
+    for i in range(2):
+        row_copy(i).wait_send()
+
+
+def run_backward(
+    position,
+    exps,
+    scale,
+    key_values,
+    states,
+    queries,
+    mixed,
+    self_w,
+    cross_w,
+    ff_grads,
+    grad,
+    residual,
+    target,
+    gains,
+    qkv,
+    self_mixed,
+    self_exps,
+    self_scale,
+    buckets,
+    gain_three,
+    slots,
+):
+    low, wide = jnp.bfloat16, jnp.float32
+    groups = 4
+    rows, columns = ff_grads.shape[-2:]
+    heads = exps.shape[0]
+    key_count, half = states.shape[1:]
+    tokens, model = grad.shape
+    block_rows = key_count // CHIPS
+    tile_rows = TILE * block_rows
+    width = queries.shape[1]
+    small_shape = (16, model)
+    vmem = pltpu.VMEM
     return pl.pallas_call(
-        scatter_kernel,
+        backward_kernel,
         out_shape=(
-            jax.ShapeDtypeStruct((groups, rows, columns), jnp.float32),
+            jax.ShapeDtypeStruct((groups, rows, columns), wide),
             jax.ShapeDtypeStruct((slots, block_rows // RANKS, half), low),
-            jax.ShapeDtypeStruct(small.shape, jnp.float32),
+            jax.ShapeDtypeStruct(small_shape, wide),
+            jax.ShapeDtypeStruct((tokens, model), low),
         ),
-        in_specs=[IN_SMEM, IN_VMEM, IN_VMEM, IN_VMEM],
-        out_specs=(IN_VMEM, IN_VMEM, IN_VMEM),
+        in_specs=[IN_SMEM, ANY, IN_VMEM, ANY] + [IN_VMEM] * 16,
+        out_specs=(IN_VMEM,) * 4,
         scratch_shapes=[
-            pltpu.VMEM((groups, 4, 2, rows, columns), low),
-            pltpu.VMEM((groups, 4, 2, rows, columns), low),
-            pltpu.VMEM((groups, 4, rows, columns), low),
-            pltpu.VMEM((groups, 4, rows, columns), low),
-            pltpu.VMEM((groups, 3, rows, columns), low),
-            pltpu.VMEM((CHIPS, block_rows, half), low),
-            pltpu.VMEM((CHIPS, block_rows, half), low),
-            pltpu.VMEM((CHIPS, block_rows, half), low),
-            pltpu.VMEM((6,) + small.shape, jnp.float32),
-            pltpu.VMEM((2,) + small.shape, jnp.float32),
+            vmem((2, heads, tile_rows, tokens), low),
+            vmem((2, tile_rows, 2 * width), low),
+            vmem((2, 4, 2, 2, rows, columns), low),
+            vmem((groups, 4, 2, rows, columns), low),
+            vmem((groups, 4, rows, columns), low),
+            vmem((groups, 3, rows, columns), low),
+            vmem((key_count, 2 * width), low),
+            vmem((2, tile_rows, half), low),
+            vmem((CHIPS, block_rows, half), low),
+            vmem((CHIPS // TILE, tile_rows, half), low),
+            vmem((CHIPS, block_rows, half), low),
+            vmem(small_shape, wide),
+            vmem((8,) + small_shape, wide),
+            vmem((heads, tokens, 2 * HEAD_DIM), low),
+            vmem((heads, tokens, 2 * HEAD_DIM), low),
+            vmem((heads, 2 * HEAD_DIM, tokens), low),
+            vmem((8, tokens), wide),
+            vmem((width, tokens), wide),
+            vmem((2, tokens, model), wide),
+            vmem((2, tokens, model), wide),
+            vmem((tokens, model), wide),
+            vmem((heads, tokens, tokens), low),
+            DMA((2,)),
+            DMA((2,)),
             DMA((groups,)),
             DMA((groups,)),
             DMA((groups,)),
             DMA((groups,)),
             DMA((groups, 3)),
             DMA((groups, 3)),
+            DMA((2,)),
+            DMA((CHIPS // TILE,)),
             DMA((CHIPS,)),
             DMA((CHIPS,)),
-            DMA((CHIPS - 1,)),
-            DMA((CHIPS - 1,)),
             DMA((5,)),
             DMA((5,)),
+            DMA((2,)),
+            DMA((2,)),
         ],
         compiler_params=pltpu.CompilerParams(
-            collective_id=2, has_side_effects=True, vmem_limit_bytes=VMEM_LIMIT
+            collective_id=2, has_side_effects=True, vmem_limit_bytes=62 * 2**20
         ),
-    )(position, grads, passage_parts, small)
-
-
-def rows_nt(left, right):
-    return lax.dot_general(
-        left, right, (((1,), (1,)), ((), ())), preferred_element_type=jnp.float32
-    )
-
-
-def rows_tn(left, right):
-    return lax.dot_general(
-        left, right, (((0,), (0,)), ((), ())), preferred_element_type=jnp.float32
+    )(
+        position,
+        exps,
+        scale,
+        key_values,
+        states,
+        queries,
+        mixed,
+        self_w,
+        cross_w,
+        ff_grads,
+        grad,
+        residual,
+        target,
+        gains,
+        qkv,
+        self_mixed,
+        self_exps,
+        self_scale,
+        buckets,
+        gain_three,
     )
 
 
@@ -953,6 +1310,9 @@
     key_values = key_values.astype(low).reshape(1, key_rows_n, 2, heads_here, HEAD_DIM)
     key_rows = key_values[:, :, 0]
     value_rows = key_values[:, :, 1]
+    scores_t = jnp.einsum(
+        "jhe,ihe->hji", key_rows[0], cross_queries[0], preferred_element_type=jnp.float32
+    )
     head_block = 2
     head_ranges = [
         slice(start_head, start_head + head_block)
@@ -985,74 +1345,44 @@
     normed_grad = over_pair(rows_nt(before_grad, expand_full))
     back_three, gain_three = rms_backward(normed_grad, unit_three, factor_three, norm_gains[2])
     grad_three = grad_out + back_three
-    grad_low = grad_three.astype(low)
-    cross_output_grad_t = rows_tn(grad_low, merged_cross)
-    mixed_grad = jnp.dot(grad_low, cross_output_t, preferred_element_type=jnp.float32).astype(low)
-    mixed_grad = mixed_grad.reshape(1, TLEN, heads_here, HEAD_DIM)
-    query_parts = []
-    key_parts = []
-    value_parts = []
-    for number, head_range in enumerate(head_ranges):
-        query_part, key_part, value_part, unused_scores = attend_back(
-            cross_queries[:, :, head_range],
-            key_rows[:, :, head_range],
-            value_rows[:, :, head_range],
-            allowed,
-            None,
-            cross_totals[number],
-            mixed_grad[:, :, head_range],
-        )
-        query_parts.append(query_part)
-        key_parts.append(key_part)
-        value_parts.append(value_part)
-    cross_query_rows = jnp.concatenate(query_parts, axis=2).astype(low).reshape(TLEN, w)
-    kv_grad = jnp.stack(
-        [jnp.concatenate(key_parts, axis=2), jnp.concatenate(value_parts, axis=2)], axis=2
-    )
-    kv_grad = kv_grad.astype(low).reshape(key_rows_n, 2 * w)
-    kv_weight_grad = jnp.concatenate([rows_tn(states[0], kv_grad), rows_tn(states[1], kv_grad)])
-    passage_parts = jnp.stack(
-        [rows_nt(kv_grad, kv_weights[:half]), rows_nt(kv_grad, kv_weights[half:])]
+    totals_t = jnp.concatenate(cross_totals, axis=1)[0, :, :, 0]
+    live_column = (live_keys[0] > 0)[None, :, None]
+    exps = jnp.where(live_column, jnp.exp(scores_t - totals_t[:, None, :]), 0.0).astype(low)
+    tiles = CHIPS // TILE
+    scale = jnp.ones((tiles, 8, TLEN), jnp.float32)
+    self_scores_t = jnp.einsum(
+        "jhe,ihe->hji", keys_self[0], queries_self[0], preferred_element_type=jnp.float32
+    ) + jnp.swapaxes(bias_full[0], 1, 2)
+    self_exps = jnp.where(
+        causal.T[None], jnp.exp(self_scores_t - total_self[0, :, :, 0][:, None, :]), 0.0
     ).astype(low)
-    passage_parts = passage_parts.reshape(2, CHIPS, RANKS * passage_len, half)
-    cross_query_grad = rows_tn(normed_two, cross_query_rows)
-    normed_grad = over_pair(rows_nt(cross_query_rows, cross_query_full))
-    back_two, gain_two = rms_backward(normed_grad, unit_two, factor_two, norm_gains[1])
-    grad_two = grad_three + back_two
-    grad_low = grad_two.astype(low)
-    self_output_grad_t = rows_tn(grad_low, merged_self)
-    attended_grad = jnp.dot(grad_low, output_t, preferred_element_type=jnp.float32).astype(low)
-    attended_grad = attended_grad.reshape(1, TLEN, heads_here, HEAD_DIM)
-    query_grad, key_grad, value_grad, score_grad = attend_back(
-        queries_self, keys_self, values_self, causal, bias_full, total_self, attended_grad
-    )
-    bias_grad = jnp.einsum(
-        "hij,bij->bh",
-        jnp.sum(score_grad.astype(jnp.float32), axis=0),
-        one_hot,
-        precision=lax.Precision.HIGHEST,
-    )
-    projected_grad = jnp.stack([query_grad, key_grad, value_grad], axis=2).astype(low)
-    projected_grad = projected_grad.reshape(TLEN, 3 * w)
-    self_weight_grad = rows_tn(normed_one, projected_grad)
-    normed_grad = over_pair(rows_nt(projected_grad, self_in))
-    back_one, gain_one = rms_backward(normed_grad, unit_one, factor_one, norm_gains[0])
-    target_grad = (grad_two + back_one).astype(low)
-
-    grads = jnp.stack(
-        [
-            jnp.concatenate([self_weight_grad, self_output_grad_t], axis=1),
-            jnp.concatenate([cross_query_grad, kv_weight_grad, cross_output_grad_t], axis=1),
-            expand_grad,
-            reduce_grad_t,
-        ]
-    ).astype(low)
-    grads = grads.reshape((4, 4, 2, 2) + shards.shape[1:])
-    bias_row = jnp.pad(bias_grad.reshape(-1), (0, norm_gains.shape[1] - bias_grad.size))
-    small = jnp.stack([gain_one, gain_two, gain_three, bias_row])
-    small = jnp.pad(small, ((0, 4), (0, 0)))
-    shard_grads, passage_grad, small_total = scatter_everything(
-        position, grads, passage_parts, small, slots_here
+    self_scale = jnp.ones((8, TLEN), jnp.float32)
+    ff_grads = jnp.stack([expand_grad, reduce_grad_t]).astype(low)
+    ff_grads = ff_grads.reshape((2, 4, 2, 2) + shards.shape[1:])
+    distance = np.zeros((TLEN, 128), np.float32)
+    distance[np.arange(TLEN), bucket_table(TLEN, bucket_count, MAXDIST)[:, 0]] = 1.0
+    shard_grads, passage_grad, small_total, target_grad = run_backward(
+        position,
+        exps,
+        scale,
+        key_values.reshape(key_rows_n, 2 * w),
+        states,
+        cross_queries.reshape(TLEN, w),
+        merged_cross,
+        full[0],
+        full[1],
+        ff_grads,
+        grad_three,
+        residual_two,
+        target_states,
+        norm_gains,
+        projected.reshape(TLEN, 3 * w),
+        merged_self,
+        self_exps,
+        self_scale,
+        jnp.asarray(distance),
+        gain_three[None, :],
+        slots_here,
     )
     first, second = shard_grads[0], shard_grads[1]
     return (
@@ -1064,7 +1394,7 @@
         first[:, w : 2 * w],
         first[:, 2 * w : 3 * w],
         first[:, 3 * w :].T,
-        small_total[3, : bias_grad.size].reshape(bias_grad.shape),
+        small_total[8 : 8 + heads_here, :bucket_count].T,
         second[:, :w],
         second[:, w : 2 * w],
         second[:, 2 * w : 3 * w],

time: 548 us -> 406 us (0.74)
  the two profiles are of different devices: /device:TPU:25 before, /device:TPU:0 now
where the time goes in v2:
time: 406 us; the launch traced here: 401 us
  Pallas kernels  294 us (72%)
  matrix products  49 us (12%)
  local copies, waits for them, and re-layouts  36.4 us (9%)
  other arithmetic  19.9 us (5%)
    pallas_call x1, Pallas kernels, gather_everything(): pl.pallas_call(gather_kernel, out_shape=(jax.ShapeDtypeStruct((groups, 4,...  139 us
    pallas_call x1, Pallas kernels, run_backward(): pl.pallas_call(backward_kernel, out_shape=(jax.ShapeDtypeStruct((groups,...  138 us
    pallas_call x4, Pallas kernels, over_pair(): pl.pallas_call(pair_kernel, out_shape=jax.ShapeDtypeStruct(partial_rows.s...  17.7 us
    dot_general x1, matrix products, body(): jnp.einsum('jhe,ihe->hji', key_rows[0], cross_queries[0], preferred_eleme...  8.53 us
    dot_general x4, matrix products, rows_nt(): lax.dot_general(left, right, (((1,), (1,)), ((), ())), preferred_element_...  8.42 us

profile of v2, /device:TPU:0, one launch (start us, length us, event | category | flops | bytes accessed | tf_op | source)
XLA Modules:
  0.0 400.7 jit_solution(18102969485241865208)
XLA Ops:
  9.2 1.9 pad_maximum_fusion.1.shard_ref
  11.1 4.0 fusion
  15.0 2.3 copy.65
  17.4 138.8 %shard_map.307 = (bf16[4,4,2,2,48,1536]{5,4,3,2,1,0:T(8,128)(2,1)}, bf16[2,16,208,384]{3,2,1,0:T(8,128)(2,1)}) custom-call(s32[48]{0:T(128)} %get-tuple-element.38.index_ref, bf16[4,48,1536]{2,1,0:T(8,128)(2,1)} %pad_maximum_fusion.1.shard_ref, bf16[40,64,384]{2,1,0:T(8,128)(2,1)} %passage_ref.1, bf16[16,16,384]{2,1,0:T(8,128)(2,1)} %broadcast_in_dim.119.flag_ref), custom_call_target="tpu_custom_call" | custom-call | tf_op jit(solution)/shard_map/pallas_call | solution.py:557
  157.2 2.2 convolution_convert_fusion.2.qkv_ref
  160.9 1.5 fusion.20.self_exps_ref
  163.2 2.4 fusion.37.mine_ref
  165.5 4.4 %shard_map.308 = f32[256,768]{1,0:T(8,128)} custom-call(f32[256,768]{1,0:T(8,128)} %fusion.37.mine_ref), custom_call_target="tpu_custom_call" | custom-call | tf_op jit(solution)/shard_map/pallas_call | solution.py:598
  171.3 1.8 convolution_convert_fusion.3.query_ref
  173.2 5.2 %slice.183 = bf16[2,16,192,384]{3,2,1,0:T(8,128)(2,1)} slice(bf16[2,16,208,384]{3,2,1,0:T(8,128)(2,1)} %get-tuple-element.22), slice={[0:2], [0:16], [0:192], [0:384]} | slice | bytes 9437184 | tf_op jit(solution)/shard_map/slice | solution.py:1282
  178.9 3.7 fusion.36
  182.6 5.4 %add_convert_fusion.kv_ref = bf16[3072,768]{1,0:T(8,128)(2,1)} fusion(f32[3072,768]{1,0:T(8,128)S(1)} %fusion.36, bf16[3072,384]{1,0:T(8,128)(2,1)S(1)} %bitcast.174, bf16[4,768,1536]{2,1,0:T(8,128)(2,1)} %bitcast.184), kind=kOutput, calls=%fused_computation.1 | convolution fusion | flops 1816657920 | bytes 17104896 | tf_op jit(solution)/shard_map/dot_general | solution.py:1307
  188.0 6.8 %copy.69 = bf16[3072,768]{0,1:T(8,128)(2,1)} copy(bf16[3072,768]{1,0:T(8,128)(2,1)} %add_convert_fusion.kv_ref) | data formatting | bytes 9437184 | tf_op jit(solution)/shard_map/convert_element_type | solution.py:1310
  194.8 2.8 slice_bitcast_fusion
  199.8 2.7 exponential_reduce_fusion.2
  203.8 2.5 exponential_reduce_fusion.1
  209.7 2.4 fusion.35.mine_ref
  212.0 4.4 %shard_map.309 = f32[256,768]{1,0:T(8,128)} custom-call(f32[256,768]{1,0:T(8,128)} %fusion.35.mine_ref), custom_call_target="tpu_custom_call" | custom-call | tf_op jit(solution)/shard_map/pallas_call | solution.py:598
  216.5 1.5 multiply_reduce_fusion.2
  218.0 8.5 %select_convert_fusion.exps_ref = bf16[6,3072,256]{2,1,0:T(8,128)(2,1)} fusion(f32[6,256]{1,0:T(8,128)S(1)} %maximum_bitcast_fusion.2, pred[3072]{0:T(1024)(128)(4,1)S(1)} %gt.23, bf16[256,6,64]{0,2,1:T(8,128)(2,1)S(1)} %bitcast.207, bf16[1,3072,2,6,64]{1,4,3,2,0:T(8,128)(2,1)} %bitcast.176), kind=kOutput, calls=%fused_computation | convolution fusion | flops 618135552 | bytes 12002304 | tf_op jit(solution)/shard_map/jhe,ihe->hji/dot_general | solution.py:1313
  226.5 2.6 fusion.50
  230.1 1.4 fusion.16
  231.5 2.0 fusion.49.mine_ref
  233.5 1.7 fusion.53.mine_ref
  235.2 4.4 %shard_map.311 = f32[256,768]{1,0:T(8,128)} custom-call(f32[256,768]{1,0:T(8,128)} %fusion.53.mine_ref), custom_call_target="tpu_custom_call" | custom-call | tf_op jit(solution)/shard_map/pallas_call | solution.py:598
  239.6 4.5 %shard_map.310 = f32[256,768]{1,0:T(8,128)} custom-call(f32[256,768]{1,0:T(8,128)} %fusion.49.mine_ref), custom_call_target="tpu_custom_call" | custom-call | tf_op jit(solution)/shard_map/pallas_call | solution.py:598
  244.1 1.5 multiply_reduce_fusion
  246.2 2.5 multiply_add_fusion
  250.5 2.6 pad_maximum_fusion.ff_ref
  254.4 137.7 %shard_map.312 = (f32[4,48,1536]{2,1,0:T(8,128)}, bf16[40,64,384]{2,1,0:T(8,128)(2,1)}, f32[16,768]{1,0:T(8,128)}, bf16[256,768]{1,0:T(8,128)(2,1)}) custom-call(s32[40]{0:T(128)} %copy-done.11, bf16[6,3072,256]{2,1,0:T(8,128)(2,1)} %select_convert_fusion.exps_ref, f32[8,8,256]{2,1,0:T(8,128)} %broadcast_in_dim.126.scale_ref, ...), custom_call_target="tpu_custom_call" | custom-call | tf_op jit(solution)/shard_map/pallas_call | solution.py:1145
  392.1 1.4 slice_bitcast_fusion.46
  394.9 2.1 slice_bitcast_fusion.26
  (88 shorter events, 30.0 us)
Async XLA Ops:
  0.6 10.4 %copy-start = (f32[32,6]{0,1:T(8,128)S(1)}, f32[32,6]{0,1:T(8,128)}, u32[]{:S(2)}) copy-start(f32[32,6]{0,1:T(8,128)} %param.29) | copy-start | bytes 2308
  0.7 10.4 %copy-start.10 = (s32[256,256]{1,0:T(8,128)S(1)}, s32[256,256]{1,0:T(8,128)}, u32[]{:S(2)}) copy-start(s32[256,256]{1,0:T(8,128)} %constant.48.clone) | copy-start | bytes 786436
  2.3 12.8 %copy-start.11 = (s32[40]{0:T(128)}, s32[40]{0:T(128)S(1)}, u32[]{:S(2)}) copy-start(s32[40]{0:T(128)S(1)} %multiply_add_fusion.1.position_ref) | copy-start | bytes 484
  15.0 142.1 %copy-start.4 = (bf16[256,768]{1,0:T(8,128)(2,1)S(1)}, bf16[256,768]{1,0:T(8,128)(2,1)}, u32[]{:S(2)}) copy-start(bf16[256,768]{1,0:T(8,128)(2,1)} %target_ref.1) | copy-start | bytes 1179652
  159.4 0.8 copy-start.5
  171.2 45.2 %copy-start.2 = (f32[256,768]{1,0:T(8,128)}, f32[256,768]{1,0:T(8,128)S(1)}, u32[]{:S(2)}) copy-start(f32[256,768]{1,0:T(8,128)S(1)} %get-tuple-element.42.residual_ref) | copy-start | bytes 2359300
  173.0 5.3 %copy-start.7 = (bf16[256,384]{1,0:T(8,128)(2,1)}, bf16[256,384]{1,0:T(8,128)(2,1)S(1)}, u32[]{:S(2)}) copy-start(bf16[256,384]{1,0:T(8,128)(2,1)S(1)} %convolution_convert_fusion.3.query_ref) | copy-start | bytes 589828
  173.2 5.2 %slice-start = ((s8[5111808]{0:T(1024)(128)(4,1)}), s8[4194304]{0:T(1024)(128)(4,1)S(1)}, s32[]{:S(2)}) async-start(s8[5111808]{0:T(1024)(128)(4,1)} %bitcast.178), calls=%async_computation | async-start | bytes 8388608
  173.2 5.2 %slice-start.1 = ((s8[5111808]{0:T(1024)(128)(4,1)}), s8[917504]{0:T(1024)(128)(4,1)S(1)}, s32[]{:S(2)}) async-start(s8[5111808]{0:T(1024)(128)(4,1)} %bitcast.178), calls=%async_computation.1 | async-start | bytes 1835008
  216.4 10.1 %slice-start.2 = ((s8[9437184]{0:T(1024)(128)(4,1)}), s8[4194304]{0:T(1024)(128)(4,1)S(1)}, s32[]{:S(2)}) async-start(s8[9437184]{0:T(1024)(128)(4,1)} %bitcast.186), calls=%async_computation.2 | async-start | bytes 8388608
  218.0 8.6 %slice-start.3 = ((s8[9437184]{0:T(1024)(128)(4,1)}), s8[4194304]{0:T(1024)(128)(4,1)S(1)}, s32[]{:S(2)}) async-start(s8[9437184]{0:T(1024)(128)(4,1)} %bitcast.186), calls=%async_computation.3 | async-start | bytes 8388608
  218.0 8.6 %slice-start.4 = ((s8[9437184]{0:T(1024)(128)(4,1)}), s8[1048576]{0:T(1024)(128)(4,1)S(1)}, s32[]{:S(2)}) async-start(s8[9437184]{0:T(1024)(128)(4,1)} %bitcast.186), calls=%async_computation.4 | async-start | bytes 2097152
  229.1 1.0 copy-start.8
  239.6 6.6 %copy-start.3 = (f32[256,768]{1,0:T(8,128)S(1)}, f32[256,768]{1,0:T(8,128)}, u32[]{:S(2)}) copy-start(f32[256,768]{1,0:T(8,128)} %shard_map.311) | copy-start | bytes 2359300
  392.1 6.3 %copy-start.9 = (bf16[256,768]{1,0:T(8,128)(2,1)S(1)}, bf16[256,768]{1,0:T(8,128)(2,1)}, u32[]{:S(2)}) copy-start(bf16[256,768]{1,0:T(8,128)(2,1)} %get-tuple-element.88) | copy-start | bytes 1179652
  392.1 7.1 %copy-start.6 = (bf16[40,64,384]{2,1,0:T(8,128)(2,1)S(1)}, bf16[40,64,384]{2,1,0:T(8,128)(2,1)}, u32[]{:S(2)}) copy-start(bf16[40,64,384]{2,1,0:T(8,128)(2,1)} %get-tuple-element.89) | copy-start | bytes 5898244
  398.4 2.0 copy-start.1

commit v3 on v2

--- a/solution.py
+++ b/solution.py
@@ -422,189 +422,10 @@
     pl.semaphore_wait(barrier, CHIPS)
 
 
-def gather_kernel(
-    index_ref,
-    shard_ref,
-    passage_ref,
-    flag_ref,
-    full_ref,
-    states_ref,
-    outgoing,
-    own_sem,
-    z_send,
-    z_recv,
-    near_send,
-    near_recv,
-    far_send,
-    far_recv,
-    slot_send,
-    slot_recv,
-    core_send,
-    core_recv,
-    slot_own,
-):
-    me, core, x, y, z, near, far = places()
-    groups = shard_ref.shape[0]
-    greet_all(me, core)
-
-    def z_copy(g, k):
-        return remote(
-            shard_ref.at[g],
-            full_ref.at[g, z, y, x],
-            z_send.at[g, k - 1],
-            z_recv.at[g, k - 1],
-            ((me + 4 * k) % CHIPS, core),
-        )
-
-    def near_copy(g):
-        block = full_ref.at[g, :, y, x]
-        return remote(block, block, near_send.at[g], near_recv.at[g], (near, core))
-
-    def far_copy(g, across_x):
-        block = full_ref.at[g, :, :, x] if across_x else full_ref.at[g, :, y, :]
-        return remote(block, block, far_send.at[g], far_recv.at[g], (far, core))
-
-    def own_copy(g):
-        return pltpu.make_async_copy(shard_ref.at[g], full_ref.at[g, z, y, x], own_sem.at[g])
-
-    def slot_copy(k):
-        to = (me + k) % CHIPS
-        return remote(
-            outgoing.at[to],
-            states_ref.at[core, me],
-            slot_send.at[k - 1],
-            slot_recv.at[k - 1],
-            (to, core),
-        )
-
-    def core_copy(k):
-        block = states_ref.at[core, (me + CHIPS - k) % CHIPS]
-        return remote(block, block, core_send.at[k], core_recv.at[k], (me, 1 - core))
-
-    for g in range(groups):
-        own_copy(g).start()
-        for k in range(1, 4):
-            z_copy(g, k).start()
-
-    def fill(to, carry):
-        for rank in range(RANKS):
-            rows = passage_ref.shape[1]
-            outgoing[to, rank * rows : (rank + 1) * rows, :] = passage_ref[
-                index_ref[to * RANKS + rank]
-            ]
-        outgoing[to, RANKS * passage_ref.shape[1] :, :] = flag_ref[to]
-        return carry
-
-    lax.fori_loop(0, CHIPS, fill, 0)
-    for k in range(1, CHIPS):
-        slot_copy(k).start()
-    mine = pltpu.make_async_copy(outgoing.at[me], states_ref.at[core, me], slot_own)
-    mine.start()
-
-    def second(g):
-        own_copy(g).wait()
-        for k in range(1, 4):
-            z_copy(g, k).wait_recv()
-        near_copy(g).start()
-
-    def third(g):
-        near_copy(g).wait_recv()
-
-        @pl.when(core == 0)
-        def _():
-            far_copy(g, True).start()
-
-        @pl.when(core == 1)
-        def _():
-            far_copy(g, False).start()
-
-    second(0)
-    second(1)
-    third(0)
-    second(2)
-    third(1)
-    second(3)
-    third(2)
-    third(3)
-    mine.wait()
-    core_copy(0).start()
-    for k in range(1, CHIPS):
-        slot_copy(k).wait_recv()
-        core_copy(k).start()
-    for g in range(groups):
-        far_copy(g, True).wait_recv()
-    for k in range(CHIPS):
-        core_copy(k).wait()
-    for k in range(1, CHIPS):
-        slot_copy(k).wait_send()
-    for g in range(groups):
-        for k in range(1, 4):
-            z_copy(g, k).wait_send()
-        near_copy(g).wait_send()
-        far_copy(g, True).wait_send()
-
-
 ANY = pl.BlockSpec(memory_space=pl.ANY)
 IN_VMEM = pl.BlockSpec(memory_space=pltpu.VMEM)
 IN_SMEM = pl.BlockSpec(memory_space=pltpu.SMEM)
 DMA = pltpu.SemaphoreType.DMA
-
-
-def gather_everything(index, shards, passages, flags):
-    groups, rows, columns = shards.shape
-    passage_len, half = passages.shape[1:]
-    block_rows = RANKS * passage_len + FLAG_ROWS
-    return pl.pallas_call(
-        gather_kernel,
-        out_shape=(
-            jax.ShapeDtypeStruct((groups, 4, 2, 2, rows, columns), jnp.bfloat16),
-            jax.ShapeDtypeStruct((2, CHIPS, block_rows, half), jnp.bfloat16),
-        ),
-        in_specs=[IN_SMEM, ANY, IN_VMEM, IN_VMEM],
-        out_specs=(ANY, ANY),
-        scratch_shapes=[
-            pltpu.VMEM((CHIPS, block_rows, half), jnp.bfloat16),
-            DMA((groups,)),
-            DMA((groups, 3)),
-            DMA((groups, 3)),
-            DMA((groups,)),
-            DMA((groups,)),
-            DMA((groups,)),
-            DMA((groups,)),
-            DMA((CHIPS - 1,)),
-            DMA((CHIPS - 1,)),
-            DMA((CHIPS,)),
-            DMA((CHIPS,)),
-            DMA,
-        ],
-        compiler_params=pltpu.CompilerParams(
-            collective_id=0, has_side_effects=True, vmem_limit_bytes=VMEM_LIMIT
-        ),
-    )(index, shards, passages, flags)
-
-
-def pair_kernel(mine_ref, sum_ref, other, send_sem, recv_sem):
-    partner = (lax.axis_index("pas"), 1 - lax.axis_index("mdl"))
-    barrier = pltpu.get_barrier_semaphore()
-    pl.semaphore_signal(barrier, inc=1, device_id=partner, device_id_type=MESH_ID)
-    pl.semaphore_wait(barrier, 1)
-    copy = remote(mine_ref, other, send_sem, recv_sem, partner)
-    copy.start()
-    copy.wait()
-    sum_ref[...] = mine_ref[...] + other[...]
-
-
-def over_pair(partial_rows):
-    return pl.pallas_call(
-        pair_kernel,
-        out_shape=jax.ShapeDtypeStruct(partial_rows.shape, partial_rows.dtype),
-        in_specs=[IN_VMEM],
-        out_specs=IN_VMEM,
-        scratch_shapes=[pltpu.VMEM(partial_rows.shape, partial_rows.dtype), DMA, DMA],
-        compiler_params=pltpu.CompilerParams(
-            collective_id=1, has_side_effects=True, vmem_limit_bytes=VMEM_LIMIT
-        ),
-    )(partial_rows)
 
 
 def rows_nt(left, right):
@@ -1219,6 +1040,494 @@
     )
 
 
+def exp_rows(scores):
+    highest = jnp.max(scores, axis=0, keepdims=True)
+    exps = jnp.exp(scores - highest)
+    return exps, highest, jnp.sum(exps, axis=0, keepdims=True)
+
+
+def gelu_both(values):
+    first = math.sqrt(2 / math.pi)
+    square = values * values
+    curve = jnp.tanh(first * values * (1.0 + 0.044715 * square))
+    half = 0.5 * (1.0 + curve)
+    slope = half + 0.5 * values * (1.0 - curve * curve) * first * (1.0 + 3 * 0.044715 * square)
+    return values * half, slope
+
+
+def forward_kernel(
+    index_ref,
+    shard_ref,
+    passage_ref,
+    flag_ref,
+    target_ref,
+    cotangent_ref,
+    gains_ref,
+    table_ref,
+    bucket_ref,
+    weights_ref,
+    states_out,
+    exps_out,
+    kv_out,
+    scale_ref,
+    query_ref,
+    mixed_ref,
+    residual_ref,
+    qkv_ref,
+    self_mixed_ref,
+    self_exps_ref,
+    self_scale_ref,
+    ff_ref,
+    grad_ref,
+    gain_ref,
+    block_ref,
+    full,
+    states,
+    flags,
+    outgoing,
+    exps,
+    keys,
+    bias,
+    q_rows,
+    out_t,
+    highest,
+    total,
+    tile_highest,
+    row_sent,
+    row_got,
+    z_send,
+    z_recv,
+    near_send,
+    near_recv,
+    first_send,
+    first_recv,
+    second_send,
+    second_recv,
+    slot_send,
+    slot_recv,
+    flag_send,
+    flag_recv,
+    core_send,
+    core_recv,
+    row_send,
+    row_recv,
+    own_sem,
+    exps_sem,
+    keys_sem,
+    out_sem,
+):
+    low, wide = jnp.bfloat16, jnp.float32
+    me, core, x, y, z, near, far = places()
+    groups = shard_ref.shape[0]
+    partner = (me, 1 - core)
+    pair = me // TILE
+    tiles = CHIPS // TILE
+    block_rows = states.shape[2]
+    passage_len = block_rows // RANKS
+    tile_rows = TILE * block_rows
+    tokens = target_ref.shape[0]
+    width = query_ref.shape[1]
+    pairs = width // (2 * HEAD_DIM)
+    heads = 2 * pairs
+    half = states.shape[3]
+    other_y = y + (1 - core) * (1 - 2 * y)
+    other_x = x + core * (1 - 2 * x)
+
+    def own_copy(g):
+        return pltpu.make_async_copy(shard_ref.at[g], full.at[g, z, y, x], own_sem.at[g])
+
+    def z_copy(g, k):
+        return remote(
+            shard_ref.at[g],
+            full.at[g, z, y, x],
+            z_send.at[g, k - 1],
+            z_recv.at[g, k - 1],
+            ((me + 4 * k) % CHIPS, core),
+        )
+
+    def held(g, k):
+        return shard_ref.at[g] if k == 0 else full.at[g, (z + k) % 4, y, x]
+
+    def near_copy(g, k):
+        dst = full.at[g, (z + k) % 4, y, x]
+        return remote(held(g, k), dst, near_send.at[g, k], near_recv.at[g, k], (near, core))
+
+    def first_copy(g, k):
+        dst = full.at[g, (z + k) % 4, y, x]
+        return remote(held(g, k), dst, first_send.at[g, k], first_recv.at[g, k], (far, core))
+
+    def second_copy(g, k):
+        block = full.at[g, (z + k) % 4, other_y, other_x]
+        return remote(block, block, second_send.at[g, k], second_recv.at[g, k], (far, core))
+
+    def slot_copy(to):
+        return remote(
+            outgoing.at[to], states.at[core, me], slot_send.at[to], slot_recv.at[me], (to, core)
+        )
+
+    def slot_arrival(came):
+        block = states.at[core, came]
+        return remote(block, block, slot_send.at[came], slot_recv.at[came], (came, core))
+
+    def flag_copy(to):
+        return remote(flag_ref.at[to], flags.at[me], flag_send.at[to], flag_recv.at[me], (to, core))
+
+    def flag_arrival(came):
+        block = flags.at[came]
+        return remote(block, block, flag_send.at[came], flag_recv.at[came], (came, core))
+
+    def core_copy(came):
+        block = states.at[core, came]
+        return remote(block, block, core_send.at[came], core_recv.at[came], partner)
+
+    def row_copy(i):
+        return remote(row_sent.at[i], row_got.at[i], row_send.at[i], row_recv.at[i], partner)
+
+    def pair_sum(i):
+        row_copy(i).wait_recv()
+        return row_sent[i] + row_got[i]
+
+    def launch(g):
+        for k in range(1, 4):
+            z_copy(g, k).start()
+        near_copy(g, 0).start()
+        first_copy(g, 0).start()
+        own_copy(g).start()
+
+    def relay(g):
+        for k in range(1, 4):
+            z_copy(g, 4 - k).wait_recv()
+            near_copy(g, k).start()
+            first_copy(g, k).start()
+
+    def relay_near(g):
+        for k in range(4):
+            near_copy(g, k).wait_recv()
+            second_copy(g, k).start()
+
+    def arrived(g):
+        own_copy(g).wait()
+        for k in range(4):
+            first_copy(g, k).wait_recv()
+            second_copy(g, k).wait_recv()
+
+    def weight(g):
+        return full[g].reshape(full.shape[1] * 4 * full.shape[4], full.shape[5])
+
+    def weights_copy(g):
+        return pltpu.make_async_copy(full.at[g], weights_ref.at[g], out_sem.at[g])
+
+    greet_all(me, core)
+    launch(0)
+    launch(1)
+
+    def fill(to, carry):
+        for rank in range(RANKS):
+            outgoing[to, rank * passage_len : (rank + 1) * passage_len, :] = passage_ref[
+                index_ref[to * RANKS + rank]
+            ]
+        return carry
+
+    lax.fori_loop(0, CHIPS, fill, 0)
+    mate = me + 1 - 2 * x
+    flag_copy(mate).start()
+    slot_copy(mate).start()
+
+    def send_pair(j, carry):
+        for i in range(TILE):
+            to = (pair + j) % tiles * TILE + i
+            flag_copy(to).start()
+            slot_copy(to).start()
+        return carry
+
+    lax.fori_loop(1, tiles, send_pair, 0)
+    states[core, me] = outgoing[me]
+    flags[me] = flag_ref[me]
+    core_copy(me).start()
+
+    line = jnp.dot(
+        table_ref[...], bucket_ref[...], precision=lax.Precision.HIGHEST, preferred_element_type=wide
+    )
+    for h in range(heads):
+        for s in range(8):
+            row = line[h : h + 1]
+            bias[h, s : s + 1, :] = row if s == 0 else pltpu.roll(row, s, 1)
+    base = bias[:, 0:8, :].reshape(heads * 8, tokens)
+
+    def bias_step(i, carry):
+        rows = pltpu.roll(base, 8 * i, 1).reshape(heads, 8, tokens)
+        bias[:, pl.ds(pl.multiple_of(8 * i, 8), 8), :] = rows
+        return carry
+
+    lax.fori_loop(1, tokens // 8, bias_step, 0)
+    residual = target_ref[...].astype(wide)
+    normed = (unit_of(residual)[0] * gains_ref[0:1, :]).astype(low)
+
+    relay(0)
+    relay_near(0)
+    relay(1)
+    arrived(0)
+
+    qkv_ref[...] = mm(normed, weight(0)[:, : 3 * width]).astype(low)
+    weights_copy(0).start()
+    relay_near(1)
+    launch(2)
+    launch(3)
+    queries_t = qkv_ref[:, :width].astype(wide).T
+    for h in range(heads):
+        q_rows[h] = halves_of_rows(queries_t, h)
+    key_at = lax.broadcasted_iota(jnp.int32, (tokens, tokens), 0)
+    query_at = lax.broadcasted_iota(jnp.int32, (tokens, tokens), 1)
+    self_scale_ref[...] = jnp.zeros_like(self_scale_ref)
+    for p in range(pairs):
+        at = 2 * HEAD_DIM * p
+        head_keys = qkv_ref[:, width + at : width + at + 2 * HEAD_DIM]
+        values_t = qkv_ref[:, 2 * width + at : 2 * width + at + 2 * HEAD_DIM].T
+        for a in range(2):
+            h = 2 * p + a
+            scores = mm(head_keys, q_rows[h]) + bias[h]
+            scores = jnp.where(key_at <= query_at, scores, MASKED)
+            head_exps, unused, sums = exp_rows(scores)
+            head_exps = head_exps.astype(low)
+            self_exps_ref[h] = head_exps
+            inverse = 1.0 / sums
+            self_scale_ref[h : h + 1, :] = inverse
+            first = at + a * HEAD_DIM
+            out_t[first : first + HEAD_DIM, :] = (
+                mm(values_t[a * HEAD_DIM : (a + 1) * HEAD_DIM], head_exps) * inverse
+            )
+    self_mixed_ref[...] = out_t[...].T.astype(low)
+    row_sent[0] = rows_nt(self_mixed_ref[...], weight(0)[:, 3 * width :])
+    row_copy(0).start()
+    relay(2)
+    arrived(1)
+    weights_copy(1).start()
+    residual_ref[...] = residual + pair_sum(0)
+
+    normed = (unit_of(residual_ref[...])[0] * gains_ref[1:2, :]).astype(low)
+    query_ref[...] = mm(normed, weight(1)[:, :width]).astype(low)
+    queries_t = query_ref[...].astype(wide).T
+    for h in range(heads):
+        q_rows[h] = halves_of_rows(queries_t, h)
+    out_t[...] = jnp.zeros_like(out_t)
+    highest[...] = jnp.full_like(highest, MASKED)
+    total[...] = jnp.zeros_like(total)
+    tile_highest[...] = jnp.zeros_like(tile_highest)
+
+    def take_in(t):
+        for i in range(TILE):
+            came = (pair - t + tiles) % tiles * TILE + i
+
+            @pl.when(came != me)
+            def _():
+                flag_arrival(came).wait_recv()
+                slot_arrival(came).wait_recv()
+                core_copy(came).start()
+
+    def exps_copy(t):
+        rows = pl.ds((pair - t + tiles) % tiles * tile_rows, tile_rows)
+        return pltpu.make_async_copy(exps.at[t % 2], exps_out.at[:, rows], exps_sem.at[t % 2])
+
+    def keys_copy(t):
+        rows = pl.ds((pair - t + tiles) % tiles * tile_rows, tile_rows)
+        return pltpu.make_async_copy(keys.at[t % 2], kv_out.at[rows], keys_sem.at[t % 2])
+
+    take_in(0)
+
+    def tile_step(t, carry):
+        tile = (pair - t + tiles) % tiles
+
+        @pl.when(t + 1 < tiles)
+        def _():
+            take_in(t + 1)
+
+        @pl.when(t >= 2)
+        def _():
+            exps_copy(t - 2).wait()
+            keys_copy(t - 2).wait()
+
+        for i in range(TILE):
+            core_copy(tile * TILE + i).wait_recv()
+        kv_parts = []
+        for c in range(2):
+            rows = states[c, pl.ds(tile * TILE, TILE)].reshape(tile_rows, half)
+            w = full[1, 2 * c : 2 * c + 2, :, :, :, width : 3 * width]
+            kv_parts.append(mm(rows, w.reshape(half, 2 * width)))
+        keys[t % 2] = (kv_parts[0] + kv_parts[1]).astype(low)
+        keys_copy(t).start()
+        masks = []
+        for i in range(TILE):
+            for rank in range(RANKS):
+                masks.append(flags[tile * TILE + i, rank : rank + 1, :].astype(wide)[None])
+        masks = jnp.concatenate(masks, axis=0)
+        for p in range(pairs):
+            at = 2 * HEAD_DIM * p
+            head_keys = keys[t % 2, :, at : at + 2 * HEAD_DIM]
+            values_t = keys[t % 2, :, width + at : width + at + 2 * HEAD_DIM].T
+            for a in range(2):
+                h = 2 * p + a
+                scores = mm(head_keys, q_rows[h]).reshape(TILE * RANKS, passage_len, tokens) + masks
+                head_exps, top, sums = exp_rows(scores.reshape(tile_rows, tokens))
+                head_exps = head_exps.astype(low)
+                exps[t % 2, h] = head_exps
+                before = highest[h : h + 1, :]
+                now = jnp.maximum(before, top)
+                keep, add = jnp.exp(before - now), jnp.exp(top - now)
+                highest[h : h + 1, :] = now
+                tile_highest[tile, h : h + 1, :] = top
+                total[h : h + 1, :] = total[h : h + 1, :] * keep + sums * add
+                first = at + a * HEAD_DIM
+                out_t[first : first + HEAD_DIM, :] = (
+                    out_t[first : first + HEAD_DIM, :] * keep
+                    + mm(values_t[a * HEAD_DIM : (a + 1) * HEAD_DIM], head_exps) * add
+                )
+        exps_copy(t).start()
+
+        @pl.when(t == 1)
+        def _():
+            relay_near(2)
+            relay(3)
+
+        @pl.when(t == 3)
+        def _():
+            relay_near(3)
+
+        return carry
+
+    lax.fori_loop(0, tiles, tile_step, 0)
+    states_copy = pltpu.make_async_copy(states, states_out, out_sem.at[2])
+    states_copy.start()
+    for h in range(heads):
+        inverse = 1.0 / total[h : h + 1, :]
+        out_t[h * HEAD_DIM : (h + 1) * HEAD_DIM, :] *= inverse
+        scale_ref[:, h, :] = jnp.exp(tile_highest[:, h, :] - highest[h : h + 1, :]) * inverse
+    mixed_ref[...] = out_t[...].T.astype(low)
+    row_sent[1] = rows_nt(mixed_ref[...], weight(1)[:, 3 * width :])
+    row_copy(1).start()
+    residual_three = residual_ref[...] + pair_sum(1)
+    unit, factor = unit_of(residual_three)
+    normed = (unit * gains_ref[2:3, :]).astype(low)
+
+    def store_grad(i, value):
+        ff_ref[i] = value.astype(low).reshape(ff_ref.shape[1:])
+
+    arrived(2)
+    hidden, slope = gelu_both(mm(normed, weight(2)))
+    hidden = hidden.astype(low)
+    arrived(3)
+    hidden_grad = mm(cotangent_ref[...], weight(3))
+    before_grad = (hidden_grad * slope).astype(low)
+    row_sent[2] = rows_nt(before_grad, weight(2))
+    row_copy(2).start()
+    row_sent[3] = rows_nt(hidden, weight(3))
+    row_copy(3).start()
+    store_grad(0, rows_tn(normed, before_grad))
+    store_grad(1, rows_tn(cotangent_ref[...], hidden))
+    back, gain = rms_backward(pair_sum(2), unit, factor, gains_ref[2:3, :])
+    grad_ref[...] = cotangent_ref[...].astype(wide) + back
+    gain_ref[...] = gain[None, :]
+    block_ref[...] = (residual_three + pair_sum(3)).astype(low)
+
+    for g in range(groups):
+        for k in range(1, 4):
+            z_copy(g, k).wait_send()
+        for k in range(4):
+            near_copy(g, k).wait_send()
+            first_copy(g, k).wait_send()
+            second_copy(g, k).wait_send()
+    for k in range(1, CHIPS):
+        to = (me + k) % CHIPS
+        slot_copy(to).wait_send()
+        flag_copy(to).wait_send()
+    for k in range(CHIPS):
+        core_copy(k).wait_send()
+    for i in range(4):
+        row_copy(i).wait_send()
+    for t in range(tiles - 2, tiles):
+        exps_copy(t).wait()
+        keys_copy(t).wait()
+    for g in range(2):
+        weights_copy(g).wait()
+    states_copy.wait()
+
+
+def run_forward(index, shards, passages, flags, target, cotangent, gains, table, buckets):
+    low, wide = jnp.bfloat16, jnp.float32
+    groups, rows, columns = shards.shape
+    passage_len, half = passages.shape[1:]
+    tokens, model = target.shape
+    width = columns // 4
+    heads = width // HEAD_DIM
+    block_rows = RANKS * passage_len
+    key_count = CHIPS * block_rows
+    tile_rows = TILE * block_rows
+    tiles = CHIPS // TILE
+    shape = jax.ShapeDtypeStruct
+    vmem = pltpu.VMEM
+    return pl.pallas_call(
+        forward_kernel,
+        out_shape=(
+            shape((2, 4, 2, 2, rows, columns), low),
+            shape((2, CHIPS, block_rows, half), low),
+            shape((heads, key_count, tokens), low),
+            shape((key_count, 2 * width), low),
+            shape((tiles, 8, tokens), wide),
+            shape((tokens, width), low),
+            shape((tokens, width), low),
+            shape((tokens, model), wide),
+            shape((tokens, 3 * width), low),
+            shape((tokens, width), low),
+            shape((heads, tokens, tokens), low),
+            shape((8, tokens), wide),
+            shape((2, 4, 2, 2, rows, columns), low),
+            shape((tokens, model), wide),
+            shape((1, model), wide),
+            shape((tokens, model), low),
+        ),
+        in_specs=[IN_SMEM] + [IN_VMEM] * 8,
+        out_specs=(ANY,) * 4 + (IN_VMEM,) * 12,
+        scratch_shapes=[
+            vmem((groups, 4, 2, 2, rows, columns), low),
+            vmem((2, CHIPS, block_rows, half), low),
+            vmem((CHIPS, FLAG_ROWS, tokens), low),
+            vmem((CHIPS, block_rows, half), low),
+            vmem((2, heads, tile_rows, tokens), low),
+            vmem((2, tile_rows, 2 * width), low),
+            vmem((heads, tokens, tokens), wide),
+            vmem((heads, 2 * HEAD_DIM, tokens), low),
+            vmem((width, tokens), wide),
+            vmem((8, tokens), wide),
+            vmem((8, tokens), wide),
+            vmem((tiles, 8, tokens), wide),
+            vmem((4, tokens, model), wide),
+            vmem((4, tokens, model), wide),
+            DMA((groups, 3)),
+            DMA((groups, 3)),
+            DMA((groups, 4)),
+            DMA((groups, 4)),
+            DMA((groups, 4)),
+            DMA((groups, 4)),
+            DMA((groups, 4)),
+            DMA((groups, 4)),
+            DMA((CHIPS,)),
+            DMA((CHIPS,)),
+            DMA((CHIPS,)),
+            DMA((CHIPS,)),
+            DMA((CHIPS,)),
+            DMA((CHIPS,)),
+            DMA((4,)),
+            DMA((4,)),
+            DMA((groups,)),
+            DMA((2,)),
+            DMA((2,)),
+            DMA((3,)),
+        ],
+        compiler_params=pltpu.CompilerParams(
+            collective_id=0, has_side_effects=True, vmem_limit_bytes=VMEM_LIMIT
+        ),
+    )(index, shards, passages, flags, target, cotangent, gains, table, buckets)
+
+
 def route(slot_query, slot_live):
     matching = slot_query[:, None] == slot_query[None, :]
     earlier = jnp.tril(jnp.ones(matching.shape, jnp.bool_), -1)
@@ -1265,128 +1574,68 @@
         ]
     )
     position, index, live = route(slot_query, slot_live)
-    flags = jnp.repeat(live.reshape(CHIPS, RANKS), passage_len, axis=1).astype(low)
-    flags = jnp.pad(flags, ((0, 0), (0, half - RANKS * passage_len)))
-    flags = jnp.broadcast_to(flags[:, None, :], (CHIPS, FLAG_ROWS, half))
-    full, states = gather_everything(index, shards, passage_states, flags)
-    full = full.reshape(4, -1, full.shape[-1])
-    w = width_here
-    self_in, output_t = full[0, :, : 3 * w], full[0, :, 3 * w :]
-    cross_query_full = full[1, :, :w]
-    kv_weights = full[1, :, w : 3 * w]
-    cross_output_t = full[1, :, 3 * w :]
-    expand_full, reduce_t = full[2], full[3]
-    key_rows_n = CHIPS * RANKS * passage_len
-    live_keys = states[0, :, RANKS * passage_len, : RANKS * passage_len].reshape(1, key_rows_n)
-    allowed = (live_keys > 0)[:, None, None, :]
-    states = states[:, :, : RANKS * passage_len].reshape(2, key_rows_n, half)
-
-    residual = target_states.astype(jnp.float32)
-    unit_one, factor_one, normed_one = rms_forward(residual, norm_gains[0])
-    projected = jnp.dot(normed_one, self_in, preferred_element_type=jnp.float32).astype(low)
-    projected = projected.reshape(1, TLEN, 3, heads_here, HEAD_DIM)
-    queries_self = projected[:, :, 0]
-    keys_self = projected[:, :, 1]
-    values_self = projected[:, :, 2]
-    buckets = jnp.asarray(bucket_table(TLEN, bucket_count, MAXDIST))
-    one_hot = (jnp.arange(bucket_count, dtype=jnp.int32)[:, None, None] == buckets[None]).astype(
-        jnp.float32
-    )
-    bias_full = jnp.einsum("bij,bh->hij", one_hot, position_bias, precision=lax.Precision.HIGHEST)[
-        None
-    ]
-    causal = jnp.asarray(np.tril(np.ones((TLEN, TLEN), dtype=bool)))
-    attended_self, total_self = attend(queries_self, keys_self, values_self, causal, bias_full)
-    merged_self = attended_self.reshape(TLEN, w)
-    residual_two = residual + over_pair(rows_nt(merged_self, output_t))
-    unit_two, factor_two, normed_two = rms_forward(residual_two, norm_gains[1])
-    cross_queries = jnp.dot(
-        normed_two, cross_query_full, preferred_element_type=jnp.float32
-    ).astype(low)
-    cross_queries = cross_queries.reshape(1, TLEN, heads_here, HEAD_DIM)
-    key_values = jnp.dot(states[0], kv_weights[:half], preferred_element_type=jnp.float32) + jnp.dot(
-        states[1], kv_weights[half:], preferred_element_type=jnp.float32
-    )
-    key_values = key_values.astype(low).reshape(1, key_rows_n, 2, heads_here, HEAD_DIM)
-    key_rows = key_values[:, :, 0]
-    value_rows = key_values[:, :, 1]
-    scores_t = jnp.einsum(
-        "jhe,ihe->hji", key_rows[0], cross_queries[0], preferred_element_type=jnp.float32
-    )
-    head_block = 2
-    head_ranges = [
-        slice(start_head, start_head + head_block)
-        for start_head in range(0, heads_here, head_block)
-    ]
-    cross_parts = []
-    cross_totals = []
-    for head_range in head_ranges:
-        mixed_part, total_part = attend(
-            cross_queries[:, :, head_range],
-            key_rows[:, :, head_range],
-            value_rows[:, :, head_range],
-            allowed,
-            None,
-        )
-        cross_parts.append(mixed_part)
-        cross_totals.append(total_part)
-    merged_cross = jnp.concatenate(cross_parts, axis=2).reshape(TLEN, w)
-    residual_three = residual_two + over_pair(rows_nt(merged_cross, cross_output_t))
-    unit_three, factor_three, normed_three = rms_forward(residual_three, norm_gains[2])
-    before = jnp.dot(normed_three, expand_full, preferred_element_type=jnp.float32)
-    hidden = jax.nn.gelu(before, approximate=True).astype(low)
-    block_out = residual_three + over_pair(rows_nt(hidden, reduce_t))
-    grad_out = output_cotangent.astype(jnp.float32)
-    reduce_grad_t = rows_tn(output_cotangent, hidden)
-    hidden_grad = jnp.dot(output_cotangent, reduce_t, preferred_element_type=jnp.float32)
-    unused_value, gelu_pullback = jax.vjp(partial(jax.nn.gelu, approximate=True), before)
-    before_grad = gelu_pullback(hidden_grad)[0].astype(low)
-    expand_grad = rows_tn(normed_three, before_grad)
-    normed_grad = over_pair(rows_nt(before_grad, expand_full))
-    back_three, gain_three = rms_backward(normed_grad, unit_three, factor_three, norm_gains[2])
-    grad_three = grad_out + back_three
-    totals_t = jnp.concatenate(cross_totals, axis=1)[0, :, :, 0]
-    live_column = (live_keys[0] > 0)[None, :, None]
-    exps = jnp.where(live_column, jnp.exp(scores_t - totals_t[:, None, :]), 0.0).astype(low)
-    tiles = CHIPS // TILE
-    scale = jnp.ones((tiles, 8, TLEN), jnp.float32)
-    self_scores_t = jnp.einsum(
-        "jhe,ihe->hji", keys_self[0], queries_self[0], preferred_element_type=jnp.float32
-    ) + jnp.swapaxes(bias_full[0], 1, 2)
-    self_exps = jnp.where(
-        causal.T[None], jnp.exp(self_scores_t - total_self[0, :, :, 0][:, None, :]), 0.0
-    ).astype(low)
-    self_scale = jnp.ones((8, TLEN), jnp.float32)
-    ff_grads = jnp.stack([expand_grad, reduce_grad_t]).astype(low)
-    ff_grads = ff_grads.reshape((2, 4, 2, 2) + shards.shape[1:])
+    flags = jnp.where(live > 0, 0.0, MASKED).astype(low).reshape(CHIPS, RANKS, 1)
+    flags = jnp.pad(flags, ((0, 0), (0, FLAG_ROWS - RANKS), (0, 0)))
+    flags = jnp.broadcast_to(flags, (CHIPS, FLAG_ROWS, TLEN))
     distance = np.zeros((TLEN, 128), np.float32)
     distance[np.arange(TLEN), bucket_table(TLEN, bucket_count, MAXDIST)[:, 0]] = 1.0
+    table = jnp.pad(position_bias.T, ((0, 8 - heads_here), (0, 0)))
+    (
+        weights,
+        states,
+        exps,
+        key_values,
+        scale,
+        queries,
+        mixed,
+        residual,
+        qkv,
+        self_mixed,
+        self_exps,
+        self_scale,
+        ff_grads,
+        grad,
+        gain,
+        block_out,
+    ) = run_forward(
+        index,
+        shards,
+        passage_states,
+        flags,
+        target_states,
+        output_cotangent,
+        norm_gains,
+        table,
+        jnp.asarray(distance[:, :bucket_count].T),
+    )
+    w = width_here
+    weights = weights.reshape(2, -1, weights.shape[-1])
     shard_grads, passage_grad, small_total, target_grad = run_backward(
         position,
         exps,
         scale,
-        key_values.reshape(key_rows_n, 2 * w),
-        states,
-        cross_queries.reshape(TLEN, w),
-        merged_cross,
-        full[0],
-        full[1],
+        key_values,
+        states.reshape(2, -1, half),
+        queries,
+        mixed,
+        weights[0],
+        weights[1],
         ff_grads,
-        grad_three,
-        residual_two,
+        grad,
+        residual,
         target_states,
         norm_gains,
-        projected.reshape(TLEN, 3 * w),
-        merged_self,
+        qkv,
+        self_mixed,
         self_exps,
         self_scale,
         jnp.asarray(distance),
-        gain_three[None, :],
+        gain,
         slots_here,
     )
     first, second = shard_grads[0], shard_grads[1]
     return (
-        block_out.astype(low),
+        block_out,
         target_grad,
         passage_grad,
         small_total[:3],

time: 406 us -> 321 us (0.79); the launches traced: 401 us -> 320 us
  matrix products: 49 us -> 0 us
  local copies, waits for them, and re-layouts: 36.4 us -> 16.3 us
  other arithmetic: 19.9 us -> 5.64 us
    dot_general x23 -> x0, matrix products: 49 us -> none  [the longest x1 8.53 us: body(): jnp.einsum('jhe,ihe->hji', key_rows[0], cross_queries[0], preferred_eleme...]
    reduce_sum x6 -> x0, other arithmetic: 8.14 us -> none  [the longest x3 3.98 us: rms_forward(): jnp.mean(values * values, axis=-1, keepdims=True) + EPSILON]
    convert_element_type x5 -> x1, local copies, waits for them, and re-layouts: 7.41 us -> 0.09 us  [body(): jnp.where(live > 0, 0.0, MASKED).astype(low).reshape(CHIPS, RANKS, 1)]
    pallas_call x1, Pallas kernels: 138 us -> 144 us  [run_backward(): pl.pallas_call(backward_kernel, out_shape=(jax.ShapeDtypeStruct((groups,...]
    slice x4 -> x1, local copies, waits for them, and re-layouts: 9.09 us -> 4.99 us  [body(): weights[1]]
    pallas_call x5 -> x1, Pallas kernels: 156 us -> 154 us  [run_forward(): pl.pallas_call(forward_kernel, out_shape=(shape((2, 4, 2, 2, rows, column...]
where the time goes in v3:
time: 321 us; the launch traced here: 320 us
  Pallas kernels  298 us (93%)
  local copies, waits for them, and re-layouts  16.3 us (5%)
  other arithmetic  5.64 us (2%)
    pallas_call x1, Pallas kernels, run_forward(): pl.pallas_call(forward_kernel, out_shape=(shape((2, 4, 2, 2, rows, column...  154 us
    pallas_call x1, Pallas kernels, run_backward(): pl.pallas_call(backward_kernel, out_shape=(jax.ShapeDtypeStruct((groups,...  144 us

profile of v3, /device:TPU:0, one launch (start us, length us, event | category | flops | bytes accessed | tf_op | source)
XLA Modules:
  0.0 320.3 jit_solution(1394099804929469364)
XLA Ops:
  0.7 0.9 convert_reduce_fusion
  1.6 0.7 multiply_add_fusion.position_ref
  2.2 0.0 copy-start.3
  2.2 1.3 select_reduce_fusion
  3.5 0.1 convert_element_type.22
  3.6 1.3 pad.9.table_ref
  4.9 0.8 broadcast_in_dim.48.flag_ref
  5.7 0.9 maximum_bitcast_fusion
  6.6 1.9 pad_maximum_fusion.shard_ref
  8.5 153.7 %shard_map.298 = (bf16[2,4,2,2,48,1536]{5,4,3,2,1,0:T(8,128)(2,1)}, bf16[2,16,192,384]{3,2,1,0:T(8,128)(2,1)}, bf16[6,3072,256]{2,1,0:T(8,128)(2,1)}, bf16[3072,...) custom-call(s32[48]{0:T(128)} %get-tuple-element.56.index_ref, ...), custom_call_target="tpu_custom_call" | custom-call | tf_op jit(solution)/shard_map/pallas_call | solution.py:1467
  162.2 0.0 copy-done.3
  162.2 5.0 %fusion.2 = (bf16[1,4,2,2,48,1536]{5,4,3,2,1,0:T(8,128)(2,1)}, bf16[1,4,2,2,48,1536]{5,4,3,2,1,0:T(8,128)(2,1)}) fusion(bf16[2,4,2,2,48,1536]{5,4,3,2,1,0:T(8,128)(2,1)} %get-tuple-element.42), kind=kLoop, calls=%fused_computation.21 | loop fusion | bytes 9437184 | tf_op jit(solution)/shard_map/slice | solution.py:1622
  167.1 144.0 %shard_map.299 = (f32[4,48,1536]{2,1,0:T(8,128)}, bf16[40,64,384]{2,1,0:T(8,128)(2,1)}, f32[16,768]{1,0:T(8,128)}, bf16[256,768]{1,0:T(8,128)(2,1)}) custom-call(s32[40]{0:T(128)} %copy-done.3, bf16[6,3072,256]{2,1,0:T(8,128)(2,1)} %get-tuple-element.36.exps_ref, f32[8,8,256]{2,1,0:T(8,128)} %get-tuple-element.37.scale_ref, ...), custom_call_target="tpu_custom_call" | custom-call | tf_op jit(solution)/shard_map/pallas_call | solution.py:966
  311.2 0.0 copy-start.1
  311.2 0.0 copy-start.2
  311.2 1.3 slice_bitcast_fusion.6
  312.6 1.3 slice.52
  313.9 0.0 copy-start
  313.9 2.3 slice_bitcast_fusion
  316.1 0.7 slice_bitcast_fusion.4
  316.9 0.7 slice_bitcast_fusion.5
  317.6 0.0 copy-done.1
  317.6 0.7 copy.37
  318.3 0.0 copy-done.2
  318.3 0.7 copy.38
  319.1 0.0 copy-done
  319.1 1.3 copy.39
  (3 shorter events, 0.0 us)
Async XLA Ops:
  2.2 159.9 %copy-start.3 = (s32[40]{0:T(128)}, s32[40]{0:T(128)S(1)}, u32[]{:S(2)}) copy-start(s32[40]{0:T(128)S(1)} %multiply_add_fusion.position_ref) | copy-start | bytes 484
  311.2 6.4 %copy-start.1 = (bf16[256,768]{1,0:T(8,128)(2,1)S(1)}, bf16[256,768]{1,0:T(8,128)(2,1)}, u32[]{:S(2)}) copy-start(bf16[256,768]{1,0:T(8,128)(2,1)} %get-tuple-element.88) | copy-start | bytes 1179652
  311.2 7.1 %copy-start.2 = (bf16[256,768]{1,0:T(8,128)(2,1)S(1)}, bf16[256,768]{1,0:T(8,128)(2,1)}, u32[]{:S(2)}) copy-start(bf16[256,768]{1,0:T(8,128)(2,1)} %get-tuple-element.89) | copy-start | bytes 1179652
  313.9 5.2 %copy-start = (bf16[40,64,384]{2,1,0:T(8,128)(2,1)S(1)}, bf16[40,64,384]{2,1,0:T(8,128)(2,1)}, u32[]{:S(2)}) copy-start(bf16[40,64,384]{2,1,0:T(8,128)(2,1)} %get-tuple-element.90) | copy-start | bytes 5898244

commit v4 on v3

--- a/solution.py
+++ b/solution.py
@@ -509,8 +509,7 @@
     states_ref,
     query_ref,
     mixed_ref,
-    self_w_ref,
-    cross_w_ref,
+    weights_ref,
     ff_ref,
     grad_ref,
     residual_ref,
@@ -531,7 +530,8 @@
     grads,
     far_got,
     near_got,
-    z_got,
+    next_got,
+    skip_got,
     dkv,
     outgoing,
     kept_sum,
@@ -554,8 +554,10 @@
     far_recv,
     near_send,
     near_recv,
-    z_send,
-    z_recv,
+    next_send,
+    next_recv,
+    skip_send,
+    skip_recv,
     pair_send,
     pair_recv,
     slot_send,
@@ -570,6 +572,7 @@
     groups = shard_ref.shape[0]
     across_x, across_y = me + 1 - 2 * x, me + 2 - 4 * y
     kept = (1 - core) * y + core * x
+    own_side = (1 - core) * x + core * y
     partner = (me, 1 - core)
     width = query_ref.shape[1]
     pairs = width // (2 * HEAD_DIM)
@@ -597,65 +600,72 @@
     def source(g):
         return ff_ref.at[g - 2] if g >= 2 else grads.at[g]
 
-    def far_copy(g, over_x):
-        block = source(g).at[:, :, 1 - x] if over_x else source(g).at[:, 1 - y, :]
-        return remote(block, far_got.at[g], far_send.at[g], far_recv.at[g], (far, core))
+    def block_at(k, o, side):
+        return z_turned(z, k), (1 - core) * o + core * side, (1 - core) * side + core * o
+
+    def far_copy(g, i, k):
+        a, b, c = block_at(k, kept + (1 - i) * (1 - 2 * kept), 1 - own_side)
+        return remote(
+            source(g).at[a, b, c],
+            far_got.at[g, i, k],
+            far_send.at[g, i, k],
+            far_recv.at[g, i, k],
+            (far, core),
+        )
 
     def far_start(g):
-        @pl.when(core == 0)
-        def _():
-            far_copy(g, True).start()
-
-        @pl.when(core == 1)
-        def _():
-            far_copy(g, False).start()
-
-    def near_copy(g):
+        for i in range(2):
+            for k in range(3, -1, -1):
+                far_copy(g, i, k).start()
+
+    def near_copy(g, k):
         return remote(
-            far_got.at[g, :, 1 - kept], near_got.at[g], near_send.at[g], near_recv.at[g], (near, core)
+            far_got.at[g, 0, k], near_got.at[g, k], near_send.at[g, k], near_recv.at[g, k], (near, core)
         )
 
-    def z_copy(g, k):
+    def next_copy(g, k):
+        to = (me - 4 * z + 4 * z_turned(z, 2), core)
         return remote(
-            near_got.at[g, (z + k) % 4],
-            z_got.at[g, k - 1],
-            z_send.at[g, k - 1],
-            z_recv.at[g, k - 1],
-            ((me + 4 * k) % CHIPS, core),
+            near_got.at[g, 2 + k], next_got.at[g, k], next_send.at[g, k], next_recv.at[g, k], to
         )
 
+    def skip_copy(g):
+        to = (me - 4 * z + 4 * z_turned(z, 1), core)
+        return remote(near_got.at[g, 1], skip_got.at[g], skip_send.at[g], skip_recv.at[g], to)
+
     def far_add(g):
-        far_copy(g, True).wait_recv()
-
-        def step(i, carry):
-            zi, o = i // 2, i % 2
-            mine = source(g)[zi, (1 - core) * o + core * y, (1 - core) * x + core * o]
-            far_got[g, zi, o] = (mine.astype(wide) + far_got[g, zi, o].astype(wide)).astype(low)
-            return carry
-
-        lax.fori_loop(0, 8, step, 0)
-        near_copy(g).start()
+        for k in range(3, -1, -1):
+            far_copy(g, 0, k).wait_recv()
+            a, b, c = block_at(k, 1 - kept, own_side)
+            far_got[g, 0, k] = (
+                source(g)[a, b, c].astype(wide) + far_got[g, 0, k].astype(wide)
+            ).astype(low)
+            near_copy(g, k).start()
 
     def near_add(g):
-        near_copy(g).wait_recv()
-
-        def step(zi, carry):
-            near_got[g, zi] = (
-                far_got[g, zi, kept].astype(wide) + near_got[g, zi].astype(wide)
+        for k in range(3, -1, -1):
+            far_copy(g, 1, k).wait_recv()
+            near_copy(g, k).wait_recv()
+            a, b, c = block_at(k, kept, own_side)
+            near_got[g, k] = (
+                source(g)[a, b, c].astype(wide)
+                + far_got[g, 1, k].astype(wide)
+                + near_got[g, k].astype(wide)
             ).astype(low)
-            return carry
-
-        lax.fori_loop(0, 4, step, 0)
-        for k in range(1, 4):
-            z_copy(g, k).start()
-
-    def z_add(g):
-        for k in range(1, 4):
-            z_copy(g, k).wait_recv()
-        total = near_got[g, z].astype(wide)
-        for k in range(3):
-            total = total + z_got[g, k].astype(wide)
-        shard_ref[g] = total
+            if k >= 2:
+                next_copy(g, k - 2).start()
+
+    def next_add(g):
+        next_copy(g, 1).wait_recv()
+        near_got[g, 1] = (near_got[g, 1].astype(wide) + next_got[g, 1].astype(wide)).astype(low)
+        skip_copy(g).start()
+
+    def skip_add(g):
+        next_copy(g, 0).wait_recv()
+        skip_copy(g).wait_recv()
+        shard_ref[g] = (
+            near_got[g, 0].astype(wide) + next_got[g, 0].astype(wide) + skip_got[g].astype(wide)
+        )
 
     def pair_copy(t):
         return remote(
@@ -708,7 +718,7 @@
     upper_grad[...] = grad_ref[...]
     grad_low = upper_grad[...].astype(low)
     store_grad(1, 3 * width, rows_tn(grad_low, mixed_ref[...]))
-    mixed_grad = mm(grad_low, cross_w_ref[:, 3 * width :]).astype(low)
+    mixed_grad = mm(grad_low, weights_ref[1, :, 3 * width :]).astype(low)
     prepare_heads(heads, query_ref, mixed_grad, mixed_ref[...], q_pair, o_pair, o_rows, centre)
     dq_t[...] = jnp.zeros_like(dq_t)
 
@@ -751,10 +761,10 @@
         def _():
             pair_copy(t - 2).wait_send()
 
-        weights = cross_w_ref[pl.ds((1 - core) * half, half), width : 3 * width]
+        weights = weights_ref[1, pl.ds((1 - core) * half, half), width : 3 * width]
         outgoing[t % 2] = rows_nt(here, weights).astype(low)
         pair_copy(t).start()
-        weights = cross_w_ref[pl.ds(core * half, half), width : 3 * width]
+        weights = weights_ref[1, pl.ds(core * half, half), width : 3 * width]
         mine = rows_nt(here, weights).astype(low)
         for j in range(TILE):
             kept_sum[tile * TILE + j] = mine[j * block_rows : (j + 1) * block_rows]
@@ -763,18 +773,22 @@
         def _():
             finish_tile(t - 1)
 
-        @pl.when(t == 5)
+        @pl.when(t == 3)
         def _():
             far_add(2)
 
+        @pl.when(t == 6)
+        def _():
+            far_add(3)
+
         return carry
 
     lax.fori_loop(0, tiles, tile_step, 0)
     dq = dq_t[...].T.astype(low)
-    row_sent[0] = rows_nt(dq, cross_w_ref[:, :width])
+    row_sent[0] = rows_nt(dq, weights_ref[1, :, :width])
     row_copy(0).start()
     finish_tile(tiles - 1)
-    far_add(3)
+    near_add(2)
     unit_two, factor_two = unit_of(residual_ref[...])
     normed_two = (unit_two * gains_ref[1:2, :]).astype(low)
     store_grad(1, 0, rows_tn(normed_two, dq))
@@ -784,7 +798,8 @@
         parts = [rows_tn(states_ref[i], dkv[:, columns]) for i in range(2)]
         store_grad(1, width + n * 256, jnp.concatenate(parts))
     far_start(1)
-    near_add(2)
+    next_add(2)
+    near_add(3)
 
     row_copy(0).wait_recv()
     normed_grad = row_sent[0] + row_got[0]
@@ -793,7 +808,7 @@
 
     grad_low = upper_grad[...].astype(low)
     store_grad(0, 3 * width, rows_tn(grad_low, self_mixed_ref[...]))
-    mixed_grad = mm(grad_low, self_w_ref[:, 3 * width :]).astype(low)
+    mixed_grad = mm(grad_low, weights_ref[0, :, 3 * width :]).astype(low)
     prepare_heads(
         heads,
         qkv_ref.at[:, :width],
@@ -830,13 +845,14 @@
         query_rows.extend(query_parts)
     dq = jnp.concatenate(query_rows, axis=0).T.astype(low)
     dqkv = jnp.concatenate([dq] + key_columns + value_columns, axis=1)
-    row_sent[1] = rows_nt(dqkv, self_w_ref[:, : 3 * width])
+    row_sent[1] = rows_nt(dqkv, weights_ref[0, :, : 3 * width])
     row_copy(1).start()
     unit_one, factor_one = unit_of(target_ref[...].astype(wide))
     normed_one = (unit_one * gains_ref[0:1, :]).astype(low)
     store_grad(0, 0, rows_tn(normed_one, dqkv))
     far_start(0)
-    near_add(3)
+    far_add(1)
+    next_add(3)
 
     length = self_scores.shape[1]
 
@@ -885,21 +901,22 @@
         )
 
     small_copy(0).start()
-    far_add(1)
+    skip_add(2)
+    near_add(1)
     small_copy(0).wait_recv()
     small_got[6] = small[...] + small_got[0]
     small_copy(1).start()
-    z_add(2)
-    near_add(1)
+    far_add(0)
+    skip_add(3)
+    next_add(1)
     small_copy(1).wait_recv()
     small_got[7] = small_got[6] + small_got[1]
     for step in range(2, 5):
         small_copy(step).start()
     small_got[2 + z] = small_got[7]
-    far_add(0)
-    z_add(3)
-    z_add(1)
     near_add(0)
+    skip_add(1)
+    next_add(0)
     for step in range(2, 5):
         small_copy(step).wait_recv()
     small_ref[...] = small_got[2] + small_got[3] + small_got[4] + small_got[5]
@@ -913,12 +930,15 @@
         return carry
 
     lax.fori_loop(0, slots_ref.shape[0], pick, 0)
-    z_add(0)
+    skip_add(0)
     for g in range(groups):
-        far_copy(g, True).wait_send()
-        near_copy(g).wait_send()
-        for k in range(1, 4):
-            z_copy(g, k).wait_send()
+        for k in range(4):
+            far_copy(g, 0, k).wait_send()
+            far_copy(g, 1, k).wait_send()
+            near_copy(g, k).wait_send()
+        for k in range(2):
+            next_copy(g, k).wait_send()
+        skip_copy(g).wait_send()
     for t in range(tiles - 2, tiles):
         pair_copy(t).wait_send()
     for k in range(1, CHIPS):
@@ -937,8 +957,7 @@
     states,
     queries,
     mixed,
-    self_w,
-    cross_w,
+    weights,
     ff_grads,
     grad,
     residual,
@@ -971,15 +990,16 @@
             jax.ShapeDtypeStruct(small_shape, wide),
             jax.ShapeDtypeStruct((tokens, model), low),
         ),
-        in_specs=[IN_SMEM, ANY, IN_VMEM, ANY] + [IN_VMEM] * 16,
+        in_specs=[IN_SMEM, ANY, IN_VMEM, ANY] + [IN_VMEM] * 15,
         out_specs=(IN_VMEM,) * 4,
         scratch_shapes=[
             vmem((2, heads, tile_rows, tokens), low),
             vmem((2, tile_rows, 2 * width), low),
             vmem((2, 4, 2, 2, rows, columns), low),
-            vmem((groups, 4, 2, rows, columns), low),
+            vmem((groups, 2, 4, rows, columns), low),
             vmem((groups, 4, rows, columns), low),
-            vmem((groups, 3, rows, columns), low),
+            vmem((groups, 2, rows, columns), low),
+            vmem((groups, rows, columns), low),
             vmem((key_count, 2 * width), low),
             vmem((2, tile_rows, half), low),
             vmem((CHIPS, block_rows, half), low),
@@ -998,12 +1018,14 @@
             vmem((heads, tokens, tokens), low),
             DMA((2,)),
             DMA((2,)),
+            DMA((groups, 2, 4)),
+            DMA((groups, 2, 4)),
+            DMA((groups, 4)),
+            DMA((groups, 4)),
+            DMA((groups, 2)),
+            DMA((groups, 2)),
             DMA((groups,)),
             DMA((groups,)),
-            DMA((groups,)),
-            DMA((groups,)),
-            DMA((groups, 3)),
-            DMA((groups, 3)),
             DMA((2,)),
             DMA((CHIPS // TILE,)),
             DMA((CHIPS,)),
@@ -1024,8 +1046,7 @@
         states,
         queries,
         mixed,
-        self_w,
-        cross_w,
+        weights,
         ff_grads,
         grad,
         residual,
@@ -1038,6 +1059,15 @@
         buckets,
         gain_three,
     )
+
+
+def z_turned(z, k):
+    high, low = z // 2, z % 2
+    if k % 2:
+        high = 1 - high
+    if k // 2:
+        low = 1 - low
+    return 2 * high + low
 
 
 def exp_rows(scores):
@@ -1095,8 +1125,10 @@
     tile_highest,
     row_sent,
     row_got,
-    z_send,
-    z_recv,
+    skip_send,
+    skip_recv,
+    next_send,
+    next_recv,
     near_send,
     near_recv,
     first_send,
@@ -1136,28 +1168,33 @@
     def own_copy(g):
         return pltpu.make_async_copy(shard_ref.at[g], full.at[g, z, y, x], own_sem.at[g])
 
-    def z_copy(g, k):
+    def z_at(k):
+        return z_turned(z, k)
+
+    def skip_copy(g):
+        dst = full.at[g, z, y, x]
         return remote(
-            shard_ref.at[g],
-            full.at[g, z, y, x],
-            z_send.at[g, k - 1],
-            z_recv.at[g, k - 1],
-            ((me + 4 * k) % CHIPS, core),
+            shard_ref.at[g], dst, skip_send.at[g], skip_recv.at[g], (me - 4 * z + 4 * z_at(1), core)
         )
 
+    def next_copy(g, k):
+        dst = full.at[g, z_at(k), y, x]
+        to = (me - 4 * z + 4 * z_at(2), core)
+        return remote(held(g, k), dst, next_send.at[g, k], next_recv.at[g, k], to)
+
     def held(g, k):
-        return shard_ref.at[g] if k == 0 else full.at[g, (z + k) % 4, y, x]
+        return shard_ref.at[g] if k == 0 else full.at[g, z_at(k), y, x]
 
     def near_copy(g, k):
-        dst = full.at[g, (z + k) % 4, y, x]
+        dst = full.at[g, z_at(k), y, x]
         return remote(held(g, k), dst, near_send.at[g, k], near_recv.at[g, k], (near, core))
 
     def first_copy(g, k):
-        dst = full.at[g, (z + k) % 4, y, x]
+        dst = full.at[g, z_at(k), y, x]
         return remote(held(g, k), dst, first_send.at[g, k], first_recv.at[g, k], (far, core))
 
     def second_copy(g, k):
-        block = full.at[g, (z + k) % 4, other_y, other_x]
+        block = full.at[g, z_at(k), other_y, other_x]
         return remote(block, block, second_send.at[g, k], second_recv.at[g, k], (far, core))
 
     def slot_copy(to):
@@ -1188,17 +1225,23 @@
         return row_sent[i] + row_got[i]
 
     def launch(g):
-        for k in range(1, 4):
-            z_copy(g, k).start()
+        skip_copy(g).start()
+        next_copy(g, 0).start()
         near_copy(g, 0).start()
         first_copy(g, 0).start()
         own_copy(g).start()
 
-    def relay(g):
-        for k in range(1, 4):
-            z_copy(g, 4 - k).wait_recv()
-            near_copy(g, k).start()
-            first_copy(g, k).start()
+    def relay_skip(g):
+        skip_copy(g).wait_recv()
+        next_copy(g, 1).start()
+        near_copy(g, 1).start()
+        first_copy(g, 1).start()
+
+    def relay_next(g):
+        for k in range(2):
+            next_copy(g, k).wait_recv()
+            near_copy(g, k + 2).start()
+            first_copy(g, k + 2).start()
 
     def relay_near(g):
         for k in range(4):
@@ -1218,8 +1261,16 @@
         return pltpu.make_async_copy(full.at[g], weights_ref.at[g], out_sem.at[g])
 
     greet_all(me, core)
+    def send_pair(j):
+        for i in range(TILE):
+            to = (pair + j) % tiles * TILE + i
+
+            @pl.when(to != me)
+            def _():
+                flag_copy(to).start()
+                slot_copy(to).start()
+
     launch(0)
-    launch(1)
 
     def fill(to, carry):
         for rank in range(RANKS):
@@ -1229,18 +1280,10 @@
         return carry
 
     lax.fori_loop(0, CHIPS, fill, 0)
-    mate = me + 1 - 2 * x
-    flag_copy(mate).start()
-    slot_copy(mate).start()
-
-    def send_pair(j, carry):
-        for i in range(TILE):
-            to = (pair + j) % tiles * TILE + i
-            flag_copy(to).start()
-            slot_copy(to).start()
-        return carry
-
-    lax.fori_loop(1, tiles, send_pair, 0)
+    send_pair(0)
+    launch(1)
+    send_pair(1)
+    send_pair(2)
     states[core, me] = outgoing[me]
     flags[me] = flag_ref[me]
     core_copy(me).start()
@@ -1263,16 +1306,20 @@
     residual = target_ref[...].astype(wide)
     normed = (unit_of(residual)[0] * gains_ref[0:1, :]).astype(low)
 
-    relay(0)
+    relay_skip(0)
+    send_pair(3)
+    launch(2)
+    relay_next(0)
     relay_near(0)
-    relay(1)
+    relay_skip(1)
+    send_pair(4)
+    relay_next(1)
     arrived(0)
 
     qkv_ref[...] = mm(normed, weight(0)[:, : 3 * width]).astype(low)
     weights_copy(0).start()
     relay_near(1)
-    launch(2)
-    launch(3)
+    relay_skip(2)
     queries_t = qkv_ref[:, :width].astype(wide).T
     for h in range(heads):
         q_rows[h] = halves_of_rows(queries_t, h)
@@ -1299,7 +1346,8 @@
     self_mixed_ref[...] = out_t[...].T.astype(low)
     row_sent[0] = rows_nt(self_mixed_ref[...], weight(0)[:, 3 * width :])
     row_copy(0).start()
-    relay(2)
+    launch(3)
+    send_pair(5)
     arrived(1)
     weights_copy(1).start()
     residual_ref[...] = residual + pair_sum(0)
@@ -1332,14 +1380,32 @@
         rows = pl.ds((pair - t + tiles) % tiles * tile_rows, tile_rows)
         return pltpu.make_async_copy(keys.at[t % 2], kv_out.at[rows], keys_sem.at[t % 2])
 
+    send_pair(6)
+    send_pair(7)
     take_in(0)
 
     def tile_step(t, carry):
         tile = (pair - t + tiles) % tiles
+
+        @pl.when(t == 5)
+        def _():
+            relay_skip(3)
+
+        @pl.when(t == 6)
+        def _():
+            relay_next(3)
 
         @pl.when(t + 1 < tiles)
         def _():
             take_in(t + 1)
+
+        @pl.when(t == 2)
+        def _():
+            relay_next(2)
+
+        @pl.when(t == 3)
+        def _():
+            relay_near(2)
 
         @pl.when(t >= 2)
         def _():
@@ -1383,18 +1449,10 @@
                 )
         exps_copy(t).start()
 
-        @pl.when(t == 1)
-        def _():
-            relay_near(2)
-            relay(3)
-
-        @pl.when(t == 3)
-        def _():
-            relay_near(3)
-
         return carry
 
     lax.fori_loop(0, tiles, tile_step, 0)
+    relay_near(3)
     states_copy = pltpu.make_async_copy(states, states_out, out_sem.at[2])
     states_copy.start()
     for h in range(heads):
@@ -1429,8 +1487,9 @@
     block_ref[...] = (residual_three + pair_sum(3)).astype(low)
 
     for g in range(groups):
-        for k in range(1, 4):
-            z_copy(g, k).wait_send()
+        skip_copy(g).wait_send()
+        for k in range(2):
+            next_copy(g, k).wait_send()
         for k in range(4):
             near_copy(g, k).wait_send()
             first_copy(g, k).wait_send()
@@ -1501,8 +1560,10 @@
             vmem((tiles, 8, tokens), wide),
             vmem((4, tokens, model), wide),
             vmem((4, tokens, model), wide),
-            DMA((groups, 3)),
-            DMA((groups, 3)),
+            DMA((groups,)),
+            DMA((groups,)),
+            DMA((groups, 2)),
+            DMA((groups, 2)),
             DMA((groups, 4)),
             DMA((groups, 4)),
             DMA((groups, 4)),
@@ -1618,8 +1679,7 @@
         states.reshape(2, -1, half),
         queries,
         mixed,
-        weights[0],
-        weights[1],
+        weights,
         ff_grads,
         grad,
         residual,

time: 321 us -> 291 us (0.907)
  Pallas kernels: 298 us -> 272 us
  local copies, waits for them, and re-layouts: 16.3 us -> 12.2 us
    pallas_call x1, Pallas kernels: 154 us -> 133 us  [run_forward(): pl.pallas_call(forward_kernel, out_shape=(shape((2, 4, 2, 2, rows, column...]
    slice x1 -> x0, local copies, waits for them, and re-layouts: 4.99 us -> none  [body(): weights[1]]
    pallas_call x1, Pallas kernels: 144 us -> 139 us  [run_backward(): pl.pallas_call(backward_kernel, out_shape=(jax.ShapeDtypeStruct((groups,...]
where the time goes in v4:
time: 291 us; the launch traced here: 290 us
  Pallas kernels  272 us (93%)
  local copies, waits for them, and re-layouts  12.2 us (4%)
  other arithmetic  5.64 us (2%)
    pallas_call x1, Pallas kernels, run_backward(): pl.pallas_call(backward_kernel, out_shape=(jax.ShapeDtypeStruct((groups,...  139 us
    pallas_call x1, Pallas kernels, run_forward(): pl.pallas_call(forward_kernel, out_shape=(shape((2, 4, 2, 2, rows, column...  133 us

profile of v4, /device:TPU:0, one launch (start us, length us, event | category | flops | bytes accessed | tf_op | source)
XLA Modules:
  0.0 290.3 jit_solution(3425363432731796797)
XLA Ops:
  0.7 0.9 convert_reduce_fusion
  1.6 0.7 multiply_add_fusion.position_ref
  2.2 0.0 copy-start.2
  2.2 1.3 select_reduce_fusion
  3.5 0.1 convert_element_type.22
  3.6 1.3 pad.9.table_ref
  4.9 0.8 broadcast_in_dim.48.flag_ref
  5.7 0.9 maximum_bitcast_fusion
  6.6 1.9 pad_maximum_fusion.shard_ref
  8.5 132.6 %shard_map.298 = (bf16[2,4,2,2,48,1536]{5,4,3,2,1,0:T(8,128)(2,1)}, bf16[2,16,192,384]{3,2,1,0:T(8,128)(2,1)}, bf16[6,3072,256]{2,1,0:T(8,128)(2,1)}, bf16[3072,...) custom-call(s32[48]{0:T(128)} %get-tuple-element.56.index_ref, ...), custom_call_target="tpu_custom_call" | custom-call | tf_op jit(solution)/shard_map/pallas_call | solution.py:1526
  141.1 0.0 copy-done.2
  141.1 0.0 copy-start.1
  141.1 139.1 %shard_map.299 = (f32[4,48,1536]{2,1,0:T(8,128)}, bf16[40,64,384]{2,1,0:T(8,128)(2,1)}, f32[16,768]{1,0:T(8,128)}, bf16[256,768]{1,0:T(8,128)(2,1)}) custom-call(s32[40]{0:T(128)} %copy-done.2, bf16[6,3072,256]{2,1,0:T(8,128)(2,1)} %get-tuple-element.36.exps_ref, f32[8,8,256]{2,1,0:T(8,128)} %get-tuple-element.37.scale_ref, ...), custom_call_target="tpu_custom_call" | custom-call | tf_op jit(solution)/shard_map/pallas_call | solution.py:985
  280.2 0.0 copy-start
  280.3 1.4 slice_bitcast_fusion.6
  281.7 1.3 slice.42
  283.0 2.1 slice_bitcast_fusion
  285.1 0.7 slice_bitcast_fusion.4
  285.8 0.7 slice_bitcast_fusion.5
  286.5 0.0 copy-done.1
  286.6 0.7 copy.37
  287.3 1.8 copy.38
  289.1 0.0 copy-done
  289.1 1.3 copy.39
  (3 shorter events, 0.0 us)
Async XLA Ops:
  2.2 138.8 %copy-start.2 = (s32[40]{0:T(128)}, s32[40]{0:T(128)S(1)}, u32[]{:S(2)}) copy-start(s32[40]{0:T(128)S(1)} %multiply_add_fusion.position_ref) | copy-start | bytes 484
  141.1 145.5 %copy-start.1 = (bf16[256,768]{1,0:T(8,128)(2,1)S(1)}, bf16[256,768]{1,0:T(8,128)(2,1)}, u32[]{:S(2)}) copy-start(bf16[256,768]{1,0:T(8,128)(2,1)} %get-tuple-element.86) | copy-start | bytes 1179652
  280.2 8.8 %copy-start = (bf16[40,64,384]{2,1,0:T(8,128)(2,1)S(1)}, bf16[40,64,384]{2,1,0:T(8,128)(2,1)}, u32[]{:S(2)}) copy-start(bf16[40,64,384]{2,1,0:T(8,128)(2,1)} %get-tuple-element.88) | copy-start | bytes 5898244

commit v5 on v0

--- a/solution.py
+++ b/solution.py
@@ -5,6 +5,8 @@
 import jax.numpy as jnp
 import numpy as np
 from jax import lax
+from jax.experimental import pallas as pl
+from jax.experimental.pallas import tpu as pltpu
 from jax.sharding import PartitionSpec as P
 
 HEAD_DIM = 64
@@ -123,7 +125,7 @@
     return jnp.zeros((total_rows,) + rows.shape[1:], rows.dtype).at[gather_index].add(rows)
 
 
-def body(
+def body_any(
     target_states,
     passage_states,
     slot_query,
@@ -379,9 +381,1150 @@
     )
 
 
+CHIPS = 16
+RANKS = 3
+FLAG_ROWS = 16
+MESH_ID = pl.DeviceIdType.MESH
+VMEM_LIMIT = 56 * 2**20
+
+
+def fits(mesh):
+    return mesh.shape["pas"] == CHIPS and mesh.shape["mdl"] == 2
+
+
+def places():
+    me, core = lax.axis_index("pas"), lax.axis_index("mdl")
+    x, y, z = me % 2, (me // 2) % 2, me // 4
+    across_x, across_y = me + 1 - 2 * x, me + 2 - 4 * y
+    near = across_y + (across_x - across_y) * core
+    far = across_x + (across_y - across_x) * core
+    return me, core, x, y, z, near, far
+
+
+def remote(src, dst, send_sem, recv_sem, device):
+    return pltpu.make_async_remote_copy(
+        src_ref=src,
+        dst_ref=dst,
+        send_sem=send_sem,
+        recv_sem=recv_sem,
+        device_id=device,
+        device_id_type=MESH_ID,
+    )
+
+
+def greet_all(me, core):
+    barrier = pltpu.get_barrier_semaphore()
+    for k in range(1, CHIPS):
+        pl.semaphore_signal(
+            barrier, inc=1, device_id=((me + k) % CHIPS, core), device_id_type=MESH_ID
+        )
+    pl.semaphore_signal(barrier, inc=1, device_id=(me, 1 - core), device_id_type=MESH_ID)
+    pl.semaphore_wait(barrier, CHIPS)
+
+
+ANY = pl.BlockSpec(memory_space=pl.ANY)
+IN_VMEM = pl.BlockSpec(memory_space=pltpu.VMEM)
+IN_SMEM = pl.BlockSpec(memory_space=pltpu.SMEM)
+DMA = pltpu.SemaphoreType.DMA
+
+
+def rows_nt(left, right):
+    return lax.dot_general(
+        left, right, (((1,), (1,)), ((), ())), preferred_element_type=jnp.float32
+    )
+
+
+def rows_tn(left, right):
+    return lax.dot_general(
+        left, right, (((0,), (0,)), ((), ())), preferred_element_type=jnp.float32
+    )
+
+
+TILE = 2
+
+
+def mm(left, right):
+    return jnp.dot(left, right, preferred_element_type=jnp.float32)
+
+
+def halves_of_pair(rows, head):
+    lane = lax.broadcasted_iota(jnp.int32, (rows.shape[0], 2 * HEAD_DIM), 1)
+    at = head // 2 * 2 * HEAD_DIM
+    return jnp.where(lane // HEAD_DIM == head % 2, rows[:, at : at + 2 * HEAD_DIM], 0.0).astype(
+        jnp.bfloat16
+    )
+
+
+def halves_of_rows(rows, head):
+    row = lax.broadcasted_iota(jnp.int32, (2 * HEAD_DIM, rows.shape[1]), 0)
+    at = head // 2 * 2 * HEAD_DIM
+    return jnp.where(row // HEAD_DIM == head % 2, rows[at : at + 2 * HEAD_DIM], 0.0).astype(
+        jnp.bfloat16
+    )
+
+
+def unit_of(values):
+    factor = lax.rsqrt(jnp.mean(values * values, axis=-1, keepdims=True) + EPSILON)
+    return values * factor, factor
+
+
+def prepare_heads(heads, query_ref, grad, mixed, q_pair, o_pair, o_rows, centre):
+    grad = grad.astype(jnp.float32)
+    grad_t = grad.T
+    product = (grad * mixed.astype(jnp.float32)).T
+    queries = query_ref[...].astype(jnp.float32)
+    for h in range(heads):
+        q_pair[h] = halves_of_pair(queries, h)
+        o_pair[h] = halves_of_pair(grad, h)
+        o_rows[h] = halves_of_rows(grad_t, h)
+        centre[h : h + 1, :] = jnp.sum(
+            product[h * HEAD_DIM : (h + 1) * HEAD_DIM], axis=0, keepdims=True
+        )
+
+
+def head_pair_back(p, keys, values, prob, q_pair, o_pair, o_rows, centre, keep_scores):
+    low = jnp.bfloat16
+    keys_t = keys.T
+    query_parts = []
+    for a in range(2):
+        h = 2 * p + a
+        prob_grad = mm(values, o_rows[h])
+        weights = prob(h)
+        score_grad = (weights * (prob_grad - centre[h : h + 1, :])).astype(low)
+        if keep_scores is not None:
+            keep_scores(h, score_grad)
+        key_part = mm(score_grad, q_pair[h])
+        value_part = mm(weights.astype(low), o_pair[h])
+        key_grad = key_part if a == 0 else key_grad + key_part
+        value_grad = value_part if a == 0 else value_grad + value_part
+        query_parts.append(mm(keys_t[a * HEAD_DIM : (a + 1) * HEAD_DIM], score_grad))
+    return key_grad.astype(low), value_grad.astype(low), query_parts
+
+
+def z_turned(z, k):
+    high, low = z // 2, z % 2
+    if k % 2:
+        high = 1 - high
+    if k // 2:
+        low = 1 - low
+    return 2 * high + low
+
+
+def exp_rows(scores):
+    highest = jnp.max(scores, axis=0, keepdims=True)
+    exps = jnp.exp(scores - highest)
+    return exps, highest, jnp.sum(exps, axis=0, keepdims=True)
+
+
+def gelu_both(values):
+    first = math.sqrt(2 / math.pi)
+    square = values * values
+    curve = jnp.tanh(first * values * (1.0 + 0.044715 * square))
+    half = 0.5 * (1.0 + curve)
+    slope = half + 0.5 * values * (1.0 - curve * curve) * first * (1.0 + 3 * 0.044715 * square)
+    return values * half, slope
+
+
+ROW_BUFFER = (0, 1, 0, 2, 1, 0)
+ROW_BEFORE = {2: 0, 4: 1, 5: 2}
+
+
+def block_kernel(
+    index_ref,
+    position_ref,
+    shard_ref,
+    passage_ref,
+    flag_ref,
+    target_ref,
+    cotangent_ref,
+    gains_ref,
+    table_ref,
+    bucket_ref,
+    count_ref,
+    shard_out,
+    slots_ref,
+    small_ref,
+    target_grad_ref,
+    block_ref,
+    exps_out,
+    kv_out,
+    full,
+    states,
+    flags,
+    kept,
+    slot_got,
+    exps,
+    keys,
+    bias,
+    q_rows,
+    q_pair,
+    o_pair,
+    o_rows,
+    centre,
+    out_t,
+    highest,
+    total,
+    tile_highest,
+    scale_ref,
+    query_ref,
+    mixed_ref,
+    residual_ref,
+    qkv_ref,
+    self_mixed_ref,
+    self_exps_ref,
+    self_scale_ref,
+    upper_grad,
+    row_sent,
+    row_got,
+    far_got,
+    near_got,
+    next_got,
+    skip_got,
+    dkv,
+    outgoing,
+    pair_got,
+    small,
+    small_got,
+    skip_send,
+    skip_recv,
+    next_send,
+    next_recv,
+    near_send,
+    near_recv,
+    first_send,
+    first_recv,
+    second_send,
+    second_recv,
+    fold_far_send,
+    fold_far_recv,
+    fold_near_send,
+    fold_near_recv,
+    fold_next_send,
+    fold_next_recv,
+    fold_skip_send,
+    fold_skip_recv,
+    slot_send,
+    slot_recv,
+    flag_send,
+    flag_recv,
+    core_send,
+    core_recv,
+    return_send,
+    return_recv,
+    pair_send,
+    pair_recv,
+    row_send,
+    row_recv,
+    small_send,
+    small_recv,
+    own_sem,
+    exps_sem,
+    keys_sem,
+    out_sem,
+):
+    low, wide = jnp.bfloat16, jnp.float32
+    me, core, x, y, z, near, far = places()
+    groups = shard_ref.shape[0]
+    partner = (me, 1 - core)
+    pair = me // TILE
+    tiles = CHIPS // TILE
+    passage_len = states.shape[2]
+    block_rows = RANKS * passage_len
+    tile_rows = TILE * block_rows
+    tokens = target_ref.shape[0]
+    width = query_ref.shape[1]
+    kept_side = (1 - core) * y + core * x
+    own_side = (1 - core) * x + core * y
+    across_x, across_y = me + 1 - 2 * x, me + 2 - 4 * y
+    pairs = width // (2 * HEAD_DIM)
+    heads = 2 * pairs
+    half = states.shape[3]
+    other_y = y + (1 - core) * (1 - 2 * y)
+    other_x = x + core * (1 - 2 * x)
+
+    def slots_of(ref, source):
+        return ref.at[pl.ds(source * RANKS, RANKS)]
+
+    def own_copy(g):
+        return pltpu.make_async_copy(shard_ref.at[g], full.at[g, z, y, x], own_sem.at[g])
+
+    def z_at(k):
+        return z_turned(z, k)
+
+    def skip_copy(g):
+        dst = full.at[g, z, y, x]
+        return remote(
+            shard_ref.at[g], dst, skip_send.at[g], skip_recv.at[g], (me - 4 * z + 4 * z_at(1), core)
+        )
+
+    def next_copy(g, k):
+        dst = full.at[g, z_at(k), y, x]
+        to = (me - 4 * z + 4 * z_at(2), core)
+        return remote(held(g, k), dst, next_send.at[g, k], next_recv.at[g, k], to)
+
+    def held(g, k):
+        return shard_ref.at[g] if k == 0 else full.at[g, z_at(k), y, x]
+
+    def near_copy(g, k):
+        dst = full.at[g, z_at(k), y, x]
+        return remote(held(g, k), dst, near_send.at[g, k], near_recv.at[g, k], (near, core))
+
+    def first_copy(g, k):
+        dst = full.at[g, z_at(k), y, x]
+        return remote(held(g, k), dst, first_send.at[g, k], first_recv.at[g, k], (far, core))
+
+    def second_copy(g, k):
+        block = full.at[g, z_at(k), other_y, other_x]
+        return remote(block, block, second_send.at[g, k], second_recv.at[g, k], (far, core))
+
+    def slot_copy(to):
+        return remote(
+            slots_of(kept, to), slots_of(states.at[core], me), slot_send.at[to], slot_recv.at[me], (to, core)
+        )
+
+    def slot_arrival(came):
+        block = slots_of(states.at[core], came)
+        return remote(block, block, slot_send.at[came], slot_recv.at[came], (came, core))
+
+    def flag_copy(to):
+        return remote(flag_ref.at[to], flags.at[me], flag_send.at[to], flag_recv.at[me], (to, core))
+
+    def flag_arrival(came):
+        block = flags.at[came]
+        return remote(block, block, flag_send.at[came], flag_recv.at[came], (came, core))
+
+    def core_copy(came):
+        block = slots_of(states.at[core], came)
+        return remote(block, block, core_send.at[came], core_recv.at[came], partner)
+
+    def row_copy(i):
+        b = ROW_BUFFER[i]
+        return remote(row_sent.at[b], row_got.at[b], row_send.at[i], row_recv.at[i], partner)
+
+    def give(i, value):
+        if i in ROW_BEFORE:
+            row_copy(ROW_BEFORE[i]).wait_send()
+        row_sent[ROW_BUFFER[i]] = value
+        row_copy(i).start()
+
+    def pair_sum(i):
+        row_copy(i).wait_recv()
+        return row_sent[ROW_BUFFER[i]] + row_got[ROW_BUFFER[i]]
+
+    def launch(g):
+        skip_copy(g).start()
+        next_copy(g, 0).start()
+        near_copy(g, 0).start()
+        first_copy(g, 0).start()
+        own_copy(g).start()
+
+    def relay_skip(g):
+        skip_copy(g).wait_recv()
+        next_copy(g, 1).start()
+        near_copy(g, 1).start()
+        first_copy(g, 1).start()
+
+    def relay_next(g):
+        for k in range(2):
+            next_copy(g, k).wait_recv()
+            near_copy(g, k + 2).start()
+            first_copy(g, k + 2).start()
+
+    def relay_near(g):
+        for k in range(4):
+            near_copy(g, k).wait_recv()
+            second_copy(g, k).start()
+
+    def arrived(g):
+        own_copy(g).wait()
+        for k in range(4):
+            first_copy(g, k).wait_recv()
+            second_copy(g, k).wait_recv()
+
+    def weight(g):
+        return full[g].reshape(full.shape[1] * 4 * full.shape[4], full.shape[5])
+
+    staging = pltpu.make_async_copy(
+        passage_ref, slot_got.at[pl.ds(0, passage_ref.shape[0])], out_sem.at[0]
+    )
+    staging.start()
+    def block_at(k, o, side):
+        return z_turned(z, k), (1 - core) * o + core * side, (1 - core) * side + core * o
+
+    def fold_far(g, i, k):
+        a, b, c = block_at(k, kept_side + (1 - i) * (1 - 2 * kept_side), 1 - own_side)
+        return remote(
+            full.at[g, a, b, c],
+            far_got.at[g, i, k],
+            fold_far_send.at[g, i, k],
+            fold_far_recv.at[g, i, k],
+            (far, core),
+        )
+
+    def far_start(g):
+        for i in range(2):
+            for k in range(3, -1, -1):
+                fold_far(g, i, k).start()
+
+    def fold_near(g, k):
+        return remote(
+            far_got.at[g, 0, k], near_got.at[g, k], fold_near_send.at[g, k], fold_near_recv.at[g, k], (near, core)
+        )
+
+    def fold_next(g, k):
+        to = (me - 4 * z + 4 * z_turned(z, 2), core)
+        return remote(
+            near_got.at[g, 2 + k], next_got.at[g, k], fold_next_send.at[g, k], fold_next_recv.at[g, k], to
+        )
+
+    def fold_skip(g):
+        to = (me - 4 * z + 4 * z_turned(z, 1), core)
+        return remote(near_got.at[g, 1], skip_got.at[g], fold_skip_send.at[g], fold_skip_recv.at[g], to)
+
+    def far_add(g):
+        for k in range(3, -1, -1):
+            fold_far(g, 0, k).wait_recv()
+            a, b, c = block_at(k, 1 - kept_side, own_side)
+            far_got[g, 0, k] = (
+                full[g, a, b, c].astype(wide) + far_got[g, 0, k].astype(wide)
+            ).astype(low)
+            fold_near(g, k).start()
+
+    def near_add(g):
+        for k in range(3, -1, -1):
+            fold_far(g, 1, k).wait_recv()
+            fold_near(g, k).wait_recv()
+            a, b, c = block_at(k, kept_side, own_side)
+            near_got[g, k] = (
+                full[g, a, b, c].astype(wide)
+                + far_got[g, 1, k].astype(wide)
+                + near_got[g, k].astype(wide)
+            ).astype(low)
+            if k >= 2:
+                fold_next(g, k - 2).start()
+
+    def next_add(g):
+        fold_next(g, 1).wait_recv()
+        near_got[g, 1] = (near_got[g, 1].astype(wide) + next_got[g, 1].astype(wide)).astype(low)
+        fold_skip(g).start()
+
+    def skip_add(g):
+        fold_next(g, 0).wait_recv()
+        fold_skip(g).wait_recv()
+        shard_out[g] = (
+            near_got[g, 0].astype(wide) + next_got[g, 0].astype(wide) + skip_got[g].astype(wide)
+        )
+
+    greet_all(me, core)
+    def send_pair(j):
+        for i in range(TILE):
+            to = (pair + j) % tiles * TILE + i
+
+            @pl.when(to != me)
+            def _():
+                flag_copy(to).start()
+                slot_copy(to).start()
+
+    launch(0)
+
+    def fill(to, carry):
+        for rank in range(RANKS):
+            kept[to * RANKS + rank] = slot_got[index_ref[to * RANKS + rank]]
+        return carry
+
+    staging.wait()
+    lax.fori_loop(0, CHIPS, fill, 0)
+    send_pair(0)
+    launch(1)
+    send_pair(1)
+    send_pair(2)
+    states[core, pl.ds(me * RANKS, RANKS)] = kept[pl.ds(me * RANKS, RANKS)]
+    flags[me] = flag_ref[me]
+    core_copy(me).start()
+
+    line = jnp.dot(
+        table_ref[...], bucket_ref[...], precision=lax.Precision.HIGHEST, preferred_element_type=wide
+    )
+    for h in range(heads):
+        for s in range(8):
+            row = line[h : h + 1]
+            bias[h, s : s + 1, :] = row if s == 0 else pltpu.roll(row, s, 1)
+    base = bias[:, 0:8, :].reshape(heads * 8, tokens)
+
+    def bias_step(i, carry):
+        rows = pltpu.roll(base, 8 * i, 1).reshape(heads, 8, tokens)
+        bias[:, pl.ds(pl.multiple_of(8 * i, 8), 8), :] = rows
+        return carry
+
+    lax.fori_loop(1, tokens // 8, bias_step, 0)
+    residual = target_ref[...].astype(wide)
+    normed = (unit_of(residual)[0] * gains_ref[0:1, :]).astype(low)
+
+    relay_skip(0)
+    send_pair(3)
+    launch(2)
+    relay_next(0)
+    relay_near(0)
+    relay_skip(1)
+    send_pair(4)
+    relay_next(1)
+    arrived(0)
+
+    qkv_ref[...] = mm(normed, weight(0)[:, : 3 * width]).astype(low)
+    relay_near(1)
+    relay_skip(2)
+    queries_t = qkv_ref[:, :width].astype(wide).T
+    for h in range(heads):
+        q_rows[h] = halves_of_rows(queries_t, h)
+    key_at = lax.broadcasted_iota(jnp.int32, (tokens, tokens), 0)
+    query_at = lax.broadcasted_iota(jnp.int32, (tokens, tokens), 1)
+    self_scale_ref[...] = jnp.zeros_like(self_scale_ref)
+    for p in range(pairs):
+        at = 2 * HEAD_DIM * p
+        head_keys = qkv_ref[:, width + at : width + at + 2 * HEAD_DIM]
+        values_t = qkv_ref[:, 2 * width + at : 2 * width + at + 2 * HEAD_DIM].T
+        for a in range(2):
+            h = 2 * p + a
+            scores = mm(head_keys, q_rows[h]) + bias[h]
+            scores = jnp.where(key_at <= query_at, scores, MASKED)
+            head_exps, unused, sums = exp_rows(scores)
+            head_exps = head_exps.astype(low)
+            self_exps_ref[h] = head_exps
+            inverse = 1.0 / sums
+            self_scale_ref[h : h + 1, :] = inverse
+            first = at + a * HEAD_DIM
+            out_t[first : first + HEAD_DIM, :] = (
+                mm(values_t[a * HEAD_DIM : (a + 1) * HEAD_DIM], head_exps) * inverse
+            )
+    self_mixed_ref[...] = out_t[...].T.astype(low)
+    give(0, rows_nt(self_mixed_ref[...], weight(0)[:, 3 * width :]))
+    launch(3)
+    send_pair(5)
+    arrived(1)
+    residual_ref[...] = residual + pair_sum(0)
+
+    normed = (unit_of(residual_ref[...])[0] * gains_ref[1:2, :]).astype(low)
+    query_ref[...] = mm(normed, weight(1)[:, :width]).astype(low)
+    queries_t = query_ref[...].astype(wide).T
+    for h in range(heads):
+        q_rows[h] = halves_of_rows(queries_t, h)
+    out_t[...] = jnp.zeros_like(out_t)
+    highest[...] = jnp.full_like(highest, MASKED)
+    total[...] = jnp.zeros_like(total)
+    tile_highest[...] = jnp.zeros_like(tile_highest)
+
+    def take_in(t):
+        for i in range(TILE):
+            came = (pair - t + tiles) % tiles * TILE + i
+
+            @pl.when(came != me)
+            def _():
+                flag_arrival(came).wait_recv()
+                slot_arrival(came).wait_recv()
+                core_copy(came).start()
+
+    def exps_copy(t):
+        rows = pl.ds((pair - t + tiles) % tiles * tile_rows, tile_rows)
+        return pltpu.make_async_copy(exps.at[t % 2], exps_out.at[:, rows], exps_sem.at[t % 2])
+
+    def keys_copy(t):
+        rows = pl.ds((pair - t + tiles) % tiles * tile_rows, tile_rows)
+        return pltpu.make_async_copy(keys.at[t % 2], kv_out.at[rows], keys_sem.at[t % 2])
+
+    send_pair(6)
+    send_pair(7)
+    take_in(0)
+
+    def tile_step(t, carry):
+        tile = (pair - t + tiles) % tiles
+
+        @pl.when(t == 5)
+        def _():
+            relay_skip(3)
+
+        @pl.when(t == 6)
+        def _():
+            relay_next(3)
+
+        @pl.when(t + 1 < tiles)
+        def _():
+            take_in(t + 1)
+
+        @pl.when(t == 2)
+        def _():
+            relay_next(2)
+
+        @pl.when(t == 3)
+        def _():
+            relay_near(2)
+
+        @pl.when(t >= 2)
+        def _():
+            exps_copy(t - 2).wait()
+            keys_copy(t - 2).wait()
+
+        for i in range(TILE):
+            core_copy(tile * TILE + i).wait_recv()
+        kv_parts = []
+        for c in range(2):
+            rows = states[c, pl.ds(tile * TILE * RANKS, TILE * RANKS)].reshape(tile_rows, half)
+            w = full[1, 2 * c : 2 * c + 2, :, :, :, width : 3 * width]
+            kv_parts.append(mm(rows, w.reshape(half, 2 * width)))
+        keys[t % 2] = (kv_parts[0] + kv_parts[1]).astype(low)
+        keys_copy(t).start()
+        masks = []
+        for i in range(TILE):
+            for rank in range(RANKS):
+                masks.append(flags[tile * TILE + i, rank : rank + 1, :].astype(wide)[None])
+        masks = jnp.concatenate(masks, axis=0)
+        for p in range(pairs):
+            at = 2 * HEAD_DIM * p
+            head_keys = keys[t % 2, :, at : at + 2 * HEAD_DIM]
+            values_t = keys[t % 2, :, width + at : width + at + 2 * HEAD_DIM].T
+            for a in range(2):
+                h = 2 * p + a
+                scores = mm(head_keys, q_rows[h]).reshape(TILE * RANKS, passage_len, tokens) + masks
+                head_exps, top, sums = exp_rows(scores.reshape(tile_rows, tokens))
+                head_exps = head_exps.astype(low)
+                exps[t % 2, h] = head_exps
+                before = highest[h : h + 1, :]
+                now = jnp.maximum(before, top)
+                keep, add = jnp.exp(before - now), jnp.exp(top - now)
+                highest[h : h + 1, :] = now
+                tile_highest[tile, h : h + 1, :] = top
+                total[h : h + 1, :] = total[h : h + 1, :] * keep + sums * add
+                first = at + a * HEAD_DIM
+                out_t[first : first + HEAD_DIM, :] = (
+                    out_t[first : first + HEAD_DIM, :] * keep
+                    + mm(values_t[a * HEAD_DIM : (a + 1) * HEAD_DIM], head_exps) * add
+                )
+        exps_copy(t).start()
+
+        return carry
+
+    lax.fori_loop(0, tiles, tile_step, 0)
+    relay_near(3)
+    for h in range(heads):
+        inverse = 1.0 / total[h : h + 1, :]
+        out_t[h * HEAD_DIM : (h + 1) * HEAD_DIM, :] *= inverse
+        scale_ref[:, h, :] = jnp.exp(tile_highest[:, h, :] - highest[h : h + 1, :]) * inverse
+    mixed_ref[...] = out_t[...].T.astype(low)
+    give(1, rows_nt(mixed_ref[...], weight(1)[:, 3 * width :]))
+    residual_three = residual_ref[...] + pair_sum(1)
+    unit, factor = unit_of(residual_three)
+    normed = (unit * gains_ref[2:3, :]).astype(low)
+
+    for g in range(groups):
+        skip_copy(g).wait_send()
+        for k in range(2):
+            next_copy(g, k).wait_send()
+        for k in range(4):
+            near_copy(g, k).wait_send()
+            first_copy(g, k).wait_send()
+
+    def second_done(g):
+        for k in range(4):
+            second_copy(g, k).wait_send()
+
+    def store_grad(g, first, value):
+        blocks = value.astype(low).reshape(full.shape[1:5] + (value.shape[1],))
+        full[g, :, :, :, :, first : first + value.shape[1]] = blocks
+
+    arrived(2)
+    hidden, slope = gelu_both(mm(normed, weight(2)))
+    hidden = hidden.astype(low)
+    arrived(3)
+    hidden_grad = mm(cotangent_ref[...], weight(3))
+    before_grad = (hidden_grad * slope).astype(low)
+    give(2, rows_nt(before_grad, weight(2)))
+    give(3, rows_nt(hidden, weight(3)))
+    second_done(2)
+    store_grad(2, 0, rows_tn(normed, before_grad))
+    far_start(2)
+    second_done(3)
+    store_grad(3, 0, rows_tn(cotangent_ref[...], hidden))
+    far_start(3)
+    back, gain_three = rms_backward(pair_sum(2), unit, factor, gains_ref[2:3, :])
+    upper_grad[...] = cotangent_ref[...].astype(wide) + back
+    block_ref[...] = (residual_three + pair_sum(3)).astype(low)
+    second_done(0)
+    second_done(1)
+    for k in range(1, CHIPS):
+        to = (me + k) % CHIPS
+        slot_copy(to).wait_send()
+        flag_copy(to).wait_send()
+    for k in range(CHIPS):
+        core_copy(k).wait_send()
+    for t in range(tiles - 2, tiles):
+        exps_copy(t).wait()
+        keys_copy(t).wait()
+
+    def back_tile(t):
+        return (t + pair) % tiles
+
+    def exps_load(t):
+        rows = pl.ds(back_tile(t) * tile_rows, tile_rows)
+        return pltpu.make_async_copy(exps_out.at[:, rows], exps.at[t % 2], exps_sem.at[t % 2])
+
+    def keys_load(t):
+        rows = pl.ds(back_tile(t) * tile_rows, tile_rows)
+        return pltpu.make_async_copy(kv_out.at[rows], keys.at[t % 2], keys_sem.at[t % 2])
+
+    def loads_start(t):
+        exps_load(t).start()
+        keys_load(t).start()
+
+    def kv_weights(c):
+        w = full[1, pl.ds(2 * c, 2), :, :, :, width : 3 * width]
+        return w.reshape(half, 2 * width)
+
+    def pair_copy(t):
+        return remote(
+            outgoing.at[t % 2],
+            pair_got.at[pl.ds(back_tile(t) * TILE * RANKS, TILE * RANKS)],
+            pair_send.at[t % 2],
+            pair_recv.at[t],
+            partner,
+        )
+
+    def return_copy(to):
+        return remote(
+            slots_of(kept, to), slots_of(slot_got, me), return_send.at[to], return_recv.at[me], (to, core)
+        )
+
+    def return_arrival(came):
+        block = slots_of(slot_got, came)
+        return remote(block, block, return_send.at[came], return_recv.at[came], (came, core))
+
+    def finish_tile(t):
+        tile = back_tile(t)
+        pair_copy(t).wait_recv()
+        rows = pl.ds(tile * TILE * RANKS, TILE * RANKS)
+        kept[rows] = (kept[rows].astype(wide) + pair_got[rows].astype(wide)).astype(low)
+        for j in range(TILE):
+            to = tile * TILE + j
+
+            @pl.when(to != me)
+            def _():
+                return_copy(to).start()
+
+            @pl.when(to == me)
+            def _():
+                own = pl.ds(me * RANKS, RANKS)
+                slot_got[own] = kept[own]
+
+    grad_low = upper_grad[...].astype(low)
+    mixed_grad = mm(grad_low, weight(1)[:, 3 * width :]).astype(low)
+    prepare_heads(heads, query_ref, mixed_grad, mixed_ref[...], q_pair, o_pair, o_rows, centre)
+    out_t[...] = jnp.zeros_like(out_t)
+    loads_start(0)
+
+    def back_step(t, carry):
+        tile = back_tile(t)
+        rows = pl.ds(pl.multiple_of(tile * tile_rows, tile_rows), tile_rows)
+
+        @pl.when(t + 1 < tiles)
+        def _():
+            loads_start(t + 1)
+
+        exps_load(t).wait()
+        keys_load(t).wait()
+
+        def prob(h):
+            return exps[t % 2, h].astype(wide) * scale_ref[tile, h : h + 1, :]
+
+        for p in range(pairs):
+            at = 2 * HEAD_DIM * p
+            key_grad, value_grad, query_parts = head_pair_back(
+                p,
+                keys[t % 2, :, at : at + 2 * HEAD_DIM],
+                keys[t % 2, :, width + at : width + at + 2 * HEAD_DIM],
+                prob,
+                q_pair,
+                o_pair,
+                o_rows,
+                centre,
+                None,
+            )
+            dkv[rows, at : at + 2 * HEAD_DIM] = key_grad
+            dkv[rows, width + at : width + at + 2 * HEAD_DIM] = value_grad
+            for a in range(2):
+                first = at + a * HEAD_DIM
+                out_t[first : first + HEAD_DIM, :] += query_parts[a]
+        here = dkv[rows, :]
+
+        @pl.when(t >= 2)
+        def _():
+            pair_copy(t - 2).wait_send()
+
+        weights = kv_weights(1 - core)
+        outgoing[t % 2] = rows_nt(here, weights).astype(low).reshape(outgoing.shape[1:])
+        pair_copy(t).start()
+        weights = kv_weights(core)
+        mine = rows_nt(here, weights).astype(low).reshape(outgoing.shape[1:])
+        kept[pl.ds(tile * TILE * RANKS, TILE * RANKS)] = mine
+
+        @pl.when(t >= 1)
+        def _():
+            finish_tile(t - 1)
+
+        @pl.when(t == 3)
+        def _():
+            far_add(2)
+
+        @pl.when(t == 6)
+        def _():
+            far_add(3)
+
+        return carry
+
+    lax.fori_loop(0, tiles, back_step, 0)
+    dq = out_t[...].T.astype(low)
+    give(4, rows_nt(dq, weight(1)[:, :width]))
+    store_grad(1, 3 * width, rows_tn(upper_grad[...].astype(low), mixed_ref[...]))
+    finish_tile(tiles - 1)
+    near_add(2)
+    unit_two, factor_two = unit_of(residual_ref[...])
+    normed_two = (unit_two * gains_ref[1:2, :]).astype(low)
+    store_grad(1, 0, rows_tn(normed_two, dq))
+
+    for n in range(2 * width // 256):
+        columns = slice(n * 256, (n + 1) * 256)
+        parts = [rows_tn(states[i].reshape(-1, half), dkv[:, columns]) for i in range(2)]
+        store_grad(1, width + n * 256, jnp.concatenate(parts))
+    far_start(1)
+    next_add(2)
+    near_add(3)
+
+    back, gain_two = rms_backward(pair_sum(4), unit_two, factor_two, gains_ref[1:2, :])
+    upper_grad[...] += back
+
+    grad_low = upper_grad[...].astype(low)
+    mixed_grad = mm(grad_low, weight(0)[:, 3 * width :]).astype(low)
+    prepare_heads(
+        heads,
+        qkv_ref.at[:, :width],
+        mixed_grad,
+        self_mixed_ref[...],
+        q_pair,
+        o_pair,
+        o_rows,
+        centre,
+    )
+
+    def self_prob(h):
+        return self_exps_ref[h].astype(wide) * self_scale_ref[h : h + 1, :]
+
+    def keep_scores(h, score_grad):
+        self_exps_ref[h] = score_grad
+
+    query_rows, key_columns, value_columns = [], [], []
+    for p in range(pairs):
+        at = 2 * HEAD_DIM * p
+        key_grad, value_grad, query_parts = head_pair_back(
+            p,
+            qkv_ref[:, width + at : width + at + 2 * HEAD_DIM],
+            qkv_ref[:, 2 * width + at : 2 * width + at + 2 * HEAD_DIM],
+            self_prob,
+            q_pair,
+            o_pair,
+            o_rows,
+            centre,
+            keep_scores,
+        )
+        key_columns.append(key_grad)
+        value_columns.append(value_grad)
+        query_rows.extend(query_parts)
+    dq = jnp.concatenate(query_rows, axis=0).T.astype(low)
+    dqkv = jnp.concatenate([dq] + key_columns + value_columns, axis=1)
+    give(5, rows_nt(dqkv, weight(0)[:, : 3 * width]))
+    store_grad(0, 3 * width, rows_tn(upper_grad[...].astype(low), self_mixed_ref[...]))
+    unit_one, factor_one = unit_of(target_ref[...].astype(wide))
+    normed_one = (unit_one * gains_ref[0:1, :]).astype(low)
+    store_grad(0, 0, rows_tn(normed_one, dqkv))
+    far_start(0)
+    far_add(1)
+    next_add(3)
+
+    length = self_exps_ref.shape[1]
+
+    def diagonal_step(i, total):
+        rows = self_exps_ref[:, pl.ds(pl.multiple_of(16 * i, 16), 16), :].astype(wide)
+        rows = rows.reshape(heads * 16, length)
+        return total + pltpu.roll(rows, (length - 16 * i) % length, 1)
+
+    total = lax.fori_loop(
+        0, length // 16, diagonal_step, jnp.zeros((heads * 16, length), wide)
+    ).reshape(heads, 16, length)
+    small[...] = jnp.zeros_like(small)
+    for h in range(heads):
+        line = total[h, 0:1]
+        for s in range(1, 16):
+            line = line + pltpu.roll(total[h, s : s + 1], length - s, 1)
+        small[8 + h : 9 + h, :length] = line
+    by_bucket = jnp.dot(
+        small[8:16, :length], count_ref[...], precision=lax.Precision.HIGHEST,
+        preferred_element_type=wide,
+    )
+    small[8:16, :length] = jnp.zeros((8, length), wide)
+    small[8:16, : count_ref.shape[1]] = by_bucket
+
+    back, gain_one = rms_backward(pair_sum(5), unit_one, factor_one, gains_ref[0:1, :])
+    target_grad_ref[...] = (upper_grad[...] + back).astype(low)
+    small[0:1, :] = gain_one[None, :]
+    small[1:2, :] = gain_two[None, :]
+    small[2:3, :] = gain_three[None, :]
+
+    def small_copy(step):
+        if step == 0:
+            return remote(small, small_got.at[0], small_send.at[0], small_recv.at[0], (across_x, core))
+        if step == 1:
+            return remote(
+                small_got.at[6], small_got.at[1], small_send.at[1], small_recv.at[1], (across_y, core)
+            )
+        return remote(
+            small_got.at[7],
+            small_got.at[2 + z],
+            small_send.at[step],
+            small_recv.at[step],
+            ((me + 4 * (step - 1)) % CHIPS, core),
+        )
+
+    small_copy(0).start()
+    skip_add(2)
+    near_add(1)
+    small_copy(0).wait_recv()
+    small_got[6] = small[...] + small_got[0]
+    small_copy(1).start()
+    far_add(0)
+    skip_add(3)
+    next_add(1)
+    small_copy(1).wait_recv()
+    small_got[7] = small_got[6] + small_got[1]
+    for step in range(2, 5):
+        small_copy(step).start()
+    small_got[2 + z] = small_got[7]
+    near_add(0)
+    skip_add(1)
+    next_add(0)
+    for step in range(2, 5):
+        small_copy(step).wait_recv()
+    small_ref[...] = small_got[2] + small_got[3] + small_got[4] + small_got[5]
+    for k in range(1, CHIPS):
+        return_arrival((me + k) % CHIPS).wait_recv()
+    for k in range(1, CHIPS):
+        return_copy((me + k) % CHIPS).wait_send()
+    slots = slots_ref.shape[0]
+
+    def pick(slot, carry):
+        kept[slot] = slot_got[position_ref[slot]]
+        return carry
+
+    lax.fori_loop(0, slots, pick, 0)
+    picked = pltpu.make_async_copy(kept.at[pl.ds(0, slots)], slots_ref, out_sem.at[1])
+    picked.start()
+    skip_add(0)
+    for g in range(groups):
+        for k in range(4):
+            fold_far(g, 0, k).wait_send()
+            fold_far(g, 1, k).wait_send()
+            fold_near(g, k).wait_send()
+        for k in range(2):
+            fold_next(g, k).wait_send()
+        fold_skip(g).wait_send()
+    for t in range(tiles - 2, tiles):
+        pair_copy(t).wait_send()
+    for step in range(5):
+        small_copy(step).wait_send()
+    for i in range(3, 6):
+        row_copy(i).wait_send()
+    picked.wait()
+
+
+def run_block(index, position, shards, passages, flags, target, cotangent, gains, table, buckets, counts):
+    low, wide = jnp.bfloat16, jnp.float32
+    groups, rows, columns = shards.shape
+    slots, passage_len, half = passages.shape
+    tokens, model = target.shape
+    width = columns // 4
+    heads = width // HEAD_DIM
+    key_count = CHIPS * RANKS * passage_len
+    tile_rows = TILE * RANKS * passage_len
+    tiles = CHIPS // TILE
+    small_shape = (16, model)
+    shape = jax.ShapeDtypeStruct
+    vmem = pltpu.VMEM
+    pair_heads = vmem((heads, tokens, 2 * HEAD_DIM), low)
+    pair_rows = vmem((heads, 2 * HEAD_DIM, tokens), low)
+    all_slots = (CHIPS * RANKS, passage_len, half)
+
+    def both(*dims):
+        return [DMA(dims), DMA(dims)]
+
+    return pl.pallas_call(
+        block_kernel,
+        out_shape=(
+            shape((groups, rows, columns), wide),
+            shape((slots, passage_len, half), low),
+            shape(small_shape, wide),
+            shape((tokens, model), low),
+            shape((tokens, model), low),
+            shape((heads, key_count, tokens), low),
+            shape((key_count, 2 * width), low),
+        ),
+        in_specs=[IN_SMEM, IN_SMEM, IN_VMEM, ANY] + [IN_VMEM] * 7,
+        out_specs=(IN_VMEM, ANY, IN_VMEM, IN_VMEM, IN_VMEM, ANY, ANY),
+        scratch_shapes=[
+            vmem((groups, 4, 2, 2, rows, columns), low),
+            vmem((2,) + all_slots, low),
+            vmem((CHIPS, FLAG_ROWS, tokens), low),
+            vmem(all_slots, low),
+            vmem(all_slots, low),
+            vmem((2, heads, tile_rows, tokens), low),
+            vmem((2, tile_rows, 2 * width), low),
+            vmem((heads, tokens, tokens), wide),
+            pair_rows,
+            pair_heads,
+            pair_heads,
+            pair_rows,
+            vmem((8, tokens), wide),
+            vmem((width, tokens), wide),
+            vmem((8, tokens), wide),
+            vmem((8, tokens), wide),
+            vmem((tiles, 8, tokens), wide),
+            vmem((tiles, 8, tokens), wide),
+            vmem((tokens, width), low),
+            vmem((tokens, width), low),
+            vmem((tokens, model), wide),
+            vmem((tokens, 3 * width), low),
+            vmem((tokens, width), low),
+            vmem((heads, tokens, tokens), low),
+            vmem((8, tokens), wide),
+            vmem((tokens, model), wide),
+            vmem((3, tokens, model), wide),
+            vmem((3, tokens, model), wide),
+            vmem((groups, 2, 4, rows, columns), low),
+            vmem((groups, 4, rows, columns), low),
+            vmem((groups, 2, rows, columns), low),
+            vmem((groups, rows, columns), low),
+            vmem((key_count, 2 * width), low),
+            vmem((2, TILE * RANKS, passage_len, half), low),
+            vmem(all_slots, low),
+            vmem(small_shape, wide),
+            vmem((8,) + small_shape, wide),
+        ]
+        + both(groups)
+        + both(groups, 2)
+        + both(groups, 4)
+        + both(groups, 4)
+        + both(groups, 4)
+        + both(groups, 2, 4)
+        + both(groups, 4)
+        + both(groups, 2)
+        + both(groups)
+        + both(CHIPS)
+        + both(CHIPS)
+        + both(CHIPS)
+        + both(CHIPS)
+        + [DMA((2,)), DMA((tiles,))]
+        + both(6)
+        + both(5)
+        + [DMA((groups,)), DMA((2,)), DMA((2,)), DMA((2,))],
+        compiler_params=pltpu.CompilerParams(
+            collective_id=0, has_side_effects=True, vmem_limit_bytes=62 * 2**20
+        ),
+    )(index, position, shards, passages, flags, target, cotangent, gains, table, buckets, counts)
+
+
+def route(slot_query, slot_live):
+    matching = slot_query[:, None] == slot_query[None, :]
+    earlier = jnp.tril(jnp.ones(matching.shape, jnp.bool_), -1)
+    position = slot_query * RANKS + jnp.sum(jnp.logical_and(matching, earlier), axis=1).astype(
+        jnp.int32
+    )
+    here = position[None, :] == jnp.arange(CHIPS * RANKS, dtype=jnp.int32)[:, None]
+    slots = slot_query.shape[0]
+    index = jnp.sum(jnp.where(here, jnp.arange(slots, dtype=jnp.int32)[None, :], 0), axis=1)
+    live = jnp.sum(jnp.where(here, slot_live[None, :], 0), axis=1)
+    return position, index, live
+
+
+def body(
+    target_states,
+    passage_states,
+    slot_query,
+    slot_live,
+    norm_gains,
+    self_query,
+    self_key,
+    self_value,
+    self_output,
+    position_bias,
+    cross_query,
+    cross_key,
+    cross_value,
+    cross_output,
+    expand_weight,
+    reduce_weight,
+    output_cotangent,
+):
+    low = jnp.bfloat16
+    width_here = self_query.shape[1]
+    heads_here = width_here // HEAD_DIM
+    passage_len, half = passage_states.shape[1:]
+    bucket_count = position_bias.shape[0]
+    shards = jnp.stack(
+        [
+            jnp.concatenate([self_query, self_key, self_value, self_output.T], axis=1),
+            jnp.concatenate([cross_query, cross_key, cross_value, cross_output.T], axis=1),
+            expand_weight,
+            reduce_weight.T,
+        ]
+    )
+    position, index, live = route(slot_query, slot_live)
+    flags = jnp.where(live > 0, 0.0, MASKED).astype(low).reshape(CHIPS, RANKS, 1)
+    flags = jnp.pad(flags, ((0, 0), (0, FLAG_ROWS - RANKS), (0, 0)))
+    flags = jnp.broadcast_to(flags, (CHIPS, FLAG_ROWS, TLEN))
+    distance = np.zeros((TLEN, 128), np.float32)
+    distance[np.arange(TLEN), bucket_table(TLEN, bucket_count, MAXDIST)[:, 0]] = 1.0
+    table = jnp.pad(position_bias.T, ((0, 8 - heads_here), (0, 0)))
+    shard_grads, passage_grad, small_total, target_grad, block_out = run_block(
+        index,
+        position,
+        shards,
+        passage_states,
+        flags,
+        target_states,
+        output_cotangent,
+        norm_gains,
+        table,
+        jnp.asarray(distance[:, :bucket_count].T),
+        jnp.asarray(distance),
+    )[:5]
+    w = width_here
+    first, second = shard_grads[0], shard_grads[1]
+    return (
+        block_out,
+        target_grad,
+        passage_grad,
+        small_total[:3],
+        first[:, :w],
+        first[:, w : 2 * w],
+        first[:, 2 * w : 3 * w],
+        first[:, 3 * w :].T,
+        small_total[8 : 8 + heads_here, :bucket_count].T,
+        second[:, :w],
+        second[:, w : 2 * w],
+        second[:, 2 * w : 3 * w],
+        second[:, 3 * w :].T,
+        shard_grads[2],
+        shard_grads[3].T,
+    )
+
+
 def solution(mesh):
     return jax.shard_map(
-        body,
+        body if fits(mesh) else body_any,
         mesh=mesh,
         in_specs=(
             P("pas", None),

time: 2190 us -> 274 us (0.13)
  waiting for transfers between devices: 1340 us -> 0 us
  blocking collectives: 501 us -> 0 us
  Pallas kernels: 0 us -> 252 us
  local copies, waits for them, and re-layouts: 136 us -> 11.2 us
  matrix products: 105 us -> 0 us
  other arithmetic: 55.5 us -> 5.64 us
    reduce_scatter x8 -> x0, waiting for transfers between devices: 944 us -> none  [the longest x1 142 us: body(): lax.psum_scatter(reduce_grad, 'pas', scatter_dimension=1, tiled=True)]
    all_gather x8 -> x0, blocking collectives: 410 us -> none  [the longest x1 111 us: body(): lax.all_gather(self_query, 'pas', axis=0, tiled=True)]
    unnamed x22 -> x0, waiting for transfers between devices: 259 us -> none
    pallas_call x0 -> x1, Pallas kernels: none -> 252 us  [run_block(): pl.pallas_call(block_kernel, out_shape=(shape((groups, rows, columns), wi...]
    dot_general x47 -> x0, matrix products: 105 us -> none  [the longest x4 17 us: attend_back(): jnp.einsum('sihe,sjhe->shij', out_grad, values, preferred_element_type=jn...]
    psum x1 -> x0, blocking collectives: 90.5 us -> none  [body(): lax.psum((jnp.stack([gain_one, gain_two, gain_three]), bias_grad), 'pas')]
    all_to_all x3 -> x0, waiting for transfers between devices: 48.9 us -> none  [the longest x1 48.9 us: body(): lax.all_to_all(return_rows(kv_grad, gather_index, buffer_rows), 'pas', sp...]
    all_gather x3 -> x0, waiting for transfers between devices: 45.1 us -> none  [the longest x1 45.1 us: body(): lax.all_gather(expand_weight, 'pas', axis=0, tiled=True)]
  transfers between devices with their start and end apart: 22 -> 0, of which waited for: 15 -> 0; matrix products, arithmetic and copies ran while one was open for 9% -> 0% of each run, Pallas kernels for 0% -> 0%
where the time goes in v5:
time: 274 us; the launch traced here: 270 us
  Pallas kernels  252 us (92%)
  local copies, waits for them, and re-layouts  11.2 us (4%)
  other arithmetic  5.64 us (2%)
    pallas_call x1, Pallas kernels, run_block(): pl.pallas_call(block_kernel, out_shape=(shape((groups, rows, columns), wi...  252 us

profile of v5, /device:TPU:0, one launch (start us, length us, event | category | flops | bytes accessed | tf_op | source)
XLA Modules:
  0.0 269.7 jit_solution(4720170498709294558)
XLA Ops:
  0.7 0.9 convert_reduce_fusion
  1.6 0.7 multiply_add_fusion.position_ref
  2.2 0.0 copy-start.3
  2.2 1.3 select_reduce_fusion
  3.5 0.1 convert_element_type.22
  3.6 1.3 pad.9.table_ref
  4.9 0.8 broadcast_in_dim.48.flag_ref
  5.7 0.9 maximum_bitcast_fusion
  6.6 1.9 pad_maximum_fusion.shard_ref
  8.5 0.0 copy-done.3
  8.5 252.2 %shard_map.298 = (f32[4,48,1536]{2,1,0:T(8,128)}, bf16[40,64,384]{2,1,0:T(8,128)(2,1)}, f32[16,768]{1,0:T(8,128)}, bf16[256,768]{1,0:T(8,128)(2,1)}, bf16[256,76...) custom-call(s32[48]{0:T(128)} %get-tuple-element.26.index_ref, s32[40]{0:T(128)} %copy-done.3, ...), custom_call_target="tpu_custom_call" | custom-call | tf_op jit(solution)/shard_map/pallas_call | solution.py:1364
  260.7 0.0 copy-start.2
  260.7 1.3 slice_bitcast_fusion.6
  262.0 1.3 slice.42
  263.4 0.0 copy-start.1
  263.4 2.2 slice_bitcast_fusion
  265.5 0.0 copy-start
  265.5 0.7 slice_bitcast_fusion.4
  266.3 0.7 slice_bitcast_fusion.5
  267.0 0.0 copy-done.2
  267.0 0.7 copy.37
  267.7 0.0 copy-done.1
  267.7 0.7 copy.38
  268.5 0.0 copy-done
  268.5 1.3 copy.39
  (3 shorter events, 0.0 us)
Async XLA Ops:
  2.2 6.2 %copy-start.3 = (s32[40]{0:T(128)}, s32[40]{0:T(128)S(1)}, u32[]{:S(2)}) copy-start(s32[40]{0:T(128)S(1)} %multiply_add_fusion.position_ref) | copy-start | bytes 484
  260.7 6.3 %copy-start.2 = (bf16[256,768]{1,0:T(8,128)(2,1)S(1)}, bf16[256,768]{1,0:T(8,128)(2,1)}, u32[]{:S(2)}) copy-start(bf16[256,768]{1,0:T(8,128)(2,1)} %get-tuple-element.56) | copy-start | bytes 1179652
  263.4 4.3 %copy-start.1 = (bf16[256,768]{1,0:T(8,128)(2,1)S(1)}, bf16[256,768]{1,0:T(8,128)(2,1)}, u32[]{:S(2)}) copy-start(bf16[256,768]{1,0:T(8,128)(2,1)} %get-tuple-element.57) | copy-start | bytes 1179652
  265.5 2.9 %copy-start = (bf16[40,64,384]{2,1,0:T(8,128)(2,1)S(1)}, bf16[40,64,384]{2,1,0:T(8,128)(2,1)}, u32[]{:S(2)}) copy-start(bf16[40,64,384]{2,1,0:T(8,128)(2,1)} %get-tuple-element.58) | copy-start | bytes 5898244

commit v6 on v5

--- a/solution.py
+++ b/solution.py
@@ -412,14 +412,17 @@
     )
 
 
-def greet_all(me, core):
+def greet_signal(me, core):
     barrier = pltpu.get_barrier_semaphore()
     for k in range(1, CHIPS):
         pl.semaphore_signal(
             barrier, inc=1, device_id=((me + k) % CHIPS, core), device_id_type=MESH_ID
         )
     pl.semaphore_signal(barrier, inc=1, device_id=(me, 1 - core), device_id_type=MESH_ID)
-    pl.semaphore_wait(barrier, CHIPS)
+
+
+def greet_wait():
+    pl.semaphore_wait(pltpu.get_barrier_semaphore(), CHIPS)
 
 
 ANY = pl.BlockSpec(memory_space=pl.ANY)
@@ -525,16 +528,20 @@
     return values * half, slope
 
 
-ROW_BUFFER = (0, 1, 0, 2, 1, 0)
-ROW_BEFORE = {2: 0, 4: 1, 5: 2}
-
-
+GATHER_MIDDLE = ()
+FOLD_MIDDLE = ()
 def block_kernel(
     index_ref,
-    position_ref,
-    shard_ref,
+    live_ref,
+    query_of_ref,
+    rank_ref,
     passage_ref,
-    flag_ref,
+    read_self_refs,
+    write_self_ref,
+    read_cross_refs,
+    write_cross_ref,
+    expand_ref,
+    reduce_ref,
     target_ref,
     cotangent_ref,
     gains_ref,
@@ -543,11 +550,14 @@
     count_ref,
     shard_out,
     slots_ref,
-    small_ref,
+    gains_out,
+    bias_out,
     target_grad_ref,
     block_ref,
     exps_out,
     kv_out,
+    shard_ref,
+    flag_ref,
     full,
     states,
     flags,
@@ -555,7 +565,6 @@
     slot_got,
     exps,
     keys,
-    bias,
     q_rows,
     q_pair,
     o_pair,
@@ -581,6 +590,8 @@
     next_got,
     skip_got,
     dkv,
+    kv_sum,
+    early,
     outgoing,
     pair_got,
     small,
@@ -591,10 +602,8 @@
     next_recv,
     near_send,
     near_recv,
-    first_send,
-    first_recv,
-    second_send,
-    second_recv,
+    far_send,
+    far_recv,
     fold_far_send,
     fold_far_recv,
     fold_near_send,
@@ -633,9 +642,10 @@
     tile_rows = TILE * block_rows
     tokens = target_ref.shape[0]
     width = query_ref.shape[1]
-    kept_side = (1 - core) * y + core * x
-    own_side = (1 - core) * x + core * y
+    turn = 1 - core
     across_x, across_y = me + 1 - 2 * x, me + 2 - 4 * y
+    skip_to = (me - 4 * z + 4 * z_turned(z, 1), core)
+    next_to = (me - 4 * z + 4 * z_turned(z, 2), core)
     pairs = width // (2 * HEAD_DIM)
     heads = 2 * pairs
     half = states.shape[3]
@@ -651,31 +661,36 @@
     def z_at(k):
         return z_turned(z, k)
 
-    def skip_copy(g):
-        dst = full.at[g, z, y, x]
-        return remote(
-            shard_ref.at[g], dst, skip_send.at[g], skip_recv.at[g], (me - 4 * z + 4 * z_at(1), core)
-        )
-
-    def next_copy(g, k):
-        dst = full.at[g, z_at(k), y, x]
-        to = (me - 4 * z + 4 * z_at(2), core)
-        return remote(held(g, k), dst, next_send.at[g, k], next_recv.at[g, k], to)
-
-    def held(g, k):
-        return shard_ref.at[g] if k == 0 else full.at[g, z_at(k), y, x]
+    def spot(g, k, m):
+        if m == 0:
+            return full.at[g, z_at(k), y, x]
+        return full.at[g, z_at(k), other_y, other_x]
+
+    def block_of(g, k, m):
+        return shard_ref.at[g] if k == m == 0 else spot(g, k, m)
+
+    def skip_copy(g, m):
+        src, dst = block_of(g, 0, m), spot(g, 0, m)
+        return remote(src, dst, skip_send.at[g, m], skip_recv.at[g, m], skip_to)
+
+    def next_copy(g, k, m):
+        src, dst = block_of(g, k, m), spot(g, k, m)
+        return remote(src, dst, next_send.at[g, k, m], next_recv.at[g, k, m], next_to)
 
     def near_copy(g, k):
-        dst = full.at[g, z_at(k), y, x]
-        return remote(held(g, k), dst, near_send.at[g, k], near_recv.at[g, k], (near, core))
-
-    def first_copy(g, k):
-        dst = full.at[g, z_at(k), y, x]
-        return remote(held(g, k), dst, first_send.at[g, k], first_recv.at[g, k], (far, core))
-
-    def second_copy(g, k):
-        block = full.at[g, z_at(k), other_y, other_x]
-        return remote(block, block, second_send.at[g, k], second_recv.at[g, k], (far, core))
+        src, dst = block_of(g, k, 0), spot(g, k, 0)
+        return remote(src, dst, near_send.at[g, k], near_recv.at[g, k], (near, core))
+
+    def far_copy(g, k, m):
+        src, dst = block_of(g, k, m), spot(g, k, m)
+        return remote(src, dst, far_send.at[g, k, m], far_recv.at[g, k, m], (far, core))
+
+    def before_far(g):
+        if g in GATHER_MIDDLE:
+            copies = [near_copy(g, 0)] + [skip_copy(g, m) for m in range(2)]
+            return copies + [next_copy(g, k, m) for k in range(2) for m in range(2)]
+        copies = [skip_copy(g, 0)] + [next_copy(g, k, 0) for k in range(2)]
+        return copies + [near_copy(g, k) for k in range(4)]
 
     def slot_copy(to):
         return remote(
@@ -698,48 +713,67 @@
         return remote(block, block, core_send.at[came], core_recv.at[came], partner)
 
     def row_copy(i):
-        b = ROW_BUFFER[i]
+        b = i % 2
         return remote(row_sent.at[b], row_got.at[b], row_send.at[i], row_recv.at[i], partner)
 
     def give(i, value):
-        if i in ROW_BEFORE:
-            row_copy(ROW_BEFORE[i]).wait_send()
-        row_sent[ROW_BUFFER[i]] = value
+        if i >= 2:
+            row_copy(i - 2).wait_send()
+        row_sent[i % 2] = value
         row_copy(i).start()
 
     def pair_sum(i):
         row_copy(i).wait_recv()
-        return row_sent[ROW_BUFFER[i]] + row_got[ROW_BUFFER[i]]
+        return row_sent[i % 2] + row_got[i % 2]
 
     def launch(g):
-        skip_copy(g).start()
-        next_copy(g, 0).start()
-        near_copy(g, 0).start()
-        first_copy(g, 0).start()
+        if g in GATHER_MIDDLE:
+            near_copy(g, 0).start()
+        skip_copy(g, 0).start()
+        next_copy(g, 0, 0).start()
+        if g not in GATHER_MIDDLE:
+            near_copy(g, 0).start()
+        far_copy(g, 0, 0).start()
         own_copy(g).start()
 
-    def relay_skip(g):
-        skip_copy(g).wait_recv()
-        next_copy(g, 1).start()
-        near_copy(g, 1).start()
-        first_copy(g, 1).start()
-
-    def relay_next(g):
-        for k in range(2):
-            next_copy(g, k).wait_recv()
-            near_copy(g, k + 2).start()
-            first_copy(g, k + 2).start()
-
-    def relay_near(g):
-        for k in range(4):
-            near_copy(g, k).wait_recv()
-            second_copy(g, k).start()
+    def relay_one(g):
+        if g in GATHER_MIDDLE:
+            near_copy(g, 0).wait_recv()
+            skip_copy(g, 1).start()
+            next_copy(g, 0, 1).start()
+            far_copy(g, 0, 1).start()
+        else:
+            skip_copy(g, 0).wait_recv()
+            next_copy(g, 1, 0).start()
+            near_copy(g, 1).start()
+            far_copy(g, 1, 0).start()
+
+    def relay_two(g):
+        for i in range(2):
+            if g in GATHER_MIDDLE:
+                skip_copy(g, i).wait_recv()
+                next_copy(g, 1, i).start()
+                far_copy(g, 1, i).start()
+            else:
+                next_copy(g, i, 0).wait_recv()
+                near_copy(g, i + 2).start()
+                far_copy(g, i + 2, 0).start()
+
+    def relay_three(g):
+        for i in range(4):
+            if g in GATHER_MIDDLE:
+                k, m = i % 2, i // 2
+                next_copy(g, k, m).wait_recv()
+                far_copy(g, k + 2, m).start()
+            else:
+                near_copy(g, i).wait_recv()
+                far_copy(g, i, 1).start()
 
     def arrived(g):
         own_copy(g).wait()
         for k in range(4):
-            first_copy(g, k).wait_recv()
-            second_copy(g, k).wait_recv()
+            for m in range(2):
+                far_copy(g, k, m).wait_recv()
 
     def weight(g):
         return full[g].reshape(full.shape[1] * 4 * full.shape[4], full.shape[5])
@@ -748,74 +782,119 @@
         passage_ref, slot_got.at[pl.ds(0, passage_ref.shape[0])], out_sem.at[0]
     )
     staging.start()
-    def block_at(k, o, side):
-        return z_turned(z, k), (1 - core) * o + core * side, (1 - core) * side + core * o
-
-    def fold_far(g, i, k):
-        a, b, c = block_at(k, kept_side + (1 - i) * (1 - 2 * kept_side), 1 - own_side)
-        return remote(
-            full.at[g, a, b, c],
-            far_got.at[g, i, k],
-            fold_far_send.at[g, i, k],
-            fold_far_recv.at[g, i, k],
-            (far, core),
-        )
+
+    def mine(g, k, m, here):
+        near_at, far_at = (1 - turn) * y + turn * x, (1 - turn) * x + turn * y
+        near_at = near_at if m == 0 else 1 - near_at
+        far_at = far_at if here else 1 - far_at
+        grads = early if g == 3 else full.at[g]
+        return grads.at[
+            z_at(k),
+            (1 - turn) * near_at + turn * far_at,
+            (1 - turn) * far_at + turn * near_at,
+        ]
+
+    def next_place(g, k, m):
+        return next_got.at[g, k] if m == 0 else near_got.at[g, 1 + k]
+
+    def skip_place(g, m):
+        return skip_got.at[g] if m == 0 else near_got.at[g, 3]
+
+    def fold_far(g, k, m):
+        src, dst = mine(g, k, m, False), far_got.at[g, m, k]
+        sems = fold_far_send.at[g, k, m], fold_far_recv.at[g, k, m]
+        return remote(src, dst, *sems, (near, core))
+
+    def fold_near(g, k):
+        src, dst = far_got.at[g, 1, k], near_got.at[g, k]
+        return remote(src, dst, fold_near_send.at[g, k], fold_near_recv.at[g, k], (far, core))
+
+    def fold_next(g, k, m):
+        src = far_got.at[g, m, 2 + k] if g in FOLD_MIDDLE else near_got.at[g, 2 + k]
+        sems = fold_next_send.at[g, k, m], fold_next_recv.at[g, k, m]
+        return remote(src, next_place(g, k, m), *sems, next_to)
+
+    def fold_skip(g, m):
+        src = far_got.at[g, m, 1] if g in FOLD_MIDDLE else near_got.at[g, 1]
+        sems = fold_skip_send.at[g, m], fold_skip_recv.at[g, m]
+        return remote(src, skip_place(g, m), *sems, skip_to)
+
+    def fold_copies(g):
+        copies = [fold_far(g, k, m) for k in range(4) for m in range(2)]
+        if g in FOLD_MIDDLE:
+            copies += [fold_next(g, k, m) for k in range(2) for m in range(2)]
+            return copies + [fold_skip(g, m) for m in range(2)] + [fold_near(g, 0)]
+        copies += [fold_next(g, k, 0) for k in range(2)]
+        return copies + [fold_skip(g, 0)] + [fold_near(g, k) for k in range(4)]
+
+    def add_up(ref, *others):
+        total = ref[...].astype(wide)
+        for other in others:
+            total = total + other[...].astype(wide)
+        ref[...] = total.astype(low)
 
     def far_start(g):
-        for i in range(2):
-            for k in range(3, -1, -1):
-                fold_far(g, i, k).start()
-
-    def fold_near(g, k):
-        return remote(
-            far_got.at[g, 0, k], near_got.at[g, k], fold_near_send.at[g, k], fold_near_recv.at[g, k], (near, core)
-        )
-
-    def fold_next(g, k):
-        to = (me - 4 * z + 4 * z_turned(z, 2), core)
-        return remote(
-            near_got.at[g, 2 + k], next_got.at[g, k], fold_next_send.at[g, k], fold_next_recv.at[g, k], to
-        )
-
-    def fold_skip(g):
-        to = (me - 4 * z + 4 * z_turned(z, 1), core)
-        return remote(near_got.at[g, 1], skip_got.at[g], fold_skip_send.at[g], fold_skip_recv.at[g], to)
+        order = [(k, m) for m in (1, 0) for k in (3, 2, 1, 0)]
+        if g in FOLD_MIDDLE:
+            order = [(k, m) for k in (3, 2, 1, 0) for m in (1, 0)]
+        for k, m in order:
+            fold_far(g, k, m).start()
 
     def far_add(g):
-        for k in range(3, -1, -1):
-            fold_far(g, 0, k).wait_recv()
-            a, b, c = block_at(k, 1 - kept_side, own_side)
-            far_got[g, 0, k] = (
-                full[g, a, b, c].astype(wide) + far_got[g, 0, k].astype(wide)
-            ).astype(low)
-            fold_near(g, k).start()
+        if g in FOLD_MIDDLE:
+            for k, m in ((3, 1), (3, 0), (2, 1), (2, 0)):
+                fold_far(g, k, m).wait_recv()
+                add_up(far_got.at[g, m, k], mine(g, k, m, True))
+                fold_next(g, k - 2, m).start()
+        else:
+            for k in (3, 2, 1, 0):
+                fold_far(g, k, 1).wait_recv()
+                add_up(far_got.at[g, 1, k], mine(g, k, 1, True))
+                fold_near(g, k).start()
 
     def near_add(g):
-        for k in range(3, -1, -1):
-            fold_far(g, 1, k).wait_recv()
-            fold_near(g, k).wait_recv()
-            a, b, c = block_at(k, kept_side, own_side)
-            near_got[g, k] = (
-                full[g, a, b, c].astype(wide)
-                + far_got[g, 1, k].astype(wide)
-                + near_got[g, k].astype(wide)
-            ).astype(low)
-            if k >= 2:
-                fold_next(g, k - 2).start()
+        if g in FOLD_MIDDLE:
+            for m in (1, 0):
+                fold_far(g, 1, m).wait_recv()
+                fold_next(g, 1, m).wait_recv()
+                add_up(far_got.at[g, m, 1], mine(g, 1, m, True), next_place(g, 1, m))
+                fold_skip(g, m).start()
+        else:
+            for k in (3, 2, 1, 0):
+                fold_far(g, k, 0).wait_recv()
+                fold_near(g, k).wait_recv()
+                add_up(near_got.at[g, k], mine(g, k, 0, True), far_got.at[g, 0, k])
+                if k >= 2:
+                    fold_next(g, k - 2, 0).start()
 
     def next_add(g):
-        fold_next(g, 1).wait_recv()
-        near_got[g, 1] = (near_got[g, 1].astype(wide) + next_got[g, 1].astype(wide)).astype(low)
-        fold_skip(g).start()
+        if g in FOLD_MIDDLE:
+            fold_far(g, 0, 1).wait_recv()
+            fold_next(g, 0, 1).wait_recv()
+            fold_skip(g, 1).wait_recv()
+            add_up(
+                far_got.at[g, 1, 0], mine(g, 0, 1, True), next_place(g, 0, 1), skip_place(g, 1)
+            )
+            fold_near(g, 0).start()
+        else:
+            fold_next(g, 1, 0).wait_recv()
+            add_up(near_got.at[g, 1], next_place(g, 1, 0))
+            fold_skip(g, 0).start()
 
     def skip_add(g):
-        fold_next(g, 0).wait_recv()
-        fold_skip(g).wait_recv()
-        shard_out[g] = (
-            near_got[g, 0].astype(wide) + next_got[g, 0].astype(wide) + skip_got[g].astype(wide)
-        )
-
-    greet_all(me, core)
+        fold_next(g, 0, 0).wait_recv()
+        fold_skip(g, 0).wait_recv()
+        if g in FOLD_MIDDLE:
+            fold_far(g, 0, 0).wait_recv()
+            fold_near(g, 0).wait_recv()
+        parts = [near_got[g, 0], next_got[g, 0], skip_got[g]]
+        if g in FOLD_MIDDLE:
+            parts += [mine(g, 0, 0, True)[...], far_got[g, 0, 0]]
+        total = parts[0].astype(wide)
+        for part in parts[1:]:
+            total = total + part.astype(wide)
+        shard_out[g] = total
+
     def send_pair(j):
         for i in range(TILE):
             to = (pair + j) % tiles * TILE + i
@@ -825,13 +904,26 @@
                 flag_copy(to).start()
                 slot_copy(to).start()
 
-    launch(0)
-
     def fill(to, carry):
         for rank in range(RANKS):
             kept[to * RANKS + rank] = slot_got[index_ref[to * RANKS + rank]]
+        row = lax.broadcasted_iota(jnp.int32, flag_ref.shape[1:], 0)
+        marks = jnp.zeros(flag_ref.shape[1:], wide)
+        for rank in range(RANKS):
+            mark = jnp.where(live_ref[to * RANKS + rank] > 0, 0.0, MASKED)
+            marks = jnp.where(row == rank, mark, marks)
+        flag_ref[to] = marks.astype(low)
         return carry
 
+    greet_signal(me, core)
+    for g, reads, writes in ((0, read_self_refs, write_self_ref), (1, read_cross_refs, write_cross_ref)):
+        for i, read in enumerate(reads):
+            shard_ref[g, :, i * width : (i + 1) * width] = read[...]
+        shard_ref[g, :, 3 * width :] = writes[...]
+    shard_ref[2] = expand_ref[...]
+    shard_ref[3] = reduce_ref[...]
+    greet_wait()
+    launch(0)
     staging.wait()
     lax.fori_loop(0, CHIPS, fill, 0)
     send_pair(0)
@@ -842,37 +934,46 @@
     flags[me] = flag_ref[me]
     core_copy(me).start()
 
-    line = jnp.dot(
-        table_ref[...], bucket_ref[...], precision=lax.Precision.HIGHEST, preferred_element_type=wide
-    )
+    line = lax.dot_general(
+        table_ref[...],
+        bucket_ref[...],
+        (((1,), (0,)), ((), ())),
+        precision=lax.Precision.HIGHEST,
+        preferred_element_type=wide,
+    )
+    def bias_of(h):
+        return kv_sum.at[h // 3, pl.ds(0, tokens), pl.ds(h % 3 * tokens, tokens)]
+
+    turns = []
     for h in range(heads):
         for s in range(8):
             row = line[h : h + 1]
-            bias[h, s : s + 1, :] = row if s == 0 else pltpu.roll(row, s, 1)
-    base = bias[:, 0:8, :].reshape(heads * 8, tokens)
+            turns.append(row if s == 0 else pltpu.roll(row, s, 1))
+    base = jnp.concatenate(turns, axis=0)
 
     def bias_step(i, carry):
-        rows = pltpu.roll(base, 8 * i, 1).reshape(heads, 8, tokens)
-        bias[:, pl.ds(pl.multiple_of(8 * i, 8), 8), :] = rows
+        rows = pltpu.roll(base, 8 * i, 1)
+        for h in range(heads):
+            bias_of(h)[pl.ds(pl.multiple_of(8 * i, 8), 8), :] = rows[8 * h : 8 * h + 8]
         return carry
 
-    lax.fori_loop(1, tokens // 8, bias_step, 0)
+    lax.fori_loop(0, tokens // 8, bias_step, 0)
     residual = target_ref[...].astype(wide)
     normed = (unit_of(residual)[0] * gains_ref[0:1, :]).astype(low)
 
-    relay_skip(0)
+    relay_one(0)
     send_pair(3)
     launch(2)
-    relay_next(0)
-    relay_near(0)
-    relay_skip(1)
+    relay_two(0)
+    relay_three(0)
+    relay_one(1)
     send_pair(4)
-    relay_next(1)
+    relay_two(1)
     arrived(0)
 
     qkv_ref[...] = mm(normed, weight(0)[:, : 3 * width]).astype(low)
-    relay_near(1)
-    relay_skip(2)
+    relay_three(1)
+    relay_one(2)
     queries_t = qkv_ref[:, :width].astype(wide).T
     for h in range(heads):
         q_rows[h] = halves_of_rows(queries_t, h)
@@ -885,7 +986,7 @@
         values_t = qkv_ref[:, 2 * width + at : 2 * width + at + 2 * HEAD_DIM].T
         for a in range(2):
             h = 2 * p + a
-            scores = mm(head_keys, q_rows[h]) + bias[h]
+            scores = mm(head_keys, q_rows[h]) + bias_of(h)[...]
             scores = jnp.where(key_at <= query_at, scores, MASKED)
             head_exps, unused, sums = exp_rows(scores)
             head_exps = head_exps.astype(low)
@@ -940,11 +1041,11 @@
 
         @pl.when(t == 5)
         def _():
-            relay_skip(3)
+            relay_one(3)
 
         @pl.when(t == 6)
         def _():
-            relay_next(3)
+            relay_two(3)
 
         @pl.when(t + 1 < tiles)
         def _():
@@ -952,11 +1053,11 @@
 
         @pl.when(t == 2)
         def _():
-            relay_next(2)
+            relay_two(2)
 
         @pl.when(t == 3)
         def _():
-            relay_near(2)
+            relay_three(2)
 
         @pl.when(t >= 2)
         def _():
@@ -1003,7 +1104,7 @@
         return carry
 
     lax.fori_loop(0, tiles, tile_step, 0)
-    relay_near(3)
+    relay_three(3)
     for h in range(heads):
         inverse = 1.0 / total[h : h + 1, :]
         out_t[h * HEAD_DIM : (h + 1) * HEAD_DIM, :] *= inverse
@@ -1014,17 +1115,10 @@
     unit, factor = unit_of(residual_three)
     normed = (unit * gains_ref[2:3, :]).astype(low)
 
-    for g in range(groups):
-        skip_copy(g).wait_send()
-        for k in range(2):
-            next_copy(g, k).wait_send()
-        for k in range(4):
-            near_copy(g, k).wait_send()
-            first_copy(g, k).wait_send()
-
-    def second_done(g):
-        for k in range(4):
-            second_copy(g, k).wait_send()
+
+    def sends_done(g):
+        for copy in before_far(g) + [far_copy(g, k, m) for k in range(4) for m in range(2)]:
+            copy.wait_send()
 
     def store_grad(g, first, value):
         blocks = value.astype(low).reshape(full.shape[1:5] + (value.shape[1],))
@@ -1033,22 +1127,21 @@
     arrived(2)
     hidden, slope = gelu_both(mm(normed, weight(2)))
     hidden = hidden.astype(low)
+    early[...] = rows_tn(cotangent_ref[...], hidden).astype(low).reshape(early.shape)
+    far_start(3)
     arrived(3)
     hidden_grad = mm(cotangent_ref[...], weight(3))
     before_grad = (hidden_grad * slope).astype(low)
     give(2, rows_nt(before_grad, weight(2)))
-    give(3, rows_nt(hidden, weight(3)))
-    second_done(2)
+    sends_done(2)
     store_grad(2, 0, rows_tn(normed, before_grad))
     far_start(2)
-    second_done(3)
-    store_grad(3, 0, rows_tn(cotangent_ref[...], hidden))
-    far_start(3)
     back, gain_three = rms_backward(pair_sum(2), unit, factor, gains_ref[2:3, :])
     upper_grad[...] = cotangent_ref[...].astype(wide) + back
-    block_ref[...] = (residual_three + pair_sum(3)).astype(low)
-    second_done(0)
-    second_done(1)
+    give(3, rows_nt(hidden, weight(3)))
+    sends_done(0)
+    sends_done(1)
+    sends_done(3)
     for k in range(1, CHIPS):
         to = (me + k) % CHIPS
         slot_copy(to).wait_send()
@@ -1117,12 +1210,12 @@
     mixed_grad = mm(grad_low, weight(1)[:, 3 * width :]).astype(low)
     prepare_heads(heads, query_ref, mixed_grad, mixed_ref[...], q_pair, o_pair, o_rows, centre)
     out_t[...] = jnp.zeros_like(out_t)
+    kv_sum[...] = jnp.zeros_like(kv_sum)
     loads_start(0)
+    block_ref[...] = (residual_three + pair_sum(3)).astype(low)
 
     def back_step(t, carry):
         tile = back_tile(t)
-        rows = pl.ds(pl.multiple_of(tile * tile_rows, tile_rows), tile_rows)
-
         @pl.when(t + 1 < tiles)
         def _():
             loads_start(t + 1)
@@ -1146,12 +1239,12 @@
                 centre,
                 None,
             )
-            dkv[rows, at : at + 2 * HEAD_DIM] = key_grad
-            dkv[rows, width + at : width + at + 2 * HEAD_DIM] = value_grad
+            dkv[:, at : at + 2 * HEAD_DIM] = key_grad
+            dkv[:, width + at : width + at + 2 * HEAD_DIM] = value_grad
             for a in range(2):
                 first = at + a * HEAD_DIM
                 out_t[first : first + HEAD_DIM, :] += query_parts[a]
-        here = dkv[rows, :]
+        here = dkv[...]
 
         @pl.when(t >= 2)
         def _():
@@ -1163,6 +1256,10 @@
         weights = kv_weights(core)
         mine = rows_nt(here, weights).astype(low).reshape(outgoing.shape[1:])
         kept[pl.ds(tile * TILE * RANKS, TILE * RANKS)] = mine
+
+        rows = pl.ds(tile * TILE * RANKS, TILE * RANKS)
+        for i in range(2):
+            kv_sum[i] += rows_tn(states[i, rows].reshape(tile_rows, half), here)
 
         @pl.when(t >= 1)
         def _():
@@ -1188,13 +1285,9 @@
     normed_two = (unit_two * gains_ref[1:2, :]).astype(low)
     store_grad(1, 0, rows_tn(normed_two, dq))
 
-    for n in range(2 * width // 256):
-        columns = slice(n * 256, (n + 1) * 256)
-        parts = [rows_tn(states[i].reshape(-1, half), dkv[:, columns]) for i in range(2)]
-        store_grad(1, width + n * 256, jnp.concatenate(parts))
+    store_grad(1, width, kv_sum[...].reshape(2 * half, 2 * width))
     far_start(1)
     next_add(2)
-    near_add(3)
 
     back, gain_two = rms_backward(pair_sum(4), unit_two, factor_two, gains_ref[1:2, :])
     upper_grad[...] += back
@@ -1237,6 +1330,7 @@
         query_rows.extend(query_parts)
     dq = jnp.concatenate(query_rows, axis=0).T.astype(low)
     dqkv = jnp.concatenate([dq] + key_columns + value_columns, axis=1)
+    near_add(3)
     give(5, rows_nt(dqkv, weight(0)[:, : 3 * width]))
     store_grad(0, 3 * width, rows_tn(upper_grad[...].astype(low), self_mixed_ref[...]))
     unit_one, factor_one = unit_of(target_ref[...].astype(wide))
@@ -1293,57 +1387,57 @@
     small_copy(0).start()
     skip_add(2)
     near_add(1)
+    far_add(0)
+    skip_add(3)
+    next_add(1)
+    near_add(0)
+    next_add(0)
+    skip_add(1)
     small_copy(0).wait_recv()
     small_got[6] = small[...] + small_got[0]
     small_copy(1).start()
-    far_add(0)
-    skip_add(3)
-    next_add(1)
+    for k in range(1, CHIPS):
+        return_arrival((me + k) % CHIPS).wait_recv()
     small_copy(1).wait_recv()
     small_got[7] = small_got[6] + small_got[1]
     for step in range(2, 5):
         small_copy(step).start()
     small_got[2 + z] = small_got[7]
-    near_add(0)
-    skip_add(1)
-    next_add(0)
-    for step in range(2, 5):
-        small_copy(step).wait_recv()
-    small_ref[...] = small_got[2] + small_got[3] + small_got[4] + small_got[5]
-    for k in range(1, CHIPS):
-        return_arrival((me + k) % CHIPS).wait_recv()
     for k in range(1, CHIPS):
         return_copy((me + k) % CHIPS).wait_send()
     slots = slots_ref.shape[0]
 
     def pick(slot, carry):
-        kept[slot] = slot_got[position_ref[slot]]
+        kept[slot] = slot_got[query_of_ref[slot] * RANKS + rank_ref[slot]]
         return carry
 
     lax.fori_loop(0, slots, pick, 0)
     picked = pltpu.make_async_copy(kept.at[pl.ds(0, slots)], slots_ref, out_sem.at[1])
     picked.start()
     skip_add(0)
+    for step in range(2, 5):
+        small_copy(step).wait_recv()
+    whole = small_got[2] + small_got[3] + small_got[4] + small_got[5]
+    gains_out[...] = whole[: gains_out.shape[0]]
+    bias_out[...] = whole[8 : 8 + heads, : bias_out.shape[1]]
     for g in range(groups):
-        for k in range(4):
-            fold_far(g, 0, k).wait_send()
-            fold_far(g, 1, k).wait_send()
-            fold_near(g, k).wait_send()
-        for k in range(2):
-            fold_next(g, k).wait_send()
-        fold_skip(g).wait_send()
+        for copy in fold_copies(g):
+            copy.wait_send()
     for t in range(tiles - 2, tiles):
         pair_copy(t).wait_send()
     for step in range(5):
         small_copy(step).wait_send()
-    for i in range(3, 6):
+    for i in range(4, 6):
         row_copy(i).wait_send()
     picked.wait()
 
 
-def run_block(index, position, shards, passages, flags, target, cotangent, gains, table, buckets, counts):
+def run_block(
+    index, live, query_of, rank, passages, weights, target, cotangent, gains, table, buckets, counts
+):
     low, wide = jnp.bfloat16, jnp.float32
-    groups, rows, columns = shards.shape
+    groups = 4
+    rows, columns = weights[4].shape
     slots, passage_len, half = passages.shape
     tokens, model = target.shape
     width = columns // 4
@@ -1366,15 +1460,20 @@
         out_shape=(
             shape((groups, rows, columns), wide),
             shape((slots, passage_len, half), low),
-            shape(small_shape, wide),
+            shape(gains.shape, wide),
+            shape(table.shape, wide),
             shape((tokens, model), low),
             shape((tokens, model), low),
             shape((heads, key_count, tokens), low),
             shape((key_count, 2 * width), low),
         ),
-        in_specs=[IN_SMEM, IN_SMEM, IN_VMEM, ANY] + [IN_VMEM] * 7,
-        out_specs=(IN_VMEM, ANY, IN_VMEM, IN_VMEM, IN_VMEM, ANY, ANY),
+        in_specs=[IN_SMEM] * 4
+        + [ANY, (IN_VMEM,) * 3, IN_VMEM, (IN_VMEM,) * 3, IN_VMEM, IN_VMEM, IN_VMEM]
+        + [IN_VMEM] * 6,
+        out_specs=(IN_VMEM, ANY) + (IN_VMEM,) * 4 + (ANY, ANY),
         scratch_shapes=[
+            vmem((groups, rows, columns), low),
+            vmem((CHIPS, FLAG_ROWS, tokens), low),
             vmem((groups, 4, 2, 2, rows, columns), low),
             vmem((2,) + all_slots, low),
             vmem((CHIPS, FLAG_ROWS, tokens), low),
@@ -1382,7 +1481,6 @@
             vmem(all_slots, low),
             vmem((2, heads, tile_rows, tokens), low),
             vmem((2, tile_rows, 2 * width), low),
-            vmem((heads, tokens, tokens), wide),
             pair_rows,
             pair_heads,
             pair_heads,
@@ -1401,27 +1499,28 @@
             vmem((heads, tokens, tokens), low),
             vmem((8, tokens), wide),
             vmem((tokens, model), wide),
-            vmem((3, tokens, model), wide),
-            vmem((3, tokens, model), wide),
+            vmem((2, tokens, model), wide),
+            vmem((2, tokens, model), wide),
             vmem((groups, 2, 4, rows, columns), low),
             vmem((groups, 4, rows, columns), low),
             vmem((groups, 2, rows, columns), low),
             vmem((groups, rows, columns), low),
-            vmem((key_count, 2 * width), low),
+            vmem((tile_rows, 2 * width), low),
+            vmem((2, half, 2 * width), wide),
+            vmem((4, 2, 2, rows, columns), low),
             vmem((2, TILE * RANKS, passage_len, half), low),
             vmem(all_slots, low),
             vmem(small_shape, wide),
             vmem((8,) + small_shape, wide),
         ]
-        + both(groups)
         + both(groups, 2)
+        + both(groups, 2, 2)
         + both(groups, 4)
+        + both(groups, 4, 2)
+        + both(groups, 4, 2)
         + both(groups, 4)
-        + both(groups, 4)
-        + both(groups, 2, 4)
-        + both(groups, 4)
+        + both(groups, 2, 2)
         + both(groups, 2)
-        + both(groups)
         + both(CHIPS)
         + both(CHIPS)
         + both(CHIPS)
@@ -1433,20 +1532,19 @@
         compiler_params=pltpu.CompilerParams(
             collective_id=0, has_side_effects=True, vmem_limit_bytes=62 * 2**20
         ),
-    )(index, position, shards, passages, flags, target, cotangent, gains, table, buckets, counts)
+    )(index, live, query_of, rank, passages, *weights, target, cotangent, gains, table, buckets, counts)
 
 
 def route(slot_query, slot_live):
     matching = slot_query[:, None] == slot_query[None, :]
     earlier = jnp.tril(jnp.ones(matching.shape, jnp.bool_), -1)
-    position = slot_query * RANKS + jnp.sum(jnp.logical_and(matching, earlier), axis=1).astype(
-        jnp.int32
-    )
+    rank = jnp.sum(jnp.logical_and(matching, earlier), axis=1).astype(jnp.int32)
+    position = slot_query * RANKS + rank
     here = position[None, :] == jnp.arange(CHIPS * RANKS, dtype=jnp.int32)[:, None]
     slots = slot_query.shape[0]
     index = jnp.sum(jnp.where(here, jnp.arange(slots, dtype=jnp.int32)[None, :], 0), axis=1)
     live = jnp.sum(jnp.where(here, slot_live[None, :], 0), axis=1)
-    return position, index, live
+    return rank, index, live
 
 
 def body(
@@ -1473,46 +1571,42 @@
     heads_here = width_here // HEAD_DIM
     passage_len, half = passage_states.shape[1:]
     bucket_count = position_bias.shape[0]
-    shards = jnp.stack(
-        [
-            jnp.concatenate([self_query, self_key, self_value, self_output.T], axis=1),
-            jnp.concatenate([cross_query, cross_key, cross_value, cross_output.T], axis=1),
+    rank, index, live = route(slot_query, slot_live)
+    distance = np.zeros((TLEN, 128), np.float32)
+    distance[np.arange(TLEN), bucket_table(TLEN, bucket_count, MAXDIST)[:, 0]] = 1.0
+    shard_grads, passage_grad, gains_grad, bias_grad, target_grad, block_out = run_block(
+        index,
+        live,
+        slot_query,
+        rank,
+        passage_states,
+        (
+            (self_query, self_key, self_value),
+            self_output.T,
+            (cross_query, cross_key, cross_value),
+            cross_output.T,
             expand_weight,
             reduce_weight.T,
-        ]
-    )
-    position, index, live = route(slot_query, slot_live)
-    flags = jnp.where(live > 0, 0.0, MASKED).astype(low).reshape(CHIPS, RANKS, 1)
-    flags = jnp.pad(flags, ((0, 0), (0, FLAG_ROWS - RANKS), (0, 0)))
-    flags = jnp.broadcast_to(flags, (CHIPS, FLAG_ROWS, TLEN))
-    distance = np.zeros((TLEN, 128), np.float32)
-    distance[np.arange(TLEN), bucket_table(TLEN, bucket_count, MAXDIST)[:, 0]] = 1.0
-    table = jnp.pad(position_bias.T, ((0, 8 - heads_here), (0, 0)))
-    shard_grads, passage_grad, small_total, target_grad, block_out = run_block(
-        index,
-        position,
-        shards,
-        passage_states,
-        flags,
+        ),
         target_states,
         output_cotangent,
         norm_gains,
-        table,
+        position_bias.T,
         jnp.asarray(distance[:, :bucket_count].T),
         jnp.asarray(distance),
-    )[:5]
+    )[:6]
     w = width_here
     first, second = shard_grads[0], shard_grads[1]
     return (
         block_out,
         target_grad,
         passage_grad,
-        small_total[:3],
+        gains_grad,
         first[:, :w],
         first[:, w : 2 * w],
         first[:, 2 * w : 3 * w],
         first[:, 3 * w :].T,
-        small_total[8 : 8 + heads_here, :bucket_count].T,
+        bias_grad.T,
         second[:, :w],
         second[:, w : 2 * w],
         second[:, 2 * w : 3 * w],

time: 274 us -> 259 us (0.945); the launches traced: 270 us -> 259 us
  local copies, waits for them, and re-layouts: 11.2 us -> 6.98 us
  Pallas kernels: 252 us -> 248 us
  other arithmetic: 5.64 us -> 2.84 us
    pallas_call x1, Pallas kernels: 252 us -> 248 us  [run_block(): pl.pallas_call(block_kernel, out_shape=(shape((groups, rows, columns), wi...]
    another operation x2 -> x0, other arithmetic: 2.79 us -> none  [body(): jnp.stack([jnp.concatenate([self_query, self_key, self_value, self_output...]
where the time goes in v6:
time: 259 us
  Pallas kernels  248 us (96%)
  local copies, waits for them, and re-layouts  6.98 us (3%)
  other arithmetic  2.84 us (1%)
    pallas_call x1, Pallas kernels, run_block(): pl.pallas_call(block_kernel, out_shape=(shape((groups, rows, columns), wi...  248 us

profile of v6, /device:TPU:0, one launch (start us, length us, event | category | flops | bytes accessed | tf_op | source)
XLA Modules:
  0.0 258.5 jit_solution(1198572986054825713)
XLA Ops:
  0.7 0.9 convert_reduce_fusion.rank_ref
  1.6 0.0 copy-start.5
  1.6 0.7 multiply_add_fusion
  2.2 1.3 select_reduce_fusion
  3.5 0.0 copy-done.5
  3.5 248.0 %shard_map.298 = (f32[4,48,1536]{2,1,0:T(8,128)}, bf16[40,64,384]{2,1,0:T(8,128)(2,1)}, f32[3,768]{1,0:T(4,128)}, f32[6,32]{1,0:T(8,128)}, bf16[256,768]{1,0:T(8...) custom-call(s32[48]{0:T(128)} %get-tuple-element.28.index_ref, ...), custom_call_target="tpu_custom_call" | custom-call | tf_op jit(solution)/shard_map/pallas_call | solution.py:1458
  251.5 0.0 copy-start.2
  251.5 0.0 copy-start.1
  251.6 2.2 slice_bitcast_fusion
  253.7 0.0 copy-start
  253.7 0.8 slice_bitcast_fusion.4
  254.6 0.0 copy-done.2
  254.6 0.7 copy.39
  255.3 0.0 copy-done.1
  255.3 0.7 copy.40
  256.1 0.0 copy-done
  256.1 0.0 copy-start.3
  256.1 0.0 copy-start.4
  256.1 1.3 copy.41
  257.3 0.0 copy-done.3
  257.3 0.6 copy.42
  257.9 0.0 copy-done.4
  257.9 0.6 copy.43
  (1 shorter events, 0.0 us)
Async XLA Ops:
  1.6 1.9 copy-start.5
  251.5 3.0 %copy-start.2 = (bf16[256,768]{1,0:T(8,128)(2,1)S(1)}, bf16[256,768]{1,0:T(8,128)(2,1)}, u32[]{:S(2)}) copy-start(bf16[256,768]{1,0:T(8,128)(2,1)} %get-tuple-element.60) | copy-start | bytes 1179652
  251.5 3.8 %copy-start.1 = (bf16[256,768]{1,0:T(8,128)(2,1)S(1)}, bf16[256,768]{1,0:T(8,128)(2,1)}, u32[]{:S(2)}) copy-start(bf16[256,768]{1,0:T(8,128)(2,1)} %get-tuple-element.61) | copy-start | bytes 1179652
  253.7 2.3 copy-start
  256.1 1.3 copy-start.3
  256.1 1.9 copy-start.4

commit v7 on v6

--- a/solution.py
+++ b/solution.py
@@ -528,13 +528,11 @@
     return values * half, slope
 
 
-GATHER_MIDDLE = ()
+GATHER_MIDDLE = (3, )
 FOLD_MIDDLE = ()
 def block_kernel(
-    index_ref,
+    query_of_ref,
     live_ref,
-    query_of_ref,
-    rank_ref,
     passage_ref,
     read_self_refs,
     write_self_ref,
@@ -549,6 +547,8 @@
     bucket_ref,
     count_ref,
     shard_out,
+    expand_out,
+    reduce_out,
     slots_ref,
     gains_out,
     bias_out,
@@ -556,6 +556,7 @@
     block_ref,
     exps_out,
     kv_out,
+    place_ref,
     shard_ref,
     flag_ref,
     full,
@@ -893,7 +894,10 @@
         total = parts[0].astype(wide)
         for part in parts[1:]:
             total = total + part.astype(wide)
-        shard_out[g] = total
+        if g < 2:
+            shard_out[g] = total
+        else:
+            (expand_out, reduce_out)[g - 2][...] = total
 
     def send_pair(j):
         for i in range(TILE):
@@ -904,13 +908,32 @@
                 flag_copy(to).start()
                 slot_copy(to).start()
 
+    lane = lax.broadcasted_iota(jnp.int32, (1, 2 * HEAD_DIM), 1)
+    nobody = jnp.zeros_like(lane)
+
+    def at_place(row, place):
+        return jnp.sum(jnp.where(lane == place, row, 0))
+
+    def route_step(slot, carry):
+        met, found, alive, queries = carry
+        query = query_of_ref[slot]
+        hit = lane == query
+        found = tuple(jnp.where(hit & (met == r), slot, found[r]) for r in range(RANKS))
+        alive = tuple(jnp.where(hit & (met == r), live_ref[slot], alive[r]) for r in range(RANKS))
+        queries = jnp.where(lane == slot, query, queries)
+        return met + hit.astype(jnp.int32), found, alive, queries
+
+    def rank_step(slot, ranks):
+        later = (lane > slot) & (queries_here == query_of_ref[slot])
+        return ranks + later.astype(jnp.int32)
+
     def fill(to, carry):
         for rank in range(RANKS):
-            kept[to * RANKS + rank] = slot_got[index_ref[to * RANKS + rank]]
+            kept[to * RANKS + rank] = slot_got[at_place(slot_at[rank], to)]
         row = lax.broadcasted_iota(jnp.int32, flag_ref.shape[1:], 0)
         marks = jnp.zeros(flag_ref.shape[1:], wide)
         for rank in range(RANKS):
-            mark = jnp.where(live_ref[to * RANKS + rank] > 0, 0.0, MASKED)
+            mark = jnp.where(at_place(live_at[rank], to) > 0, 0.0, MASKED)
             marks = jnp.where(row == rank, mark, marks)
         flag_ref[to] = marks.astype(low)
         return carry
@@ -924,12 +947,19 @@
     shard_ref[3] = reduce_ref[...]
     greet_wait()
     launch(0)
+    launch(1)
+    slots_here = query_of_ref.shape[0]
+    unused, slot_at, live_at, queries_here = lax.fori_loop(
+        0,
+        slots_here,
+        route_step,
+        (nobody, (nobody,) * RANKS, (nobody,) * RANKS, nobody),
+        unroll=8,
+    )
     staging.wait()
-    lax.fori_loop(0, CHIPS, fill, 0)
+    lax.fori_loop(0, CHIPS, fill, 0, unroll=4)
     send_pair(0)
-    launch(1)
     send_pair(1)
-    send_pair(2)
     states[core, pl.ds(me * RANKS, RANKS)] = kept[pl.ds(me * RANKS, RANKS)]
     flags[me] = flag_ref[me]
     core_copy(me).start()
@@ -958,22 +988,31 @@
         return carry
 
     lax.fori_loop(0, tokens // 8, bias_step, 0)
+    ranks = lax.fori_loop(0, slots_here, rank_step, nobody, unroll=8)
+
+    def place_step(slot, carry):
+        place_ref[slot] = query_of_ref[slot] * RANKS + at_place(ranks, slot)
+        return carry
+
+    lax.fori_loop(0, slots_here, place_step, 0, unroll=8)
     residual = target_ref[...].astype(wide)
     normed = (unit_of(residual)[0] * gains_ref[0:1, :]).astype(low)
 
     relay_one(0)
+    launch(3)
+    launch(2)
+    relay_one(1)
+    send_pair(2)
+    relay_two(0)
     send_pair(3)
-    launch(2)
-    relay_two(0)
+    send_pair(4)
     relay_three(0)
-    relay_one(1)
-    send_pair(4)
     relay_two(1)
     arrived(0)
 
     qkv_ref[...] = mm(normed, weight(0)[:, : 3 * width]).astype(low)
     relay_three(1)
-    relay_one(2)
+    send_pair(5)
     queries_t = qkv_ref[:, :width].astype(wide).T
     for h in range(heads):
         q_rows[h] = halves_of_rows(queries_t, h)
@@ -997,10 +1036,12 @@
             out_t[first : first + HEAD_DIM, :] = (
                 mm(values_t[a * HEAD_DIM : (a + 1) * HEAD_DIM], head_exps) * inverse
             )
+        if p == 1:
+            send_pair(6)
+            send_pair(7)
     self_mixed_ref[...] = out_t[...].T.astype(low)
     give(0, rows_nt(self_mixed_ref[...], weight(0)[:, 3 * width :]))
-    launch(3)
-    send_pair(5)
+    relay_one(2)
     arrived(1)
     residual_ref[...] = residual + pair_sum(0)
 
@@ -1032,18 +1073,20 @@
         rows = pl.ds((pair - t + tiles) % tiles * tile_rows, tile_rows)
         return pltpu.make_async_copy(keys.at[t % 2], kv_out.at[rows], keys_sem.at[t % 2])
 
-    send_pair(6)
-    send_pair(7)
     take_in(0)
 
     def tile_step(t, carry):
         tile = (pair - t + tiles) % tiles
 
+        @pl.when(t == 1)
+        def _():
+            relay_two(2)
+
         @pl.when(t == 5)
         def _():
-            relay_one(3)
-
-        @pl.when(t == 6)
+            relay_three(2)
+
+        @pl.when(t == 7)
         def _():
             relay_two(3)
 
@@ -1051,13 +1094,9 @@
         def _():
             take_in(t + 1)
 
-        @pl.when(t == 2)
+        @pl.when(t == 4)
         def _():
-            relay_two(2)
-
-        @pl.when(t == 3)
-        def _():
-            relay_three(2)
+            relay_one(3)
 
         @pl.when(t >= 2)
         def _():
@@ -1104,13 +1143,13 @@
         return carry
 
     lax.fori_loop(0, tiles, tile_step, 0)
-    relay_three(3)
     for h in range(heads):
         inverse = 1.0 / total[h : h + 1, :]
         out_t[h * HEAD_DIM : (h + 1) * HEAD_DIM, :] *= inverse
         scale_ref[:, h, :] = jnp.exp(tile_highest[:, h, :] - highest[h : h + 1, :]) * inverse
     mixed_ref[...] = out_t[...].T.astype(low)
     give(1, rows_nt(mixed_ref[...], weight(1)[:, 3 * width :]))
+    relay_three(3)
     residual_three = residual_ref[...] + pair_sum(1)
     unit, factor = unit_of(residual_three)
     normed = (unit * gains_ref[2:3, :]).astype(low)
@@ -1408,10 +1447,10 @@
     slots = slots_ref.shape[0]
 
     def pick(slot, carry):
-        kept[slot] = slot_got[query_of_ref[slot] * RANKS + rank_ref[slot]]
+        kept[slot] = slot_got[place_ref[slot]]
         return carry
 
-    lax.fori_loop(0, slots, pick, 0)
+    lax.fori_loop(0, slots, pick, 0, unroll=4)
     picked = pltpu.make_async_copy(kept.at[pl.ds(0, slots)], slots_ref, out_sem.at[1])
     picked.start()
     skip_add(0)
@@ -1433,7 +1472,7 @@
 
 
 def run_block(
-    index, live, query_of, rank, passages, weights, target, cotangent, gains, table, buckets, counts
+    query_of, live, passages, weights, target, cotangent, gains, table, buckets, counts
 ):
     low, wide = jnp.bfloat16, jnp.float32
     groups = 4
@@ -1458,7 +1497,9 @@
     return pl.pallas_call(
         block_kernel,
         out_shape=(
-            shape((groups, rows, columns), wide),
+            shape((2, rows, columns), wide),
+            shape((rows, columns), wide),
+            shape((rows, columns), wide),
             shape((slots, passage_len, half), low),
             shape(gains.shape, wide),
             shape(table.shape, wide),
@@ -1467,11 +1508,12 @@
             shape((heads, key_count, tokens), low),
             shape((key_count, 2 * width), low),
         ),
-        in_specs=[IN_SMEM] * 4
+        in_specs=[IN_SMEM] * 2
         + [ANY, (IN_VMEM,) * 3, IN_VMEM, (IN_VMEM,) * 3, IN_VMEM, IN_VMEM, IN_VMEM]
         + [IN_VMEM] * 6,
-        out_specs=(IN_VMEM, ANY) + (IN_VMEM,) * 4 + (ANY, ANY),
+        out_specs=(IN_VMEM,) * 3 + (ANY,) + (IN_VMEM,) * 4 + (ANY, ANY),
         scratch_shapes=[
+            pltpu.SMEM((slots,), jnp.int32),
             vmem((groups, rows, columns), low),
             vmem((CHIPS, FLAG_ROWS, tokens), low),
             vmem((groups, 4, 2, 2, rows, columns), low),
@@ -1532,19 +1574,7 @@
         compiler_params=pltpu.CompilerParams(
             collective_id=0, has_side_effects=True, vmem_limit_bytes=62 * 2**20
         ),
-    )(index, live, query_of, rank, passages, *weights, target, cotangent, gains, table, buckets, counts)
-
-
-def route(slot_query, slot_live):
-    matching = slot_query[:, None] == slot_query[None, :]
-    earlier = jnp.tril(jnp.ones(matching.shape, jnp.bool_), -1)
-    rank = jnp.sum(jnp.logical_and(matching, earlier), axis=1).astype(jnp.int32)
-    position = slot_query * RANKS + rank
-    here = position[None, :] == jnp.arange(CHIPS * RANKS, dtype=jnp.int32)[:, None]
-    slots = slot_query.shape[0]
-    index = jnp.sum(jnp.where(here, jnp.arange(slots, dtype=jnp.int32)[None, :], 0), axis=1)
-    live = jnp.sum(jnp.where(here, slot_live[None, :], 0), axis=1)
-    return rank, index, live
+    )(query_of, live, passages, *weights, target, cotangent, gains, table, buckets, counts)
 
 
 def body(
@@ -1571,14 +1601,11 @@
     heads_here = width_here // HEAD_DIM
     passage_len, half = passage_states.shape[1:]
     bucket_count = position_bias.shape[0]
-    rank, index, live = route(slot_query, slot_live)
     distance = np.zeros((TLEN, 128), np.float32)
     distance[np.arange(TLEN), bucket_table(TLEN, bucket_count, MAXDIST)[:, 0]] = 1.0
-    shard_grads, passage_grad, gains_grad, bias_grad, target_grad, block_out = run_block(
-        index,
-        live,
+    shard_grads, expand_grad, reduce_grad, passage_grad, gains_grad, bias_grad, target_grad, block_out = run_block(
         slot_query,
-        rank,
+        slot_live,
         passage_states,
         (
             (self_query, self_key, self_value),
@@ -1594,7 +1621,7 @@
         position_bias.T,
         jnp.asarray(distance[:, :bucket_count].T),
         jnp.asarray(distance),
-    )[:6]
+    )[:8]
     w = width_here
     first, second = shard_grads[0], shard_grads[1]
     return (
@@ -1611,8 +1638,8 @@
         second[:, w : 2 * w],
         second[:, 2 * w : 3 * w],
         second[:, 3 * w :].T,
-        shard_grads[2],
-        shard_grads[3].T,
+        expand_grad,
+        reduce_grad.T,
     )
 
 

time: 259 us -> 248 us (0.958)
  Pallas kernels: 248 us -> 239 us
  other arithmetic: 2.84 us -> 0 us
    pallas_call x1, Pallas kernels: 248 us -> 239 us  [run_block(): pl.pallas_call(block_kernel, out_shape=(shape((2, rows, columns), wide),...]
    unnamed x17 -> x21, local copies, waits for them, and re-layouts: 3.98 us -> 5.41 us
where the time goes in v7:
time: 248 us; the launch traced here: 247 us
  Pallas kernels  239 us (96%)
  local copies, waits for them, and re-layouts  7.47 us (3%)
    pallas_call x1, Pallas kernels, run_block(): pl.pallas_call(block_kernel, out_shape=(shape((2, rows, columns), wide),...  239 us
    unnamed x21, local copies, waits for them, and re-layouts  5.41 us

profile of v7, /device:TPU:0, one launch (start us, length us, event | category | flops | bytes accessed | tf_op | source)
XLA Modules:
  0.0 246.8 jit_solution(12272557570656097641)
XLA Ops:
  0.7 238.7 %shard_map.298 = (f32[2,48,1536]{2,1,0:T(8,128)}, f32[48,1536]{1,0:T(8,128)}, f32[48,1536]{1,0:T(8,128)}, bf16[40,64,384]{2,1,0:T(8,128)(2,1)}, f32[3,768]{1,0:T...) custom-call(s32[40]{0:T(128)} %query_of_ref.1, ...), custom_call_target="tpu_custom_call" | custom-call | tf_op jit(solution)/shard_map/pallas_call | solution.py:1497
  239.3 0.0 copy-start.2
  239.3 0.0 copy-start.1
  239.3 0.0 copy-start
  239.4 1.2 slice_bitcast_fusion
  240.6 0.8 slice_bitcast_fusion.2
  241.4 0.0 copy-done.2
  241.4 0.7 copy.41
  242.2 0.0 copy-done.1
  242.2 0.7 copy.42
  242.9 0.0 copy-done
  242.9 0.0 copy-start.5
  242.9 0.0 copy-start.6
  242.9 0.0 copy-start.4
  242.9 0.0 copy-start.3
  242.9 1.3 copy.43
  244.2 0.0 copy-done.5
  244.2 0.6 copy.44
  244.8 0.0 copy-done.6
  244.8 0.6 copy.45
  245.4 0.0 copy-done.4
  245.4 0.7 copy.46
  246.1 0.0 copy-done.3
  246.1 0.7 copy.47
Async XLA Ops:
  239.3 2.1 copy-start.2
  239.3 2.8 %copy-start.1 = (bf16[256,768]{1,0:T(8,128)(2,1)S(1)}, bf16[256,768]{1,0:T(8,128)(2,1)}, u32[]{:S(2)}) copy-start(bf16[256,768]{1,0:T(8,128)(2,1)} %get-tuple-element.61) | copy-start | bytes 1179652
  239.3 3.6 %copy-start = (bf16[40,64,384]{2,1,0:T(8,128)(2,1)S(1)}, bf16[40,64,384]{2,1,0:T(8,128)(2,1)}, u32[]{:S(2)}) copy-start(bf16[40,64,384]{2,1,0:T(8,128)(2,1)} %get-tuple-element.62) | copy-start | bytes 5898244
  242.9 1.3 copy-start.5
  242.9 1.9 copy-start.6
  242.9 2.5 %copy-start.4 = (f32[48,1536]{1,0:T(8,128)S(1)}, f32[48,1536]{1,0:T(8,128)}, u32[]{:S(2)}) copy-start(f32[48,1536]{1,0:T(8,128)} %get-tuple-element.73) | copy-start | bytes 884740
  242.9 3.2 %copy-start.3 = (f32[48,1536]{1,0:T(8,128)S(1)}, f32[48,1536]{1,0:T(8,128)}, u32[]{:S(2)}) copy-start(f32[48,1536]{1,0:T(8,128)} %get-tuple-element.30) | copy-start | bytes 884740

commit v8 on v7

--- a/solution.py
+++ b/solution.py
@@ -1082,11 +1082,11 @@
         def _():
             relay_two(2)
 
-        @pl.when(t == 5)
+        @pl.when(t == 4)
         def _():
             relay_three(2)
 
-        @pl.when(t == 7)
+        @pl.when(t == 6)
         def _():
             relay_two(3)
 
@@ -1094,7 +1094,7 @@
         def _():
             take_in(t + 1)
 
-        @pl.when(t == 4)
+        @pl.when(t == 3)
         def _():
             relay_one(3)
 
@@ -1304,11 +1304,11 @@
         def _():
             finish_tile(t - 1)
 
-        @pl.when(t == 3)
+        @pl.when(t == 2)
         def _():
             far_add(2)
 
-        @pl.when(t == 6)
+        @pl.when(t == 5)
         def _():
             far_add(3)
 
@@ -1326,6 +1326,7 @@
 
     store_grad(1, width, kv_sum[...].reshape(2 * half, 2 * width))
     far_start(1)
+    near_add(3)
     next_add(2)
 
     back, gain_two = rms_backward(pair_sum(4), unit_two, factor_two, gains_ref[1:2, :])
@@ -1369,7 +1370,6 @@
         query_rows.extend(query_parts)
     dq = jnp.concatenate(query_rows, axis=0).T.astype(low)
     dqkv = jnp.concatenate([dq] + key_columns + value_columns, axis=1)
-    near_add(3)
     give(5, rows_nt(dqkv, weight(0)[:, : 3 * width]))
     store_grad(0, 3 * width, rows_tn(upper_grad[...].astype(low), self_mixed_ref[...]))
     unit_one, factor_one = unit_of(target_ref[...].astype(wide))

time: 248 us -> 246 us (level)
  no operation moved by 1% of the time
where the time goes in v8:
time: 246 us; the launch traced here: 245 us
  Pallas kernels  237 us (96%)
  local copies, waits for them, and re-layouts  7.47 us (3%)
    pallas_call x1, Pallas kernels, run_block(): pl.pallas_call(block_kernel, out_shape=(shape((2, rows, columns), wide),...  237 us
    unnamed x21, local copies, waits for them, and re-layouts  5.41 us

profile of v8, /device:TPU:0, one launch (start us, length us, event | category | flops | bytes accessed | tf_op | source)
XLA Modules:
  0.0 245.0 jit_solution(161003296393741327)
XLA Ops:
  0.7 236.8 %shard_map.298 = (f32[2,48,1536]{2,1,0:T(8,128)}, f32[48,1536]{1,0:T(8,128)}, f32[48,1536]{1,0:T(8,128)}, bf16[40,64,384]{2,1,0:T(8,128)(2,1)}, f32[3,768]{1,0:T...) custom-call(s32[40]{0:T(128)} %query_of_ref.1, ...), custom_call_target="tpu_custom_call" | custom-call | tf_op jit(solution)/shard_map/pallas_call | solution.py:1497
  237.5 0.0 copy-start.2
  237.5 0.0 copy-start.1
  237.5 0.0 copy-start
  237.5 1.2 slice_bitcast_fusion
  238.7 0.8 slice_bitcast_fusion.2
  239.6 0.0 copy-done.2
  239.6 0.7 copy.41
  240.3 0.0 copy-done.1
  240.3 0.7 copy.42
  241.1 0.0 copy-done
  241.1 0.0 copy-start.5
  241.1 0.0 copy-start.6
  241.1 0.0 copy-start.4
  241.1 0.0 copy-start.3
  241.1 1.3 copy.43
  242.4 0.0 copy-done.5
  242.4 0.6 copy.44
  243.0 0.0 copy-done.6
  243.0 0.6 copy.45
  243.6 0.0 copy-done.4
  243.6 0.7 copy.46
  244.3 0.0 copy-done.3
  244.3 0.7 copy.47
Async XLA Ops:
  237.5 2.1 copy-start.2
  237.5 2.8 %copy-start.1 = (bf16[256,768]{1,0:T(8,128)(2,1)S(1)}, bf16[256,768]{1,0:T(8,128)(2,1)}, u32[]{:S(2)}) copy-start(bf16[256,768]{1,0:T(8,128)(2,1)} %get-tuple-element.61) | copy-start | bytes 1179652
  237.5 3.6 %copy-start = (bf16[40,64,384]{2,1,0:T(8,128)(2,1)S(1)}, bf16[40,64,384]{2,1,0:T(8,128)(2,1)}, u32[]{:S(2)}) copy-start(bf16[40,64,384]{2,1,0:T(8,128)(2,1)} %get-tuple-element.62) | copy-start | bytes 5898244
  241.1 1.3 copy-start.5
  241.1 1.9 copy-start.6
  241.1 2.5 %copy-start.4 = (f32[48,1536]{1,0:T(8,128)S(1)}, f32[48,1536]{1,0:T(8,128)}, u32[]{:S(2)}) copy-start(f32[48,1536]{1,0:T(8,128)} %get-tuple-element.73) | copy-start | bytes 884740
  241.1 3.2 %copy-start.3 = (f32[48,1536]{1,0:T(8,128)S(1)}, f32[48,1536]{1,0:T(8,128)}, u32[]{:S(2)}) copy-start(f32[48,1536]{1,0:T(8,128)} %get-tuple-element.30) | copy-start | bytes 884740

commit v9 on v8

--- a/solution.py
+++ b/solution.py
@@ -1317,19 +1317,19 @@
     lax.fori_loop(0, tiles, back_step, 0)
     dq = out_t[...].T.astype(low)
     give(4, rows_nt(dq, weight(1)[:, :width]))
+    near_add(2)
     store_grad(1, 3 * width, rows_tn(upper_grad[...].astype(low), mixed_ref[...]))
     finish_tile(tiles - 1)
-    near_add(2)
     unit_two, factor_two = unit_of(residual_ref[...])
     normed_two = (unit_two * gains_ref[1:2, :]).astype(low)
     store_grad(1, 0, rows_tn(normed_two, dq))
 
     store_grad(1, width, kv_sum[...].reshape(2 * half, 2 * width))
     far_start(1)
+    next_add(2)
+
+    back, gain_two = rms_backward(pair_sum(4), unit_two, factor_two, gains_ref[1:2, :])
     near_add(3)
-    next_add(2)
-
-    back, gain_two = rms_backward(pair_sum(4), unit_two, factor_two, gains_ref[1:2, :])
     upper_grad[...] += back
 
     grad_low = upper_grad[...].astype(low)

time: 246 us -> 247 us (level)
  no operation moved by 1% of the time
where the time goes in v9:
time: 247 us
  Pallas kernels  239 us (97%)
  local copies, waits for them, and re-layouts  7.47 us (3%)
    pallas_call x1, Pallas kernels, run_block(): pl.pallas_call(block_kernel, out_shape=(shape((2, rows, columns), wide),...  239 us
    unnamed x21, local copies, waits for them, and re-layouts  5.41 us

profile of v9, /device:TPU:0, one launch (start us, length us, event | category | flops | bytes accessed | tf_op | source)
XLA Modules:
  0.0 247.3 jit_solution(5708011208379292160)
XLA Ops:
  0.7 239.1 %shard_map.298 = (f32[2,48,1536]{2,1,0:T(8,128)}, f32[48,1536]{1,0:T(8,128)}, f32[48,1536]{1,0:T(8,128)}, bf16[40,64,384]{2,1,0:T(8,128)(2,1)}, f32[3,768]{1,0:T...) custom-call(s32[40]{0:T(128)} %query_of_ref.1, ...), custom_call_target="tpu_custom_call" | custom-call | tf_op jit(solution)/shard_map/pallas_call | solution.py:1497
  239.7 0.0 copy-start.2
  239.8 0.0 copy-start.1
  239.8 0.0 copy-start
  239.8 1.2 slice_bitcast_fusion
  241.0 0.8 slice_bitcast_fusion.2
  241.8 0.0 copy-done.2
  241.8 0.7 copy.41
  242.6 0.0 copy-done.1
  242.6 0.7 copy.42
  243.3 0.0 copy-done
  243.3 0.0 copy-start.5
  243.3 0.0 copy-start.6
  243.3 0.0 copy-start.4
  243.3 0.0 copy-start.3
  243.4 1.3 copy.43
  244.6 0.0 copy-done.5
  244.6 0.6 copy.44
  245.2 0.0 copy-done.6
  245.2 0.6 copy.45
  245.8 0.0 copy-done.4
  245.8 0.7 copy.46
  246.5 0.0 copy-done.3
  246.6 0.7 copy.47
Async XLA Ops:
  239.7 2.1 copy-start.2
  239.8 2.8 %copy-start.1 = (bf16[256,768]{1,0:T(8,128)(2,1)S(1)}, bf16[256,768]{1,0:T(8,128)(2,1)}, u32[]{:S(2)}) copy-start(bf16[256,768]{1,0:T(8,128)(2,1)} %get-tuple-element.61) | copy-start | bytes 1179652
  239.8 3.6 %copy-start = (bf16[40,64,384]{2,1,0:T(8,128)(2,1)S(1)}, bf16[40,64,384]{2,1,0:T(8,128)(2,1)}, u32[]{:S(2)}) copy-start(bf16[40,64,384]{2,1,0:T(8,128)(2,1)} %get-tuple-element.62) | copy-start | bytes 5898244
  243.3 1.3 copy-start.5
  243.3 1.9 copy-start.6
  243.3 2.5 %copy-start.4 = (f32[48,1536]{1,0:T(8,128)S(1)}, f32[48,1536]{1,0:T(8,128)}, u32[]{:S(2)}) copy-start(f32[48,1536]{1,0:T(8,128)} %get-tuple-element.73) | copy-start | bytes 884740
  243.3 3.2 %copy-start.3 = (f32[48,1536]{1,0:T(8,128)S(1)}, f32[48,1536]{1,0:T(8,128)}, u32[]{:S(2)}) copy-start(f32[48,1536]{1,0:T(8,128)} %get-tuple-element.30) | copy-start | bytes 884740
